TPU v7x, 32 devices: a whole 2x2x4 slice. The times are simulated.
32 devices in a mesh: dp: 4 (over z), blk: 8 (over y, x, core).
Axes of the slice: x: 2, y: 2, z: 4, core: 2. Of those that a mesh axis runs over, the one named last changes fastest.
Arguments:
- latents: bfloat16 [32, 64, 1536], P('dp', 'blk'), may hold values from -6 to 6
- media: bfloat16 [32, 256, 1536], P('dp', 'blk'), may hold values from -6 to 6
- media_lengths: int32 [32], P('dp'), may hold values from 1 to 256, as said below
- cotangent: bfloat16 [32, 64, 1536], P('dp', 'blk'), may hold values from -6 to 6
- query_weight: bfloat16 [1536, 1536], P(('dp', 'blk')), may hold values from -0.15625 to 0.15625
- kv_weight: bfloat16 [1536, 3072], P(('dp', 'blk')), may hold values from -0.15625 to 0.15625
- out_weight: bfloat16 [1536, 1536], P(('dp', 'blk')), may hold values from -1.25 to 1.25
- in_weight: bfloat16 [1536, 6144], P(('dp', 'blk')), may hold values from -0.15625 to 0.15625
- down_weight: bfloat16 [1536, 6144], P(('dp', 'blk')), may hold values from -0.078125 to 0.078125
- media_gain: bfloat16 [1536], P(('dp', 'blk')), may hold values from 0.5 to 1.5
- latent_gain: bfloat16 [1536], P(('dp', 'blk')), may hold values from 0.5 to 1.5
- ffn_gain: bfloat16 [1536], P(('dp', 'blk')), may hold values from 0.5 to 1.5
Outputs:
- resampled: bfloat16 [32, 64, 1536], P('dp', 'blk')
- latents_grad: float32 [32, 64, 1536], P('dp', 'blk')
- media_grad: float32 [32, 256, 1536], P('dp', 'blk')
- query_grad: float32 [1536, 1536], P(('dp', 'blk'))
- kv_grad: float32 [1536, 3072], P(('dp', 'blk'))
- out_grad: float32 [1536, 1536], P(('dp', 'blk'))
- in_grad: float32 [1536, 6144], P(('dp', 'blk'))
- down_grad: float32 [1536, 6144], P(('dp', 'blk'))
- media_gain_grad: float32 [1536], P(('dp', 'blk'))
- latent_gain_grad: float32 [1536], P(('dp', 'blk'))
- ffn_gain_grad: float32 [1536], P(('dp', 'blk'))
Inputs may be any that keep to these rules, and one draw needn't show every extreme that they name: `media_lengths`: a prefix of each image's patch rows is valid; in each aligned block of 8 images one image has all 256.
All inputs are finite; a program needn't handle non-finite values.
Results may differ from a plain program's by a relative error of at most 0.04.
Values may be sent and summed in bfloat16 or wider, within the bound.
No kernel may reach another device: no remote copies, remote signals or barrier semaphores. Data moves between devices by JAX's collectives and lax.ppermute only.
A program may use at most 256 MiB of HBM per device.

v0:
```python
from functools import partial
import math

import jax
import jax.numpy as jnp
from jax import lax
from jax.experimental import pallas as pl
from jax.experimental.pallas import tpu as pltpu
from jax.sharding import PartitionSpec as P

HEADS = 16
NORM_EPS = 1e-05
MASKED = -1e30
GAUSS_DENSITY = 0.3989422804014327
BF = jnp.bfloat16
F32 = jnp.float32
MIB = 1 << 20
VMEM_MIB = 56
NT = ((1,), (1,))
TN = ((0,), (0,))


def chip_bits():
    return lax.axis_size("blk").bit_length() - 2


def hop_bit(j, core):
    return 2 << ((j + core) % chip_bits())


def hop(array, j):
    return lax.ppermute(
        array, "blk", [(i, i ^ hop_bit(j, i % 2)) for i in range(lax.axis_size("blk"))]
    )


def swap(array, bit, axis="blk"):
    return lax.ppermute(array, axis, [(i, i ^ bit) for i in range(lax.axis_size(axis))])


def gather_kind(block):
    blocks = [block]
    for j in range(chip_bits()):
        blocks = blocks + [hop(b, j) for b in blocks]
    return blocks


def gather_all(block):
    return with_other(gather_kind(block))


def with_other(blocks):
    return blocks + [swap(b, 1) for b in blocks]


def owners(me):
    tables = []
    for core in range(2):
        steps = [hop_bit(j, core) for j in range(chip_bits())]
        tables.append(
            [sum(s for j, s in enumerate(steps) if m >> j & 1) for m in range(1 << len(steps))]
        )
    both = [tables[c] + [1 ^ k for k in tables[1 - c]] for c in range(2)]
    return me ^ jnp.where(me % 2 == 0, jnp.array(both[0]), jnp.array(both[1])).astype(jnp.int32)


def after(array, *others):
    return lax.optimization_barrier((array, *others))[0]


def dot(left, right, dims=((1,), (0,))):
    return lax.dot_general(left, right, (dims, ((), ())), preferred_element_type=F32)


def padded_bytes(shape, kind):
    item = jnp.dtype(kind).itemsize
    *lead, rows, lanes = (1, *shape) if len(shape) == 1 else shape
    tile = 32 // item
    return math.prod(lead) * (-(-rows // tile) * tile) * (-(-lanes // 128) * 128) * item


def begin(pairs, sems, first=0):
    copies = [pltpu.make_async_copy(s, d, sems.at[first + i]) for i, (s, d) in enumerate(pairs)]
    for copy in copies:
        copy.start()
    return copies


def call(kernel, outs, spaces, scratch=(), cost=2, big=False, room=6):
    fetched = [i for i, letter in enumerate(spaces) if letter == "d"]
    stored = [i for i, out in enumerate(outs) if out[2] == "d"]
    first = len(spaces)
    last = first + len(outs)
    sems = pltpu.SemaphoreType.DMA

    def run(*operands):
        held = [pltpu.VMEM(operands[i].shape, operands[i].dtype) for i in fetched]
        made = [pltpu.VMEM(outs[i][0], outs[i][1]) for i in stored]
        size = sum(
            padded_bytes(b.shape, b.dtype)
            for b in (*scratch, *held, *made)
            if b.memory_space == pltpu.VMEM
        )

        def whole(*refs):
            at = last + len(scratch)
            own, extra = list(refs[:at]), list(refs[at:])
            out_sems, in_sems = extra.pop(), extra.pop()
            held_refs, made_refs = extra[: len(fetched)], extra[len(fetched) :]
            copies = begin([(own[i], r) for i, r in zip(fetched, held_refs)], in_sems)
            results = [(r, own[first + i]) for i, r in zip(stored, made_refs)]
            for i, r in zip(fetched, held_refs):
                own[i] = r
            for i, r in zip(stored, made_refs):
                own[first + i] = r
            for copy in copies:
                copy.wait()
            kernel(*own)
            for copy in begin(results, out_sems):
                copy.wait()

        return pl.pallas_call(
            whole,
            out_shape=[jax.ShapeDtypeStruct(shape, kind) for shape, kind, _ in outs],
            in_specs=[
                pl.BlockSpec(memory_space=pltpu.SMEM if s == "s" else pltpu.HBM) for s in spaces
            ],
            out_specs=[pl.BlockSpec(memory_space=pltpu.HBM)] * len(outs),
            scratch_shapes=[
                *scratch,
                *held,
                *made,
                sems((max(1, len(fetched)),)),
                sems((max(1, len(stored)),)),
            ],
            compiler_params=pltpu.CompilerParams(vmem_limit_bytes=VMEM_MIB * MIB if big else size + room * MIB),
            cost_estimate=pl.CostEstimate(
                flops=int(cost * 1.15e9), bytes_accessed=int(cost * 3.6e6), transcendentals=0
            ),
        )(*operands)

    return run


def column_steps(width, steps=3):
    step = width // steps if width % (128 * steps) == 0 else width
    return [(at, step) for at in range(0, width, step)]


def kept_and_sent(shape):
    return [(shape, BF, "h")] * 2, [
        pltpu.VMEM(shape, BF),
        pltpu.VMEM(shape, BF),
        pltpu.SemaphoreType.DMA((6,)),
    ]


def put_slots(parts, outs, at, step, values, written):
    kept, sent, sems = parts
    half = kept.shape[0]
    for m, value in enumerate(values):
        (sent if m // half else kept)[m % half, :, at : at + step] = value.astype(BF)
    for source, target in ((kept, outs[0]), (sent, outs[1])):
        cols = pl.ds(at, step)
        copy = pltpu.make_async_copy(
            source.at[:, :, cols], target.at[:, :, cols], sems.at[len(written)]
        )
        copy.start()
        written.append(copy)


def fold_kernel(kept, got, keep, send, left, right, low, high, sems):
    slots = left.shape[0]
    half = slots // 2
    order = [m for i in range(half) for m in (i + half, i)]
    pairs = [(r.at[m], h.at[m]) for m in order for r, h in ((kept, left), (got, right))]
    copies = begin(pairs, sems)
    written = []
    for i, m in enumerate(order):
        copies[2 * i].wait()
        copies[2 * i + 1].wait()
        total = (left[m].astype(F32) + right[m].astype(F32)).astype(BF)
        held, out = (high, send) if m >= half else (low, keep)
        held[m % half] = total
        copy = pltpu.make_async_copy(held.at[m % half], out.at[m % half], sems.at[2 * slots + i])
        copy.start()
        written.append(copy)
    for copy in written:
        copy.wait()


def fold(kept, got):
    slots, rows, width = kept.shape
    half = (slots // 2, rows, width)
    return call(
        fold_kernel,
        [(half, BF, "h")] * 2,
        "hh",
        [
            pltpu.VMEM(kept.shape, BF),
            pltpu.VMEM(kept.shape, BF),
            pltpu.VMEM(half, BF),
            pltpu.VMEM(half, BF),
            pltpu.SemaphoreType.DMA((3 * slots,)),
        ],
        cost=2,
    )(kept, got)


def scatter(parts, hooks=()):
    kept, sent = parts
    hooks = list(hooks)
    for j in reversed(range(chip_bits())):
        got = hop(sent, j)
        if hooks:
            got = after(got, *hooks.pop(0)(sent))
        if j:
            kept, sent = fold(kept, got)
    return kept[0], got[0]


def normalize(values):
    center = values - jnp.mean(values, -1, keepdims=True)
    inverse = lax.rsqrt(jnp.mean(center * center, -1, keepdims=True) + NORM_EPS)
    return (center * inverse, inverse)


def norm_back(grad_norm, normed, inverse):
    return inverse * (
        grad_norm
        - jnp.mean(grad_norm, -1, keepdims=True)
        - normed * jnp.mean(grad_norm * normed, -1, keepdims=True)
    )


class Layout:
    def __init__(self, span, size):
        self.span, self.size = span, size
        pad = -(-span // 128) * 128
        if (2 * span) % 128 == 0:
            self.step, self.v_at = span, span // 128 * 128
        else:
            self.step, self.v_at = pad, pad
        self.block = pad
        self.v_off = self.step - self.v_at
        self.q_at = 2 * self.step
        self.gain_at = self.q_at + span if self.step == span else 3 * pad
        self.width = -(-(self.gain_at + 2) // 128) * 128
        self.heads = span // size

    def keys(self, values):
        return values[..., : self.block]

    def values(self, values):
        return values[..., self.v_at : self.v_at + self.block]

    def queries(self, values):
        return values[..., self.q_at : self.q_at + self.block]

    def pack(self, keys, values):
        shared = self.block - self.v_at
        if not shared:
            return jnp.concatenate([keys, values], 1)
        return jnp.concatenate(
            [keys[:, : self.v_at], keys[:, self.v_at :] + values[:, :shared], values[:, shared:]], 1
        )

    def masks(self, rows, offset):
        lane = lax.broadcasted_iota(jnp.int32, (rows, self.block), 1) - offset
        return [
            (lane >= h * self.size) & (lane < (h + 1) * self.size) for h in range(self.heads)
        ]


def owned_heads(count, ring, per_ring, b):
    groups = count // ring
    return [((b % ring) * per_ring + j) * groups + b // ring for j in range(per_ring)]


def split_attn_kernel(lay, ring, per_ring, kv, query, gains, out):
    count, own, _ = out.shape
    width = query.shape[1]
    size = lay.size
    scaled = (query[...].astype(F32) * gains[:, 1:2]).astype(BF)
    both = kv[...]
    lane = lax.broadcasted_iota(jnp.int32, (own, lay.width - lay.gain_at), 1)
    tail = jnp.where(lane == 0, gains[:, 0:1], jnp.where(lane == 1, gains[:, 1:2], 0.0))
    tail = tail.astype(BF)
    for b in range(count):
        heads = owned_heads(count, ring, per_ring, b)
        pieces = []
        for source, base in ((both, 0), (both, width), (scaled, 0)):
            pieces += [source[:, base + h * size : base + (h + 1) * size] for h in heads]
            if lay.step > lay.span:
                pieces.append(jnp.zeros((own, lay.step - lay.span), BF))
        out[b] = jnp.concatenate(pieces + [tail], 1)


def split_ffn_kernel(w_in, w_down, gains, out):
    count, _, four = out.shape
    part = four // 4
    for b in range(count):
        for p in range(2):
            cols = slice((2 * b + p) * part, (2 * b + p + 1) * part)
            scaled = (w_in[:, cols].astype(F32) * gains[:, 2:3]).astype(BF)
            out[b, :, 2 * p * part : (2 * p + 1) * part] = scaled
            out[b, :, (2 * p + 1) * part : (2 * p + 2) * part] = w_down[:, cols]


def prepare_kernel(media, lats, out):
    rows = media.shape[0]
    out[:rows, :] = normalize(media[...].astype(F32))[0].astype(BF)
    out[rows:, :] = normalize(lats[...].astype(F32))[0].astype(BF)


def stacked(values, masks):
    return jnp.concatenate([jnp.where(m, values, jnp.zeros_like(values)) for m in masks], 0)


def unstacked(values, masks):
    rows = values.shape[0] // len(masks)
    total = jnp.zeros((rows, values.shape[1]), F32)
    for h, m in enumerate(masks):
        total = jnp.where(m, values[h * rows : (h + 1) * rows], total)
    return total


def patch_index(place_ref, count, media_rows, rows):
    column = lax.broadcasted_iota(jnp.int32, (rows, count * media_rows), 1)
    slot, row = column // media_rows, column % media_rows
    index = row
    for k in range(count):
        index = jnp.where(slot == k, place_ref[2 + k] * media_rows + row, index)
    return index


def scaled_columns(lay, w):
    row_media = w[:, lay.gain_at : lay.gain_at + 1].astype(F32)
    row_lat = w[:, lay.gain_at + 1 : lay.gain_at + 2].astype(F32)
    base = w[:, : lay.q_at].astype(F32)
    rest = w[:, lay.q_at :]
    return (base * row_media).astype(BF), jnp.concatenate([(base * row_lat).astype(BF), rest], 1)


def row_copies(slots, block_m, block_l, xm, xl):
    pairs = []
    for k, slot in enumerate(slots):
        pairs.append((slot.at[pl.ds(0, block_m)], xm.at[pl.ds(k * block_m, block_m)]))
        pairs.append((slot.at[pl.ds(block_m, block_l)], xl.at[pl.ds(k * block_l, block_l)]))
    return pairs


def out_copies(me, dz, near, far, held):
    planes, own, _ = near.shape
    core = me % 2
    pairs = []
    for source, which in ((near, core), (far, 1 - core)):
        for k in range(planes):
            at = pl.multiple_of(((dz ^ k) * 2 + which) * own, own)
            pairs.append((source.at[k], held.at[pl.ds(at, own)]))
    return pairs


def rows_of_heads(lay, member, wo_all, wo):
    at = pl.multiple_of(member * lay.span, lay.span)
    wo[...] = jnp.zeros(wo.shape, wo.dtype)
    wo[lay.v_off : lay.v_off + lay.span, :] = wo_all[pl.ds(at, lay.span), :]


def weight_copies(place_ref, weights, held):
    if len(weights) == 1:
        return [(weights[0], held)]
    return out_copies(place_ref[0], place_ref[1], *weights, held)


def forward_kernel(count, lay, place_ref, len_ref, *refs):
    slots, refs = refs[:count], refs[count:]
    w_hbm, kv_out, lat_out, att_out, lse_out, odd_out, low_out = refs[:7]
    xm, xl, w, wm, wl, kv_ref, lat_ref, att_ref, lse_ref, odd, low, sems, out_sems = refs[7:]
    images, media_rows = kv_ref.shape[1:3]
    lat_rows = lat_ref.shape[2]
    rows = count * lat_rows
    block_m, block_l = images * media_rows, images * lat_rows
    copies = begin([(w_hbm, w)] + row_copies(slots, block_m, block_l, xm, xl), sems)
    copies[0].wait()
    wm[...], wl[...] = scaled_columns(lay, w[...])
    step = max(1, count // 4)
    for k in range(0, count, step):
        for i in range(k, k + step):
            copies[1 + 2 * i].wait()
        proj = dot(xm[k * block_m : (k + step) * block_m, :], wm[...]).astype(BF)
        kv_ref[k : k + step] = proj.reshape(step, images, media_rows, lay.q_at)
    for k in range(count):
        copies[2 + 2 * k].wait()
    lat_ref[...] = dot(xl[...], wl[...]).reshape(lat_ref.shape)
    written = begin([(kv_ref, kv_out), (lat_ref, lat_out)], out_sems)

    scale = 1.0 / math.sqrt(lay.size)
    q_masks, v_masks = lay.masks(rows, 0), lay.masks(rows, lay.v_off)
    index = patch_index(place_ref, count, media_rows, lay.heads * rows)
    for i in range(images):
        kv = kv_ref[:, i].reshape(count * media_rows, lay.q_at)
        lat = lat_ref[:, i].reshape(rows, lay.width).astype(BF)
        queries = stacked(lay.queries(lat), q_masks)
        allowed = index < len_ref[i]
        scores = jnp.where(allowed, dot(queries, lay.keys(kv), NT) * scale, MASKED)
        lat_scores = dot(queries, lay.keys(lat), NT) * scale
        top = jnp.maximum(
            jnp.max(scores, -1, keepdims=True), jnp.max(lat_scores, -1, keepdims=True)
        )
        probs = jnp.where(allowed, jnp.exp(scores - top), 0.0)
        lat_probs = jnp.exp(lat_scores - top)
        denominator = jnp.sum(probs, -1, keepdims=True) + jnp.sum(lat_probs, -1, keepdims=True)
        weighted = dot(probs.astype(BF), lay.values(kv)) + dot(
            lat_probs.astype(BF), lay.values(lat)
        )
        attended = unstacked(weighted / denominator, v_masks)
        att_ref[:, i] = attended.reshape(count, lat_rows, lay.block)
        lse_ref[i] = jnp.broadcast_to(top + jnp.log(denominator), (lay.heads * rows, 128))
    half = count // 2
    for k in range(count):
        rounded = att_ref[k].reshape(block_l, lay.block).astype(BF)
        low[k] = rounded
        if k >= half:
            odd[k - half] = rounded
    pairs = [(odd, odd_out), (low, low_out), (att_ref, att_out), (lse_ref, lse_out)]
    written += begin(pairs, out_sems, 2)
    for copy in written:
        copy.wait()


def out_kernel(lay, ring, weights, place_ref, att_hbm, got, *refs):
    sources, outs, refs = refs[:weights], refs[weights : weights + 2], refs[weights + 2 :]
    wo_all, wo, wo_far, att, sems, *parts = refs
    half, rows = got.shape[:2]
    pairs = weight_copies(place_ref, sources, wo_all) + [(att_hbm.at[pl.ds(0, half)], att)]
    copies = begin(pairs, sems)
    for copy in copies:
        copy.wait()
    here = att[...].reshape(half * rows, lay.block)
    there = got[...].reshape(half * rows, lay.block)
    member = place_ref[0] % ring
    rows_of_heads(lay, member, wo_all, wo)
    rows_of_heads(lay, member ^ 1, wo_all, wo_far)
    written = []
    for at, step in column_steps(wo.shape[1]):
        cols = slice(at, at + step)
        total = dot(here, wo[:, cols]) + dot(there, wo_far[:, cols])
        values = [total[m * rows : (m + 1) * rows] for m in range(half)]
        put_slots(parts, outs, at, step, values, written)
    for copy in written:
        copy.wait()


def backward_kernel(count, lay, ring, weights, place_ref, len_ref, *refs):
    branch, sources, refs = refs[:count], refs[count : count + weights], refs[count + weights :]
    kv_hbm, lat_hbm, att_hbm, lse_hbm, dkv_ref, dlat_ref, dkv_odd, dlat_odd = refs[:8]
    br, kv_ref, lat_ref, wo_all, wo, att_ref, lse_ref, dwide, datt, sems = refs[8:]
    images, media_rows = kv_ref.shape[1:3]
    lat_rows = lat_ref.shape[2]
    rows = count * lat_rows
    block_m, block_l = images * media_rows, images * lat_rows
    pairs = weight_copies(place_ref, sources, wo_all)
    pairs += [(branch[k], br.at[pl.ds(k * block_l, block_l)]) for k in range(count)]
    ready = len(pairs)
    pairs += [(lat_hbm, lat_ref), (att_hbm, att_ref), (lse_hbm, lse_ref), (kv_hbm, kv_ref)]
    copies = begin(pairs, sems)
    for copy in copies[:ready]:
        copy.wait()
    rows_of_heads(lay, place_ref[0] % ring, wo_all, wo)
    datt[...] = dot(br[...], wo[...], NT).reshape(datt.shape)
    for copy in copies[ready:]:
        copy.wait()

    scale = 1.0 / math.sqrt(lay.size)
    q_masks, v_masks = lay.masks(rows, 0), lay.masks(rows, lay.v_off)
    index = patch_index(place_ref, count, media_rows, lay.heads * rows)
    for i in range(images):
        kv = kv_ref[:, i].reshape(count * media_rows, lay.q_at)
        lat = lat_ref[:, i].reshape(rows, lay.width).astype(BF)
        queries = stacked(lay.queries(lat), q_masks)
        grads = datt[:, i].reshape(rows, lay.block).astype(BF)
        attended = att_ref[:, i].reshape(rows, lay.block)
        grad_heads = stacked(grads, v_masks)
        delta = jnp.sum(stacked(grads.astype(F32) * attended, v_masks), -1, keepdims=True)
        total = lse_ref[i][:, :1]
        allowed = index < len_ref[i]
        scores = jnp.where(allowed, dot(queries, lay.keys(kv), NT) * scale, MASKED)
        lat_scores = dot(queries, lay.keys(lat), NT) * scale
        probs = jnp.where(allowed, jnp.exp(scores - total), 0.0)
        lat_probs = jnp.exp(lat_scores - total)
        score_grad = (probs * (dot(grad_heads, lay.values(kv), NT) - delta)).astype(BF)
        lat_score_grad = (lat_probs * (dot(grad_heads, lay.values(lat), NT) - delta)).astype(BF)
        query_grad = scale * unstacked(
            dot(score_grad, lay.keys(kv)) + dot(lat_score_grad, lay.keys(lat)), q_masks
        )
        dkv_ref[:, i] = (
            lay.pack(scale * dot(score_grad, queries, TN), dot(probs.astype(BF), grad_heads, TN))
            .astype(BF)
            .reshape(count, media_rows, lay.q_at)
        )
        dlat = jnp.concatenate(
            [
                lay.pack(
                    scale * dot(lat_score_grad, queries, TN),
                    dot(lat_probs.astype(BF), grad_heads, TN),
                ),
                query_grad,
            ],
            1,
        )
        dwide[:, i] = jnp.pad(dlat, ((0, 0), (0, lay.width - dlat.shape[1]))).reshape(
            count, lat_rows, lay.width
        )
    dlat_ref[...] = dwide[...].reshape(count * block_l, lay.width).astype(BF)
    half = count // 2
    for k in range(half):
        dkv_odd[k] = dkv_ref[half + k]
        dlat_odd[k] = dlat_ref[(half + k) * block_l : (half + k + 1) * block_l, :]


def input_grad_kernel(lay, *refs):
    ins, outs, refs = refs[:6], refs[6:8], refs[8:]
    dkv, dlat, w, w_far, sems, *parts = refs
    count, width, block_l = dkv.shape[0], dkv.shape[-1] // 2, dlat.shape[0] // dkv.shape[0]
    block_m = dkv.shape[1] * dkv.shape[2]
    steps = column_steps(w.shape[0])
    pairs = []
    for c, (media, lat) in enumerate(((ins[0], ins[1]), (ins[2], ins[3]))):
        pairs.append((lat.at[pl.ds(0, count * block_l)], dlat.at[:, pl.ds(c * lay.width, lay.width)]))
        pairs.append((media.at[pl.ds(0, count)], dkv.at[:, :, :, pl.ds(c * width, width)]))
    ready = len(pairs)
    for at, step in steps:
        here = pl.ds(at, step)
        pairs += [(ins[4].at[here], w.at[here]), (ins[5].at[here], w_far.at[here])]
    copies = begin(pairs, sems)
    for copy in copies[:ready]:
        copy.wait()
    media_rows = dkv[...].reshape(count * block_m, 2 * width)
    written = []
    for i, (at, step) in enumerate(steps):
        here = slice(at, at + step)
        copies[ready + 2 * i].wait()
        copies[ready + 2 * i + 1].wait()
        near, far = scaled_columns(lay, w[here, :]), scaled_columns(lay, w_far[here, :])
        back = dot(media_rows, jnp.concatenate([near[0], far[0]], 1), NT)
        lat = dot(dlat[...], jnp.concatenate([near[1], far[1]], 1), NT)
        values = []
        for m in range(count):
            rows = [back[m * block_m : (m + 1) * block_m], lat[m * block_l : (m + 1) * block_l]]
            values.append(jnp.concatenate(rows, 0))
        put_slots(parts, outs, at, step, values, written)
    for copy in written:
        copy.wait()


def attn_weight_grad_kernel(count, lay, ring, place_ref, *refs):
    slots, branch, refs = refs[:count], refs[count : 2 * count], refs[2 * count :]
    dkv_hbm, dlat_hbm, w_hbm, att_hbm, grads_out, out_keep, out_send = refs[:7]
    xm, xl, br, out_all, dkv, dlat, w, att, grads, sems, out_sems = refs[7:]
    images, media_rows = dkv.shape[1:3]
    block_m, block_l = images * media_rows, dlat.shape[0] // count
    pairs = [(branch[k], br.at[pl.ds(k * block_l, block_l)]) for k in range(count)]
    pairs += [(att_hbm, att), (dkv_hbm, dkv), (dlat_hbm, dlat)]
    ready = len(pairs)
    steps = column_steps(xm.shape[1])
    for at, step in steps:
        cols = pl.ds(at, step)
        pairs.append((w_hbm.at[cols], w.at[cols]))
        for source, target in row_copies(slots, block_m, block_l, xm, xl):
            pairs.append((source.at[:, cols], target.at[:, cols]))
    each = (len(pairs) - ready) // len(steps)
    copies = begin(pairs, sems)
    for copy in copies[: count + 1]:
        copy.wait()
    total = dot(att[...].reshape(count * block_l, lay.block), br[...], TN)
    total = total[lay.v_off : lay.v_off + lay.span]
    per_ring, own = out_keep.shape[0], out_keep.shape[1]
    for q in range(per_ring * ring):
        out_all[q] = total[q * own : (q + 1) * own].astype(BF)
    me = place_ref[0]
    for j in range(per_ring):
        for r in range(ring):
            piece = out_all[j * ring + ((me % ring) ^ r)]
            if r:
                out_send[r - 1, j] = piece
            else:
                out_keep[j] = piece
    for copy in copies[count + 1 : ready]:
        copy.wait()
    right = dkv[...].reshape(count * block_m, lay.q_at)
    written = []
    for i, (at, step) in enumerate(steps):
        for copy in copies[ready + i * each : ready + (i + 1) * each]:
            copy.wait()
        here = slice(at, at + step)
        g_media = dot(xm[:, here], right, TN)
        g_lat = dot(xl[:, here], dlat[...], TN)
        block = w[here, :].astype(F32)
        base = block[:, : lay.q_at]
        row_media = block[:, lay.gain_at : lay.gain_at + 1]
        row_lat = block[:, lay.gain_at + 1 : lay.gain_at + 2]
        gain_media = jnp.sum(g_media * base, 1, keepdims=True)
        gain_lat = jnp.sum(g_lat[:, : lay.q_at] * base, 1, keepdims=True)
        rest = g_lat[:, lay.q_at :]
        lane = lax.broadcasted_iota(jnp.int32, rest.shape, 1) + lay.q_at
        rest = jnp.where(lane == lay.gain_at, gain_media, rest)
        rest = jnp.where(lane == lay.gain_at + 1, gain_lat, rest)
        grads[here, : lay.q_at] = (
            g_media * row_media + g_lat[:, : lay.q_at] * row_lat
        ).astype(BF)
        grads[here, lay.q_at :] = rest.astype(BF)
        rows = pl.ds(at, step)
        written += begin([(grads.at[rows], grads_out.at[rows])], out_sems, i)
    for copy in written:
        copy.wait()


def mixed_kernel(keep, got, lats, mixed, normed):
    value = keep[...].astype(F32) + got[...].astype(F32) + lats[...].astype(F32)
    mixed[...] = value
    normed[...] = normalize(value)[0].astype(BF)


def erf_parts(values):
    cdf = 0.5 * (1.0 + lax.erf(values * 0.7071067811865476))
    return cdf, cdf + values * jnp.exp(-0.5 * values * values) * GAUSS_DENSITY


def side_copies(side, weights, held):
    part = held.shape[1] // 2
    if part % 128:
        return [(weights[side], held)]
    cols = pl.ds(side * part, part)
    return [(w.at[:, cols], held.at[:, pl.ds(i * part, part)]) for i, w in enumerate(weights)]


def ffn_kernel(half, *refs):
    rows_in, cots, weights = refs[:half], refs[half : 2 * half], refs[2 * half : 2 * half + 2]
    made, outs = refs[2 * half + 2 : 2 * half + 6], refs[2 * half + 6 : 2 * half + 8]
    x, c, w_in, w_down, hidden, pre_grad, sems, out_sems, *parts = refs[2 * half + 8 :]
    rows = rows_in[0].shape[0]
    pairs = [(r, x.at[pl.ds(k * rows, rows)]) for k, r in enumerate(rows_in)]
    pairs += side_copies(0, weights, w_in)
    ready = len(pairs)
    pairs += [(r, c.at[pl.ds(k * rows, rows)]) for k, r in enumerate(cots)]
    pairs += side_copies(1, weights, w_down)
    copies = begin(pairs, sems)
    for copy in copies[:ready]:
        copy.wait()
    pre = dot(x[...], w_in[...])
    cdf, slope = erf_parts(pre)
    hidden[...] = (pre * cdf).astype(BF)
    stored = begin(core_copies(hidden, made[:2]), out_sems)
    for copy in copies[ready:]:
        copy.wait()
    pre_grad[...] = (dot(c[...], w_down[...]) * slope).astype(BF)
    stored += begin(core_copies(pre_grad, made[2:]), out_sems, 2)
    back_through(pre_grad, w_in, half, outs, parts)
    for copy in stored:
        copy.wait()


def core_copies(held, outs):
    part = held.shape[1] // 2
    if part % 128:
        return [(held, outs[0])]
    return [(held.at[:, pl.ds(i * part, part)], out) for i, out in enumerate(outs)]


def back_through(left, w, half, outs, parts):
    rows = left.shape[0] // half
    written = []
    for at, step in column_steps(w.shape[0], 1):
        total = dot(left[...], w[at : at + step, :], NT)
        values = [total[m * rows : (m + 1) * rows] for m in range(half)]
        put_slots(parts, outs, at, step, values, written)
    for copy in written:
        copy.wait()


def down_kernel(half, own, far, w, w_far, keep, send, hidden, w_down, sems, *parts):
    part = hidden.shape[1] // 2
    pairs = side_copies(1, (w, w_far), w_down)
    if part % 128:
        pairs.append((own, hidden))
    else:
        pairs += [(r, hidden.at[:, pl.ds(i * part, part)]) for i, r in enumerate((own, far))]
    for copy in begin(pairs, sems):
        copy.wait()
    back_through(hidden, w_down, half, (keep, send), parts)


def ffn_weight_grad_kernel(count, *refs):
    rows_in, own, far, first = refs[:count], refs[count], refs[count + 1], refs[count + 2 : -4]
    out, x, right, sems = refs[-4:]
    part, deep = right.shape[1], own.shape[0]
    rows = rows_in[0].shape[0]
    pairs = [(own, right.at[pl.ds(0, deep)]), (far, right.at[pl.ds(deep, deep)])]
    pairs += [(r, x.at[pl.ds(k * rows, rows)]) for k, r in enumerate(rows_in)]
    for copy in begin(pairs, sems):
        copy.wait()
    for at, step in column_steps(x.shape[1], 2):
        here = slice(at, at + step)
        out[here, :part] = dot(x[:, here], right[...], TN).astype(BF)
    if first:
        out[:, part:] = first[0][...]


def total_kernel(at, left, right, out, a, b, sems):
    rows = pl.ds(at, a.shape[0])
    for copy in begin([(left.at[rows], a), (right.at[rows], b)], sems):
        copy.wait()
    out[...] = (a[...].astype(F32) + b[...].astype(F32)).astype(out.dtype)


def sum_planes_kernel(grads, out):
    planes, _, width = grads.shape
    for p in range(2):
        total = grads[p].astype(F32)
        for d in range(p + 2, planes, 2):
            total = total + grads[d].astype(F32)
        out[:, p * width : (p + 1) * width] = total.astype(BF)


def first_rows(keep, got, a, b, sems):
    rows = pl.ds(0, a.shape[0])
    for copy in begin([(keep.at[rows], a), (got.at[rows], b)], sems):
        copy.wait()
    return a[...].astype(F32) + b[...].astype(F32)


def resampled_kernel(keep, got, far, mixed, out, *held):
    total = mixed[...] + first_rows(keep, got, *held) + far[...].astype(F32)
    out[...] = total.astype(out.dtype)


def ffn_back_kernel(keep, got, far, mixed, cot, mixed_grad, branch, *held):
    normed, inverse = normalize(mixed[...])
    back = first_rows(keep, got, *held) + far[...].astype(F32)
    grad = cot[...].astype(F32) + norm_back(back, normed, inverse)
    mixed_grad[...] = grad
    branch[...] = grad.astype(BF)


def final_kernel(keep, got, media, lats, mixed_grad, media_grad, lat_grad):
    rows = media.shape[0]
    back = keep[...].astype(F32) + got[...].astype(F32)
    normed, inverse = normalize(media[...].astype(F32))
    media_grad[...] = norm_back(back[:rows], normed, inverse)
    normed, inverse = normalize(lats[...].astype(F32))
    lat_grad[...] = mixed_grad[...] + norm_back(back[rows:], normed, inverse)


def finish_ffn_kernel(grads, w_in, gains, in_grad, down_grad, gain_grad):
    part = in_grad.shape[1] // grads.shape[0] // 2
    total = jnp.zeros((w_in.shape[0], 1), F32)
    for b in range(grads.shape[0]):
        for p in range(2):
            cols = slice((2 * b + p) * part, (2 * b + p + 1) * part)
            at = 2 * p * part
            raw = grads[b, :, at : at + part].astype(F32)
            total = total + jnp.sum(raw * w_in[:, cols].astype(F32), 1, keepdims=True)
            in_grad[:, cols] = raw * gains[:, 2:3]
            down_grad[:, cols] = grads[b, :, at + part : at + 2 * part].astype(F32)
    gain_grad[...] = jnp.broadcast_to(total, gain_grad.shape)


def finish_attn_kernel(lay, ring, per_ring, rows, query, gains, q_grad, kv_grad, gain_grad):
    count, own, wide = rows.shape
    width = query.shape[1]
    size = lay.size
    slots = rows[:, :, wide - lay.width :]
    place = {}
    tail = jnp.zeros((own, lay.width - lay.gain_at), F32)
    for b in range(count):
        block = slots[b].astype(F32)
        for j, h in enumerate(owned_heads(count, ring, per_ring, b)):
            for i, at in enumerate((0, lay.step, lay.q_at)):
                place[i, h] = block[:, at + j * size : at + (j + 1) * size]
        tail = tail + block[:, lay.gain_at :]
    heads = width // size
    kv_grad[:, :width] = jnp.concatenate([place[0, h] for h in range(heads)], 1)
    kv_grad[:, width:] = jnp.concatenate([place[1, h] for h in range(heads)], 1)
    raw = jnp.concatenate([place[2, h] for h in range(heads)], 1)
    q_grad[...] = raw * gains[:, 1:2]
    of_query = jnp.sum(raw * query[...].astype(F32), 1, keepdims=True)
    lane = lax.broadcasted_iota(jnp.int32, gain_grad.shape, 1)
    gain_grad[...] = jnp.where(lane == 0, tail[:, 0:1], tail[:, 1:2] + of_query)


def body(
    latents,
    media,
    media_lengths,
    cotangent,
    query_weight,
    kv_weight,
    out_weight,
    in_weight,
    down_weight,
    media_gain,
    latent_gain,
    ffn_gain,
):
    images, lat_rows, width = latents.shape
    media_rows = media.shape[1]
    nb, nd = lax.axis_size("blk"), lax.axis_size("dp")
    half = nb // 2
    size = width // HEADS
    heads = HEADS // nb
    own = query_weight.shape[0]
    plane = nb * own
    span = heads * size
    lay = Layout(span, size)
    hidden_width = in_weight.shape[1]
    part = hidden_width // nb // 2
    me = lax.axis_index("blk").astype(jnp.int32)
    dz = lax.axis_index("dp").astype(jnp.int32)
    place = jnp.concatenate([jnp.stack([me, dz]), owners(me)])
    ring = size // own
    per_ring = nd // ring
    groups = nb // ring
    block_m, block_l = images * media_rows, images * lat_rows
    block = block_m + block_l
    all_m, all_l = nb * block_m, nb * block_l
    sems = pltpu.SemaphoreType.DMA

    gains = jnp.stack([media_gain, latent_gain, ffn_gain], 1).astype(F32)
    (attn_parts,) = call(
        partial(split_attn_kernel, lay, ring, per_ring), [((nb, own, lay.width), BF, "d")], "ddd"
    )(kv_weight, query_weight, gains)

    quick = ring == 2 and own % 16 == 0
    if quick:
        out_near = [out_weight] + [swap(out_weight, k, "dp") for k in range(1, nd)]
    else:
        ring_groups = [[g * ring + i for i in range(ring)] for g in range(groups)]
        out_w = lax.all_gather(out_weight, "dp", axis=0, tiled=False)
        out_w = lax.all_gather(out_w, "blk", axis=0, tiled=False, axis_index_groups=ring_groups)
        out_near = [out_w.transpose(1, 0, 2, 3).reshape(nd * ring * own, width)]

    mine = lax.all_to_all(attn_parts, "blk", 0, 0, tiled=True).reshape(plane, -1)
    attn_w = lax.all_gather(after(mine, *out_near), "dp", axis=0, tiled=True)

    media_flat = media.reshape(block_m, width)
    lat_flat = latents.reshape(block_l, width)
    cot_flat = cotangent.reshape(block_l, width)
    (normed,) = call(prepare_kernel, [((block, width), BF, "d")], "dd", cost=3)(
        after(media_flat, attn_parts), lat_flat
    )
    slots = gather_all(normed)
    cot_pair = jnp.concatenate([cot_flat, swap(cot_flat, 1, "dp")], 0)

    (ffn_parts,) = call(split_ffn_kernel, [((nb, own, 4 * part), BF, "d")], "ddd", cost=4, big=True)(
        after(in_weight, normed), down_weight, gains
    )
    ffn_mine = lax.all_to_all(after(ffn_parts, mine), "blk", 0, 0, tiled=True)
    ffn_mine = ffn_mine.reshape(plane, 4 * part)
    by_plane = jnp.stack(
        [ffn_mine[:, d % 2 * 2 * part : (d % 2 + 1) * 2 * part] for d in range(nd)]
    )
    ffn_w = lax.all_to_all(after(by_plane, *slots, attn_w, cot_pair), "dp", 0, 0, tiled=True)
    ffn_w = ffn_w.reshape(width, 2 * part)

    if quick:
        near = jnp.stack(out_near)
        out_w = [near, swap(near, 1)]
    else:
        out_w = out_near

    cot_kind = gather_kind(after(cot_pair, *slots))
    kv_shape = (nb, images, media_rows, lay.q_at)
    lat_shape = (nb, images, lat_rows, lay.width)
    att_shape = (nb, images, lat_rows, lay.block)
    lse_shape = (images, heads * nb * lat_rows, 128)
    odd_shape = (half, block_l, lay.block)
    low_shape = (nb, block_l, lay.block)
    shapes = [(kv_shape, BF), (lat_shape, F32), (att_shape, F32), (lse_shape, F32)]
    shapes += [(odd_shape, BF), (low_shape, BF)]
    kv, lat_proj, attended, totals, att_odd, att_low = call(
        partial(forward_kernel, nb, lay),
        [(shape, kind, "h") for shape, kind in shapes],
        "ss" + "h" * (nb + 1),
        [
            pltpu.VMEM((all_m, width), BF),
            pltpu.VMEM((all_l, width), BF),
            pltpu.VMEM((width, lay.width), BF),
            pltpu.VMEM((width, lay.q_at), BF),
            pltpu.VMEM((width, lay.width), BF),
        ]
        + [pltpu.VMEM(shape, kind) for shape, kind in shapes]
        + [sems((1 + 2 * nb,)), sems((6,))],
        big=True,
            cost=11,
    )(place, media_lengths, *slots, attn_w)

    def exchange(rows):
        return kept_and_sent((half // 2, rows, width))

    outs, scratch = exchange(block_l)
    parts = call(
        partial(out_kernel, lay, ring, len(out_w)),
        outs,
        "shd" + "h" * len(out_w),
        [
            pltpu.VMEM((nd * ring * own, width), BF),
            pltpu.VMEM((lay.block, width), BF),
            pltpu.VMEM((lay.block, width), BF),
            pltpu.VMEM(odd_shape, BF),
            sems((2 * nd + 1,)),
            *scratch,
        ],
        cost=3,
    )(place, att_low, swap(after(att_odd, *cot_kind[1:3]), 1), *out_w)
    mixed, ffn_in = call(
        mixed_kernel, [((block_l, width), F32, "d"), ((block_l, width), BF, "d")], "ddd"
    )(*scatter(parts, [lambda sent: cot_kind[3:]]), lat_flat)

    mid = block_l // 2
    in_kind = gather_kind(
        jnp.concatenate([ffn_in, swap(ffn_in[:mid], 1, "dp"), swap(ffn_in[mid:], 1, "dp")], 0)
    )
    ffn_far = swap(after(ffn_w, *in_kind[1:3]), 1)
    if part % 128:
        ffn_sides = [
            jnp.concatenate([ffn_w[:, i * part : (i + 1) * part], ffn_far[:, i * part : (i + 1) * part]], 1)
            for i in range(2)
        ]
    else:
        ffn_sides = [ffn_w, ffn_far]
    rows_pair = half * 2 * block_l
    outs, scratch = exchange(2 * block_l)
    cut = part % 128 == 0
    made_shape = (rows_pair, part if cut else 2 * part)
    spare_shape = made_shape if cut else (8, 128)
    hid_own, hid_far, pre_own, pre_far, *parts = call(
        partial(ffn_kernel, half),
        [(made_shape, BF, "h"), (spare_shape, BF, "h")] * 2 + outs,
        "h" * (2 * half + 2),
        [
            pltpu.VMEM((rows_pair, width), BF),
            pltpu.VMEM((rows_pair, width), BF),
            pltpu.VMEM((width, 2 * part), BF),
            pltpu.VMEM((width, 2 * part), BF),
            pltpu.VMEM((rows_pair, 2 * part), BF),
            pltpu.VMEM((rows_pair, 2 * part), BF),
            sems((2 * half + 4,)),
            sems((4,)),
            *scratch,
        ],
        room=14,
            cost=1,
    )(*in_kind, *cot_kind, *ffn_sides)

    def ffn_weight_grad(rows, own_rows, far_rows, *first):
        if not cut:
            own_rows, far_rows = own_rows[:, :part], own_rows[:, part:]
        return call(
            partial(ffn_weight_grad_kernel, nb),
            [((width, part * (1 + len(first))), BF, "d")],
            "h" * (nb + 2) + "d" * len(first),
            [
                pltpu.VMEM((2 * rows_pair, width), BF),
                pltpu.VMEM((2 * rows_pair, part), BF),
                sems((nb + 2,)),
            ],
            room=14,
            cost=4,
        )(*rows, own_rows, swap(far_rows, 1), *first)[0]

    few_rows = [pltpu.VMEM((block_l, width), BF)] * 2 + [sems((2,))]

    def total_far(left, right):
        return call(
            partial(total_kernel, block_l), [((block_l, width), BF, "d")], "hh", few_rows, cost=1
        )(left, right)[0]

    made = {}

    def beside_first(sent):
        made["down"] = ffn_weight_grad(with_other(cot_kind), after(hid_own, sent), hid_far)
        made["both"] = ffn_weight_grad(with_other(in_kind), pre_own, pre_far, made["down"])
        return (made["both"],)

    def beside_second(sent):
        outs, scratch = exchange(2 * block_l)
        made["parts"] = call(
            partial(down_kernel, half),
            outs,
            "hhhh",
            [
                pltpu.VMEM((rows_pair, 2 * part), BF),
                pltpu.VMEM((width, 2 * part), BF),
                sems((4,)),
                *scratch,
            ],
            cost=4,
        )(after(hid_own, sent), hid_far, *ffn_sides)
        return made["parts"]

    terms = scatter(parts, [beside_first, beside_second])
    pair_got = swap(total_far(*terms), 1, "dp")
    mixed_grad, branch = call(
        ffn_back_kernel,
        [((block_l, width), F32, "d"), ((block_l, width), BF, "d")],
        "hhddd",
        few_rows,
    )(*terms, pair_got, mixed, cot_flat)
    branch_slots = gather_all(branch)
    ffn_planes = lax.all_to_all(
        after(made["both"], branch).reshape(nd, plane, 2 * part), "dp", 0, 0, tiled=True
    )

    (ffn_rows,) = call(sum_planes_kernel, [((plane, 4 * part), BF, "d")], "d", cost=3)(ffn_planes)
    ffn_slots = lax.all_to_all(ffn_rows.reshape(nb, own, 4 * part), "blk", 0, 0, tiled=True)

    def keep_second(sent):
        made["second"] = sent
        return ()

    down_terms = scatter(made["parts"], [lambda sent: (), keep_second])

    dkv, dlat, dkv_odd, dlat_odd = call(
        partial(backward_kernel, nb, lay, ring, len(out_w)),
        [
            (kv_shape, BF, "d"),
            ((all_l, lay.width), BF, "d"),
            ((half, *kv_shape[1:]), BF, "d"),
            ((half, block_l, lay.width), BF, "d"),
        ],
        "ss" + "h" * (nb + len(out_w) + 4),
        [
            pltpu.VMEM((all_l, width), BF),
            pltpu.VMEM(kv_shape, BF),
            pltpu.VMEM(lat_shape, F32),
            pltpu.VMEM((nd * ring * own, width), BF),
            pltpu.VMEM((lay.block, width), BF),
            pltpu.VMEM(att_shape, F32),
            pltpu.VMEM(lse_shape, F32),
            pltpu.VMEM(lat_shape, F32),
            pltpu.VMEM(att_shape, F32),
            sems((nb + 2 * nd + 4,)),
        ],
        big=True,
            cost=1,
    )(place, media_lengths, *branch_slots, *out_w, kv, lat_proj, attended, totals)

    attn_grads, out_keep, out_send = call(
        partial(attn_weight_grad_kernel, nb, lay, ring),
        [
            ((width, lay.width), BF, "h"),
            ((per_ring, own, width), BF, "d"),
            ((ring - 1, per_ring, own, width), BF, "d"),
        ],
        "s" + "h" * (2 * nb + 4),
        [
            pltpu.VMEM((all_m, width), BF),
            pltpu.VMEM((all_l, width), BF),
            pltpu.VMEM((all_l, width), BF),
            pltpu.VMEM((per_ring * ring, own, width), BF),
            pltpu.VMEM(kv_shape, BF),
            pltpu.VMEM((all_l, lay.width), BF),
            pltpu.VMEM((width, lay.width), BF),
            pltpu.VMEM(low_shape, BF),
            pltpu.VMEM((width, lay.width), BF),
            sems((nb + 3 + 3 * (1 + 2 * nb),)),
            sems((3,)),
        ],
        big=True,
            cost=1,
    )(place, *slots, *branch_slots, after(dkv, *down_terms), dlat, attn_w, att_low)
    attn_sum = lax.psum_scatter(attn_grads, "dp", scatter_dimension=0, tiled=True)

    outs, scratch = exchange(block)
    parts = call(
        partial(input_grad_kernel, lay),
        outs,
        "hhhhhh",
        [
            pltpu.VMEM((half, *kv_shape[1:-1], 2 * lay.q_at), BF),
            pltpu.VMEM((half * block_l, 2 * lay.width), BF),
            pltpu.VMEM((width, lay.width), BF),
            pltpu.VMEM((width, lay.width), BF),
            sems((10,)),
            *scratch,
        ],
        big=True,
            cost=1,
    )(
        after(dkv, attn_grads),
        dlat,
        swap(dkv_odd, 1),
        swap(dlat_odd, 1).reshape(half * block_l, lay.width),
        attn_w,
        swap(attn_w, 1),
    )
    (resampled,) = call(resampled_kernel, [((block_l, width), BF, "d")], "hhdd", few_rows)(
        *down_terms, swap(total_far(*down_terms), 1, "dp"), mixed
    )

    pieces = [out_keep] + [swap(out_send[r - 1], r) for r in range(1, ring)]
    pieces = jnp.stack(pieces)
    rank = lax.axis_index("blk") % ring
    pieces = [lax.dynamic_index_in_dim(pieces, rank ^ r, 0, False) for r in range(ring)]
    out_rows = jnp.concatenate(pieces, 0).reshape(nd * own, width)
    media_grad, latents_grad = call(
        final_kernel, [((block_m, width), F32, "d"), ((block_l, width), F32, "d")], "ddddd", cost=5
    )(*scatter(parts, [lambda sent: (ffn_rows, resampled), lambda sent: (ffn_slots, out_rows)]), media_flat, lat_flat, mixed_grad)

    in_grad, down_grad, ffn_gain_grad = call(
        finish_ffn_kernel,
        [((own, hidden_width), F32, "d")] * 2 + [((own, 128), F32, "d")],
        "ddd",
        cost=3,
    )(ffn_slots, in_weight, gains)

    attn_slots = lax.all_to_all(attn_sum.reshape(nb, own, -1), "blk", 0, 0, tiled=True)
    query_grad, kv_grad, gain_grads = call(
        partial(finish_attn_kernel, lay, ring, per_ring),
        [((own, width), F32, "d"), ((own, 2 * width), F32, "d"), ((own, 128), F32, "d")],
        "ddd",
    )(attn_slots, query_weight, gains)

    out_rows = after(out_rows, attn_sum)
    out_grad = lax.psum_scatter(out_rows, "dp", scatter_dimension=0, tiled=True).astype(F32)
    return (
        resampled.reshape(latents.shape),
        latents_grad.reshape(latents.shape),
        media_grad.reshape(media.shape),
        query_grad,
        kv_grad,
        out_grad,
        in_grad,
        down_grad,
        gain_grads[:, 0],
        gain_grads[:, 1],
        ffn_gain_grad[:, 0],
    )


def solution(mesh):
    rows = P("dp", "blk", None)
    weight = P(("dp", "blk"), None)
    gain = P(("dp", "blk"))
    return jax.shard_map(
        body,
        mesh=mesh,
        in_specs=(rows, rows, P("dp"), rows) + (weight,) * 5 + (gain,) * 3,
        out_specs=(rows,) * 3 + (weight,) * 5 + (gain,) * 3,
        check_vma=False,
    )
```

profile of v0, /device:TPU:0, one launch (start us, length us, event | category | flops | bytes accessed | tf_op | source)
XLA Modules:
  0.0 329.3 jit_solution(4144627769639667619)
XLA Ops:
  11.3 5.2 %all-to-all-start = ((bf16[8,48,640]{2,1,0:T(8,128)(2,1)}), bf16[8,48,640]{2,1,0:T(8,128)(2,1)S(1)}, u32[]{:S(2)}, u32[]{:S(2)}) async-start(bf16[8,48,640]{2,1,0:T(8,128)(2,1)} %shard_map.221), calls=%async_computation | async-start | bytes 983040 | tf_op jit(solution)/shard_map/all_to_all | solution.py:843
  18.1 2.6 collective-permute-start.8
  22.1 2.0 collective-permute-start
  25.5 6.6 %collective-permute-done.8 = bf16[48,1536]{1,0:T(8,128)(2,1)S(1)} collective-permute-done((bf16[48,1536]{1,0:T(8,128)(2,1)S(1)}, bf16[48,1536]{1,0:T(8,128)(2,1)S(1)}, u32[]{:S(2)}, u32[]{:S(2)}) %collective-permute-start.8) | collective-permute-done | bytes 147488 | tf_op jit(solution)/shard_map/ppermute | solution.py:38
  33.0 2.0 collective-permute-start.1
  35.0 3.4 %collective-permute-done.refs_3_.refs_2_ = bf16[320,1536]{1,0:T(8,128)(2,1)} collective-permute-done((bf16[320,1536]{1,0:T(8,128)(2,1)S(1)}, bf16[320,1536]{1,0:T(8,128)(2,1)}, u32[]{:S(2)}, u32[]{:S(2)}) %collective-permute-start) | collective-permute-done | bytes 983072 | tf_op jit(solution)/shard_map/ppermute | solution.py:32
  38.4 2.6 collective-permute-start.2
  41.0 2.6 shard_map.227
  43.6 3.7 %all-to-all-start.1 = ((bf16[8,48,1536]{2,1,0:T(8,128)(2,1)}), bf16[8,48,1536]{2,1,0:T(8,128)(2,1)S(1)}, u32[]{:S(2)}, u32[]{:S(2)}) async-start(bf16[8,48,1536]{2,1,0:T(8,128)(2,1)} %shard_map.227), calls=%async_computation.1 | async-start | bytes 2359296 | tf_op jit(solution)/shard_map/all_to_all | solution.py:858
  48.3 15.3 %collective-permute-done.2.refs_5_.refs_4_ = bf16[320,1536]{1,0:T(8,128)(2,1)} collective-permute-done((bf16[320,1536]{1,0:T(8,128)(2,1)}, bf16[320,1536]{1,0:T(8,128)(2,1)}, u32[]{:S(2)}, u32[]{:S(2)}) %collective-permute-start.2) | collective-permute-done | bytes 983072 | tf_op jit(solution)/shard_map/ppermute | solution.py:32
  65.6 3.2 collective-permute-done.10
  68.8 2.7 all-to-all-done.1
  75.7 5.8 %all-gather.2.cloned.1.call-done.refs_10_.refs_19_.refs_4_ = bf16[1536,640]{1,0:T(8,128)(2,1)} async-done(((bf16[384,640]{1,0:T(8,128)(2,1)}), bf16[1536,640]{1,0:T(8,128)(2,1)}) %all-gather.2.cloned.1.call-update) | async-done | bytes 1966096 | tf_op jit(solution)/shard_map/all_gather | solution.py:844
  81.4 4.2 %all-to-all-start.2 = ((bf16[4,384,768]{2,1,0:T(8,128)(2,1)}), bf16[4,384,768]{2,1,0:T(8,128)(2,1)S(1)}, u32[]{:S(2)}, u32[]{:S(2)}) async-start(bf16[4,384,768]{2,1,0:T(8,128)(2,1)} %pad_maximum_fusion), calls=%async_computation.2 | async-start | bytes 4718592 | tf_op jit(solution)/shard_map/all_to_all | solution.py:863
  85.7 12.5 %shard_map.223 = (bf16[8,8,32,384]{3,2,1,0:T(8,128)(2,1)}, f32[8,8,8,640]{3,2,1,0:T(8,128)}, f32[8,8,8,256]{3,2,1,0:T(8,128)}, f32[8,128,128]{2,1,0:T(8,128)}, b...) custom-call(s32[10]{0:T(128)} %pad_add_fusion.refs_0_, s32[8]{0:T(128)} %refs_1_.9, bf16[320,1536]{1,0:T(8,128)(2,1)} %copy-done.1, ...), custom_call_target="tpu_custom_call" | custom-call | flops 12650000384 | bytes 39600000 | tf_op jit(solution)/shard_map/pallas_call | solution.py:122
  100.8 3.8 %shard_map.224 = (bf16[2,64,1536]{2,1,0:T(8,128)(2,1)S(1)}, bf16[2,64,1536]{2,1,0:T(8,128)(2,1)S(1)}) custom-call(s32[10]{0:T(128)S(1)} %copy-done.15, bf16[8,64,256]{2,1,0:T(8,128)(2,1)S(1)} %copy-done.10, bf16[4,64,256]{2,1,0:T(8,128)(2,1)S(1)} %collective-permute-done.13.refs_2_, bf16[4,48,1536]{2,1,0:T(8,128)(2,1)S(1)} %pad_maximum_fusion.1.refs_3_.refs_10_, ...), custom_call_target="tpu_custom_call" | custom-call | flops 3449999872 | bytes 10800000 | tf_op jit(solution)/shard_map/pallas_call | solution.py:122
  106.3 6.1 %collective-permute-done.15.refs_1_ = bf16[2,64,1536]{2,1,0:T(8,128)(2,1)S(1)} collective-permute-done((bf16[2,64,1536]{2,1,0:T(8,128)(2,1)S(1)}, bf16[2,64,1536]{2,1,0:T(8,128)(2,1)S(1)}, u32[]{:S(2)}, u32[]{:S(2)}) %collective-permute-start.15) | collective-permute-done | bytes 393248 | tf_op jit(solution)/shard_map/ppermute | solution.py:32
  115.7 4.2 %collective-permute-done.17 = bf16[1,64,1536]{2,1,0:T(8,128)(2,1)S(1)} collective-permute-done((bf16[1,64,1536]{2,1,0:T(8,128)(2,1)S(1)}, bf16[1,64,1536]{2,1,0:T(8,128)(2,1)S(1)}, u32[]{:S(2)}, u32[]{:S(2)}) %collective-permute-start.17) | collective-permute-done | bytes 196640 | tf_op jit(solution)/shard_map/ppermute | solution.py:32
  122.1 2.1 collective-permute-start.18
  124.3 3.1 collective-permute-done.18
  127.5 12.6 %collective-permute-done.19 = bf16[32,1536]{1,0:T(8,128)(2,1)S(1)} collective-permute-done((bf16[32,1536]{1,0:T(8,128)(2,1)S(1)}, bf16[32,1536]{1,0:T(8,128)(2,1)S(1)}, u32[]{:S(2)}, u32[]{:S(2)}) %collective-permute-start.19) | collective-permute-done | bytes 98336 | tf_op jit(solution)/shard_map/ppermute | solution.py:38
  143.0 4.8 %collective-permute-done.20.refs_1_ = bf16[128,1536]{1,0:T(8,128)(2,1)S(1)} collective-permute-done((bf16[128,1536]{1,0:T(8,128)(2,1)S(1)}, bf16[128,1536]{1,0:T(8,128)(2,1)S(1)}, u32[]{:S(2)}, u32[]{:S(2)}) %collective-permute-start.20) | collective-permute-done | bytes 393248 | tf_op jit(solution)/shard_map/ppermute | solution.py:32
  152.1 6.0 %collective-permute-done.22.refs_3_ = bf16[128,1536]{1,0:T(8,128)(2,1)S(1)} collective-permute-done((bf16[128,1536]{1,0:T(8,128)(2,1)}, bf16[128,1536]{1,0:T(8,128)(2,1)S(1)}, u32[]{:S(2)}, u32[]{:S(2)}) %collective-permute-start.22) | collective-permute-done | bytes 393248 | tf_op jit(solution)/shard_map/ppermute | solution.py:32
  160.6 7.4 %shard_map.228 = (bf16[512,384]{1,0:T(8,128)(2,1)S(1)}, bf16[512,384]{1,0:T(8,128)(2,1)S(1)}, bf16[512,384]{1,0:T(8,128)(2,1)S(1)}, bf16[512,384]{1,0:T(8,128)(2...) custom-call(bf16[128,1536]{1,0:T(8,128)(2,1)S(1)} %constant_dynamic-update-slice_fusion.refs_0_, ...), custom_call_target="tpu_custom_call" | custom-call | flops 1150000000 | bytes 3600000 | tf_op jit(solution)/shard_map/pallas_call | solution.py:122
  170.6 3.9 %shard_map.229.refs_10_ = bf16[1536,384]{1,0:T(8,128)(2,1)S(1)} custom-call(bf16[128,1536]{1,0:T(8,128)(2,1)S(1)} %pad_maximum_fusion.3.refs_4_.refs_0_, bf16[128,1536]{1,0:T(8,128)(2,1)} %collective-permute-done.11.refs_5_.refs_1_, bf16[128,1536]{1,0:T(8,128)(2,1)} %collective-permute-done.12.refs_6_.refs_2_, bf16[128,1536]{1,0:T(8,128)(2,1)S(1)} %copy-done.4, ...), custom_call_target="tpu_custom_call" | custom-call | flops 4600000000 | bytes 14400000 | tf_op jit(solution)/shard_map/pallas_call | solution.py:122
  174.5 5.5 %shard_map.230 = bf16[1536,768]{1,0:T(8,128)(2,1)} custom-call(bf16[128,1536]{1,0:T(8,128)(2,1)S(1)} %constant_dynamic-update-slice_fusion.refs_0_, bf16[128,1536]{1,0:T(8,128)(2,1)S(1)} %copy-done.6, bf16[128,1536]{1,0:T(8,128)(2,1)S(1)} %copy-done.9, bf16[128,1536]{1,0:T(8,128)(2,1)S(1)} %collective-permute-done.22.refs_3_, ...), custom_call_target="tpu_custom_call" | custom-call | flops 4600000000 | bytes 14400000 | tf_op jit(solution)/shard_map/pallas_call | solution.py:122
  183.3 2.0 shard_map.232
  185.3 5.0 %collective-permute-done.38 = bf16[1,128,1536]{2,1,0:T(8,128)(2,1)S(1)} collective-permute-done((bf16[1,128,1536]{2,1,0:T(8,128)(2,1)S(1)}, bf16[1,128,1536]{2,1,0:T(8,128)(2,1)S(1)}, u32[]{:S(2)}, u32[]{:S(2)}) %collective-permute-start.38) | collective-permute-done | bytes 393248 | tf_op jit(solution)/shard_map/ppermute | solution.py:32
  192.8 4.1 %collective-permute-done.39.refs_2_ = bf16[64,1536]{1,0:T(8,128)(2,1)S(1)} collective-permute-done((bf16[64,1536]{1,0:T(8,128)(2,1)S(1)}, bf16[64,1536]{1,0:T(8,128)(2,1)S(1)}, u32[]{:S(2)}, u32[]{:S(2)}) %collective-permute-start.39) | collective-permute-done | bytes 196640 | tf_op jit(solution)/shard_map/ppermute | solution.py:38
  196.9 2.1 shard_map.237
  199.8 6.5 %all-to-all-start.3 = ((bf16[4,384,768]{2,1,0:T(8,128)(2,1)}), bf16[4,384,768]{2,1,0:T(8,128)(2,1)S(1)}, u32[]{:S(2)}, u32[]{:S(2)}) async-start(bf16[4,384,768]{2,1,0:T(8,128)(2,1)} %bitcast.25), calls=%async_computation.3 | async-start | bytes 4718592 | tf_op jit(solution)/shard_map/all_to_all | solution.py:1011
  208.3 4.1 %collective-permute-done.40.refs_3_.refs_10_ = bf16[64,1536]{1,0:T(8,128)(2,1)S(1)} collective-permute-done((bf16[64,1536]{1,0:T(8,128)(2,1)S(1)}, bf16[64,1536]{1,0:T(8,128)(2,1)S(1)}, u32[]{:S(2)}, u32[]{:S(2)}) %collective-permute-start.40) | collective-permute-done | bytes 196640 | tf_op jit(solution)/shard_map/ppermute | solution.py:32
  213.7 2.0 shard_map.233
  215.7 2.5 collective-permute-start.36
  222.4 9.2 %shard_map.238 = (bf16[8,8,32,384]{3,2,1,0:T(8,128)(2,1)}, bf16[512,640]{1,0:T(8,128)(2,1)}, bf16[4,8,32,384]{3,2,1,0:T(8,128)(2,1)}, bf16[4,64,640]{2,1,0:T(8,128)(2,1)}) custom-call(s32[10]{0:T(128)} %pad_add_fusion.refs_0_, s32[8]{0:T(128)} %refs_1_.9, bf16[64,1536]{1,0:T(8,128)(2,1)} %copy-done.2, bf16[64,1536]{1,0:T(8,128)(2,1)} %copy-done.36, ...), custom_call_target="tpu_custom_call" | custom-call | flops 1150000000 | bytes 3600000 | tf_op jit(solution)/shard_map/pallas_call | solution.py:122
  231.8 11.6 %shard_map.239 = (bf16[1536,640]{1,0:T(8,128)(2,1)}, bf16[2,48,1536]{2,1,0:T(8,128)(2,1)}, bf16[1,2,48,1536]{3,2,1,0:T(8,128)(2,1)}) custom-call(s32[10]{0:T(128)} %pad_add_fusion.refs_0_, bf16[320,1536]{1,0:T(8,128)(2,1)} %copy-done.1, bf16[320,1536]{1,0:T(8,128)(2,1)} %collective-permute-done.refs_3_.refs_2_, ...), custom_call_target="tpu_custom_call" | custom-call | flops 1150000000 | bytes 3600000 | tf_op jit(solution)/shard_map/pallas_call | solution.py:122
  246.0 7.8 %shard_map.240 = (bf16[2,320,1536]{2,1,0:T(8,128)(2,1)}, bf16[2,320,1536]{2,1,0:T(8,128)(2,1)}) custom-call(bf16[8,8,32,384]{3,2,1,0:T(8,128)(2,1)} %get-tuple-element.117.refs_17_.refs_0_, bf16[512,640]{1,0:T(8,128)(2,1)} %get-tuple-element.115.refs_18_.refs_1_, bf16[4,8,32,384]{3,2,1,0:T(8,128)(2,1)} %collective-permute-done.47.refs_2_, ...), custom_call_target="tpu_custom_call" | custom-call | flops 1150000000 | bytes 3600000 | tf_op jit(solution)/shard_map/pallas_call | solution.py:122
  255.3 2.1 collective-permute-start.37
  257.4 17.5 %collective-permute-done.37.refs_2_ = bf16[64,1536]{1,0:T(8,128)(2,1)S(1)} collective-permute-done((bf16[64,1536]{1,0:T(8,128)(2,1)S(1)}, bf16[64,1536]{1,0:T(8,128)(2,1)S(1)}, u32[]{:S(2)}, u32[]{:S(2)}) %collective-permute-start.37) | collective-permute-done | bytes 196640 | tf_op jit(solution)/shard_map/ppermute | solution.py:38
  278.8 3.8 %all-to-all-start.4 = ((bf16[8,48,1536]{2,1,0:T(8,128)(2,1)}), bf16[8,48,1536]{2,1,0:T(8,128)(2,1)S(1)}, u32[]{:S(2)}, u32[]{:S(2)}) async-start(bf16[8,48,1536]{2,1,0:T(8,128)(2,1)} %bitcast.27), calls=%async_computation.4 | async-start | bytes 2359296 | tf_op jit(solution)/shard_map/all_to_all | solution.py:1016
  282.7 2.7 shard_map.242
  286.4 2.3 collective-permute-start.51
  294.4 5.1 %all-to-all-done.4.refs_0_ = bf16[8,48,1536]{2,1,0:T(8,128)(2,1)S(1)} async-done(((bf16[8,48,1536]{2,1,0:T(8,128)(2,1)}), bf16[8,48,1536]{2,1,0:T(8,128)(2,1)S(1)}, u32[]{:S(2)}, u32[]{:S(2)}) %all-to-all-start.4) | async-done | bytes 1179680 | tf_op jit(solution)/shard_map/all_to_all | solution.py:1016
  299.5 3.5 %all-to-all-start.5 = ((bf16[8,48,640]{2,1,0:T(8,128)(2,1)}), bf16[8,48,640]{2,1,0:T(8,128)(2,1)S(1)}, u32[]{:S(2)}, u32[]{:S(2)}) async-start(bf16[8,48,640]{2,1,0:T(8,128)(2,1)} %bitcast.68), calls=%async_computation.6 | async-start | bytes 983040 | tf_op jit(solution)/shard_map/all_to_all | solution.py:1118
  303.1 8.7 %collective-permute-done.51 = bf16[1,320,1536]{2,1,0:T(8,128)(2,1)S(1)} collective-permute-done((bf16[1,320,1536]{2,1,0:T(8,128)(2,1)}, bf16[1,320,1536]{2,1,0:T(8,128)(2,1)S(1)}, u32[]{:S(2)}, u32[]{:S(2)}) %collective-permute-start.51) | collective-permute-done | bytes 983072 | tf_op jit(solution)/shard_map/ppermute | solution.py:32
  311.7 2.3 shard_map.245
  314.6 3.7 %shard_map.243 = (f32[256,1536]{1,0:T(8,128)}, f32[64,1536]{1,0:T(8,128)}) custom-call(bf16[320,1536]{1,0:T(8,128)(2,1)S(1)} %bitcast.59, bf16[320,1536]{1,0:T(8,128)(2,1)S(1)} %bitcast.48, bf16[256,1536]{1,0:T(8,128)(2,1)S(1)} %bitcast.50, bf16[64,1536]{1,0:T(8,128)(2,1)S(1)} %bitcast.57, f32[64,1536]{1,0:T(8,128)S(1)} %copy-done.34), custom_call_target="tpu_custom_call" | custom-call | flops 5750000128 | bytes 18000000 | tf_op jit(solution)/shard_map/pallas_call | solution.py:122
  318.3 1.9 shard_map.244
  (226 shorter events, 70.4 us)
Async XLA Ops:
  11.3 20.8 %all-to-all-start = ((bf16[8,48,640]{2,1,0:T(8,128)(2,1)}), bf16[8,48,640]{2,1,0:T(8,128)(2,1)S(1)}, u32[]{:S(2)}, u32[]{:S(2)}) async-start(bf16[8,48,640]{2,1,0:T(8,128)(2,1)} %shard_map.221), calls=%async_computation | async-start | bytes 983040 | tf_op jit(solution)/shard_map/all_to_all | solution.py:843
  16.4 65.0 %all-gather.2.cloned.1.call-start = ((), (), s32[]{:S(2)}) async-start(), calls=%async_computation.8 | async-start | bytes 2457600 | tf_op jit(solution)/shard_map/all_gather | solution.py:844
  16.5 9.0 %collective-permute-start.7 = (bf16[48,1536]{1,0:T(8,128)(2,1)S(1)}, bf16[48,1536]{1,0:T(8,128)(2,1)S(1)}, u32[]{:S(2)}, u32[]{:S(2)}) collective-permute-start(bf16[48,1536]{1,0:T(8,128)(2,1)S(1)} %copy-done.45), channel_id=1, source_target_pairs={{0,8},{8,0},{16,24},{24,16},{1,9},{9,1},{17,25},{25,17},{2,10},{10... | collective-permute-start | bytes 442376 | tf_op jit(solution)/shard_map/ppermute | solution.py:38
  18.1 14.0 %collective-permute-start.8 = (bf16[48,1536]{1,0:T(8,128)(2,1)S(1)}, bf16[48,1536]{1,0:T(8,128)(2,1)S(1)}, u32[]{:S(2)}, u32[]{:S(2)}) collective-permute-start(bf16[48,1536]{1,0:T(8,128)(2,1)S(1)} %copy-done.45), channel_id=1, source_target_pairs={{0,16},{8,24},{16,0},{24,8},{1,17},{9,25},{17,1},{25,9},{2,18},{10... | collective-permute-start | bytes 442376 | tf_op jit(solution)/shard_map/ppermute | solution.py:38
  20.7 11.4 %collective-permute-start.9 = (bf16[48,1536]{1,0:T(8,128)(2,1)S(1)}, bf16[48,1536]{1,0:T(8,128)(2,1)S(1)}, u32[]{:S(2)}, u32[]{:S(2)}) collective-permute-start(bf16[48,1536]{1,0:T(8,128)(2,1)S(1)} %copy-done.45), channel_id=1, source_target_pairs={{0,24},{8,16},{16,8},{24,0},{1,25},{9,17},{17,9},{25,1},{2,26},{10... | collective-permute-start | bytes 442376 | tf_op jit(solution)/shard_map/ppermute | solution.py:38
  22.1 16.2 %collective-permute-start = (bf16[320,1536]{1,0:T(8,128)(2,1)S(1)}, bf16[320,1536]{1,0:T(8,128)(2,1)}, u32[]{:S(2)}, u32[]{:S(2)}) collective-permute-start(bf16[320,1536]{1,0:T(8,128)(2,1)S(1)} %shard_map.222.refs_2_.refs_1_), channel_id=1, source_target_pairs={{0,2},{1,5},{2,0},{3,7},{4,6},{5,1},{6,4},{7,3},{8,10},{9,13},{10,... | collective-permute-start | bytes 2949128 | tf_op jit(solution)/shard_map/ppermute | solution.py:32
  33.0 15.0 %collective-permute-start.1 = (bf16[320,1536]{1,0:T(8,128)(2,1)S(1)}, bf16[320,1536]{1,0:T(8,128)(2,1)}, u32[]{:S(2)}, u32[]{:S(2)}) collective-permute-start(bf16[320,1536]{1,0:T(8,128)(2,1)S(1)} %shard_map.222.refs_2_.refs_1_), channel_id=1, source_target_pairs={{0,4},{1,3},{2,6},{3,1},{4,0},{5,7},{6,2},{7,5},{8,12},{9,11},{10,... | collective-permute-start | bytes 2949128 | tf_op jit(solution)/shard_map/ppermute | solution.py:32
  38.4 25.2 %collective-permute-start.2 = (bf16[320,1536]{1,0:T(8,128)(2,1)}, bf16[320,1536]{1,0:T(8,128)(2,1)}, u32[]{:S(2)}, u32[]{:S(2)}) collective-permute-start(bf16[320,1536]{1,0:T(8,128)(2,1)} %collective-permute-done.refs_3_.refs_2_), channel_id=1, source_target_pairs={{0,4},{1,3},{2,6},{3,1},{4,0},{5,7},{6,2},{7,5},{8,12},{9,11},{10,... | collective-permute-start | bytes 2949128 | tf_op jit(solution)/shard_map/ppermute | solution.py:32
  43.6 27.9 %all-to-all-start.1 = ((bf16[8,48,1536]{2,1,0:T(8,128)(2,1)}), bf16[8,48,1536]{2,1,0:T(8,128)(2,1)S(1)}, u32[]{:S(2)}, u32[]{:S(2)}) async-start(bf16[8,48,1536]{2,1,0:T(8,128)(2,1)} %shard_map.227), calls=%async_computation.1 | async-start | bytes 2359296 | tf_op jit(solution)/shard_map/all_to_all | solution.py:858
  47.3 26.0 %collective-permute-start.3 = (bf16[320,1536]{1,0:T(8,128)(2,1)S(1)}, bf16[320,1536]{1,0:T(8,128)(2,1)}, u32[]{:S(2)}, u32[]{:S(2)}) collective-permute-start(bf16[320,1536]{1,0:T(8,128)(2,1)S(1)} %shard_map.222.refs_2_.refs_1_), channel_id=1, source_target_pairs={{0,1},{1,0},{2,3},{3,2},{4,5},{5,4},{6,7},{7,6},{8,9},{9,8},{10,11... | collective-permute-start | bytes 2949128 | tf_op jit(solution)/shard_map/ppermute | solution.py:38
  47.7 21.0 %collective-permute-start.10 = (bf16[64,1536]{1,0:T(8,128)(2,1)S(1)}, bf16[64,1536]{1,0:T(8,128)(2,1)S(1)}, u32[]{:S(2)}, u32[]{:S(2)}) collective-permute-start(bf16[64,1536]{1,0:T(8,128)(2,1)S(1)} %bitcast.45), channel_id=1, source_target_pairs={{0,8},{8,0},{16,24},{24,16},{1,9},{9,1},{17,25},{25,17},{2,10},{10... | collective-permute-start | bytes 589832 | tf_op jit(solution)/shard_map/ppermute | solution.py:38
  47.7 25.6 %collective-permute-start.4 = (bf16[320,1536]{1,0:T(8,128)(2,1)}, bf16[320,1536]{1,0:T(8,128)(2,1)}, u32[]{:S(2)}, u32[]{:S(2)}) collective-permute-start(bf16[320,1536]{1,0:T(8,128)(2,1)} %collective-permute-done.refs_3_.refs_2_), channel_id=1, source_target_pairs={{0,1},{1,0},{2,3},{3,2},{4,5},{5,4},{6,7},{7,6},{8,9},{9,8},{10,11... | collective-permute-start | bytes 2949128 | tf_op jit(solution)/shard_map/ppermute | solution.py:38
  48.0 25.3 %collective-permute-start.5 = (bf16[320,1536]{1,0:T(8,128)(2,1)}, bf16[320,1536]{1,0:T(8,128)(2,1)}, u32[]{:S(2)}, u32[]{:S(2)}) collective-permute-start(bf16[320,1536]{1,0:T(8,128)(2,1)} %collective-permute-done.1.refs_4_.refs_3_), channel_id=1, source_target_pairs={{0,1},{1,0},{2,3},{3,2},{4,5},{5,4},{6,7},{7,6},{8,9},{9,8},{10,11... | collective-permute-start | bytes 2949128 | tf_op jit(solution)/shard_map/ppermute | solution.py:38
  63.6 9.8 %collective-permute-start.6 = (bf16[320,1536]{1,0:T(8,128)(2,1)}, bf16[320,1536]{1,0:T(8,128)(2,1)}, u32[]{:S(2)}, u32[]{:S(2)}) collective-permute-start(bf16[320,1536]{1,0:T(8,128)(2,1)} %collective-permute-done.2.refs_5_.refs_4_), channel_id=1, source_target_pairs={{0,1},{1,0},{2,3},{3,2},{4,5},{5,4},{6,7},{7,6},{8,9},{9,8},{10,11... | collective-permute-start | bytes 2949128 | tf_op jit(solution)/shard_map/ppermute | solution.py:38
  68.7 31.1 %collective-permute-start.14 = (bf16[4,48,1536]{2,1,0:T(8,128)(2,1)S(1)}, bf16[4,48,1536]{2,1,0:T(8,128)(2,1)}, u32[]{:S(2)}, u32[]{:S(2)}) collective-permute-start(bf16[4,48,1536]{2,1,0:T(8,128)(2,1)S(1)} %pad_maximum_fusion.1.refs_3_.refs_10_), channel_id=1, source_target_pairs={{0,1},{1,0},{2,3},{3,2},{4,5},{5,4},{6,7},{7,6},{8,9},{9,8},{10,11... | collective-permute-start | bytes 1769480 | tf_op jit(solution)/shard_map/ppermute | solution.py:38
  73.3 24.9 %collective-permute-start.11 = (bf16[128,1536]{1,0:T(8,128)(2,1)S(1)}, bf16[128,1536]{1,0:T(8,128)(2,1)}, u32[]{:S(2)}, u32[]{:S(2)}) collective-permute-start(bf16[128,1536]{1,0:T(8,128)(2,1)S(1)} %pad_maximum_fusion.3.refs_4_.refs_0_), channel_id=1, source_target_pairs={{0,2},{1,5},{2,0},{3,7},{4,6},{5,1},{6,4},{7,3},{8,10},{9,13},{10,... | collective-permute-start | bytes 1179656 | tf_op jit(solution)/shard_map/ppermute | solution.py:32
  74.2 24.0 %collective-permute-start.12 = (bf16[128,1536]{1,0:T(8,128)(2,1)S(1)}, bf16[128,1536]{1,0:T(8,128)(2,1)}, u32[]{:S(2)}, u32[]{:S(2)}) collective-permute-start(bf16[128,1536]{1,0:T(8,128)(2,1)S(1)} %pad_maximum_fusion.3.refs_4_.refs_0_), channel_id=1, source_target_pairs={{0,4},{1,3},{2,6},{3,1},{4,0},{5,7},{6,2},{7,5},{8,12},{9,11},{10,... | collective-permute-start | bytes 1179656 | tf_op jit(solution)/shard_map/ppermute | solution.py:32
  81.4 68.7 %all-to-all-start.2 = ((bf16[4,384,768]{2,1,0:T(8,128)(2,1)}), bf16[4,384,768]{2,1,0:T(8,128)(2,1)S(1)}, u32[]{:S(2)}, u32[]{:S(2)}) async-start(bf16[4,384,768]{2,1,0:T(8,128)(2,1)} %pad_maximum_fusion), calls=%async_computation.2 | async-start | bytes 4718592 | tf_op jit(solution)/shard_map/all_to_all | solution.py:863
  98.3 8.1 %collective-permute-start.16 = (bf16[128,1536]{1,0:T(8,128)(2,1)}, bf16[128,1536]{1,0:T(8,128)(2,1)S(1)}, u32[]{:S(2)}, u32[]{:S(2)}) collective-permute-start(bf16[128,1536]{1,0:T(8,128)(2,1)} %collective-permute-done.11.refs_5_.refs_1_), channel_id=1, source_target_pairs={{0,4},{1,3},{2,6},{3,1},{4,0},{5,7},{6,2},{7,5},{8,12},{9,11},{10,... | collective-permute-start | bytes 1179656 | tf_op jit(solution)/shard_map/ppermute | solution.py:32
  104.6 7.8 %collective-permute-start.15 = (bf16[2,64,1536]{2,1,0:T(8,128)(2,1)S(1)}, bf16[2,64,1536]{2,1,0:T(8,128)(2,1)S(1)}, u32[]{:S(2)}, u32[]{:S(2)}) collective-permute-start(bf16[2,64,1536]{2,1,0:T(8,128)(2,1)S(1)} %get-tuple-element.82), channel_id=1, source_target_pairs={{0,4},{1,3},{2,6},{3,1},{4,0},{5,7},{6,2},{7,5},{8,12},{9,11},{10,... | collective-permute-start | bytes 1179656 | tf_op jit(solution)/shard_map/ppermute | solution.py:32
  124.2 15.8 %collective-permute-start.19 = (bf16[32,1536]{1,0:T(8,128)(2,1)S(1)}, bf16[32,1536]{1,0:T(8,128)(2,1)S(1)}, u32[]{:S(2)}, u32[]{:S(2)}) collective-permute-start(bf16[32,1536]{1,0:T(8,128)(2,1)S(1)} %get-tuple-element.145), channel_id=1, source_target_pairs={{0,8},{8,0},{16,24},{24,16},{1,9},{9,1},{17,25},{25,17},{2,10},{10... | collective-permute-start | bytes 294920 | tf_op jit(solution)/shard_map/ppermute | solution.py:38
  140.0 7.8 %collective-permute-start.20 = (bf16[128,1536]{1,0:T(8,128)(2,1)S(1)}, bf16[128,1536]{1,0:T(8,128)(2,1)S(1)}, u32[]{:S(2)}, u32[]{:S(2)}) collective-permute-start(bf16[128,1536]{1,0:T(8,128)(2,1)S(1)} %constant_dynamic-update-slice_fusion.refs_0_), channel_id=1, source_target_pairs={{0,2},{1,5},{2,0},{3,7},{4,6},{5,1},{6,4},{7,3},{8,10},{9,13},{10,... | collective-permute-start | bytes 1179656 | tf_op jit(solution)/shard_map/ppermute | solution.py:32
  141.6 7.8 %collective-permute-start.21 = (bf16[128,1536]{1,0:T(8,128)(2,1)S(1)}, bf16[128,1536]{1,0:T(8,128)(2,1)S(1)}, u32[]{:S(2)}, u32[]{:S(2)}) collective-permute-start(bf16[128,1536]{1,0:T(8,128)(2,1)S(1)} %constant_dynamic-update-slice_fusion.refs_0_), channel_id=1, source_target_pairs={{0,4},{1,3},{2,6},{3,1},{4,0},{5,7},{6,2},{7,5},{8,12},{9,11},{10,... | collective-permute-start | bytes 1179656 | tf_op jit(solution)/shard_map/ppermute | solution.py:32
  150.1 8.0 %collective-permute-start.23 = (bf16[1536,768]{1,0:T(8,128)(2,1)S(1)}, bf16[1536,768]{1,0:T(8,128)(2,1)S(1)}, u32[]{:S(2)}, u32[]{:S(2)}) collective-permute-start(bf16[1536,768]{1,0:T(8,128)(2,1)S(1)} %bitcast.42), channel_id=1, source_target_pairs={{0,1},{1,0},{2,3},{3,2},{4,5},{5,4},{6,7},{7,6},{8,9},{9,8},{10,11... | collective-permute-start | bytes 7077896 | tf_op jit(solution)/shard_map/ppermute | solution.py:38
  150.1 8.0 %collective-permute-start.22 = (bf16[128,1536]{1,0:T(8,128)(2,1)}, bf16[128,1536]{1,0:T(8,128)(2,1)S(1)}, u32[]{:S(2)}, u32[]{:S(2)}) collective-permute-start(bf16[128,1536]{1,0:T(8,128)(2,1)} %copy-done.5), channel_id=1, source_target_pairs={{0,4},{1,3},{2,6},{3,1},{4,0},{5,7},{6,2},{7,5},{8,12},{9,11},{10,... | collective-permute-start | bytes 1179656 | tf_op jit(solution)/shard_map/ppermute | solution.py:32
  151.6 16.5 %collective-permute-start.30 = (bf16[128,1536]{1,0:T(8,128)(2,1)S(1)}, bf16[128,1536]{1,0:T(8,128)(2,1)S(1)}, u32[]{:S(2)}, u32[]{:S(2)}) collective-permute-start(bf16[128,1536]{1,0:T(8,128)(2,1)S(1)} %pad_maximum_fusion.3.refs_4_.refs_0_), channel_id=1, source_target_pairs={{0,1},{1,0},{2,3},{3,2},{4,5},{5,4},{6,7},{7,6},{8,9},{9,8},{10,11... | collective-permute-start | bytes 1179656 | tf_op jit(solution)/shard_map/ppermute | solution.py:38
  151.6 16.6 %collective-permute-start.31 = (bf16[128,1536]{1,0:T(8,128)(2,1)}, bf16[128,1536]{1,0:T(8,128)(2,1)S(1)}, u32[]{:S(2)}, u32[]{:S(2)}) collective-permute-start(bf16[128,1536]{1,0:T(8,128)(2,1)} %collective-permute-done.11.refs_5_.refs_1_), channel_id=1, source_target_pairs={{0,1},{1,0},{2,3},{3,2},{4,5},{5,4},{6,7},{7,6},{8,9},{9,8},{10,11... | collective-permute-start | bytes 1179656 | tf_op jit(solution)/shard_map/ppermute | solution.py:38
  152.1 16.5 %collective-permute-start.32 = (bf16[128,1536]{1,0:T(8,128)(2,1)}, bf16[128,1536]{1,0:T(8,128)(2,1)S(1)}, u32[]{:S(2)}, u32[]{:S(2)}) collective-permute-start(bf16[128,1536]{1,0:T(8,128)(2,1)} %collective-permute-done.12.refs_6_.refs_2_), channel_id=1, source_target_pairs={{0,1},{1,0},{2,3},{3,2},{4,5},{5,4},{6,7},{7,6},{8,9},{9,8},{10,11... | collective-permute-start | bytes 1179656 | tf_op jit(solution)/shard_map/ppermute | solution.py:38
  158.1 10.6 %collective-permute-start.33 = (bf16[128,1536]{1,0:T(8,128)(2,1)S(1)}, bf16[128,1536]{1,0:T(8,128)(2,1)S(1)}, u32[]{:S(2)}, u32[]{:S(2)}) collective-permute-start(bf16[128,1536]{1,0:T(8,128)(2,1)S(1)} %copy-done.4), channel_id=1, source_target_pairs={{0,1},{1,0},{2,3},{3,2},{4,5},{5,4},{6,7},{7,6},{8,9},{9,8},{10,11... | collective-permute-start | bytes 1179656 | tf_op jit(solution)/shard_map/ppermute | solution.py:38
  158.1 11.0 %collective-permute-start.25 = (bf16[128,1536]{1,0:T(8,128)(2,1)S(1)}, bf16[128,1536]{1,0:T(8,128)(2,1)S(1)}, u32[]{:S(2)}, u32[]{:S(2)}) collective-permute-start(bf16[128,1536]{1,0:T(8,128)(2,1)S(1)} %constant_dynamic-update-slice_fusion.refs_0_), channel_id=1, source_target_pairs={{0,1},{1,0},{2,3},{3,2},{4,5},{5,4},{6,7},{7,6},{8,9},{9,8},{10,11... | collective-permute-start | bytes 1179656 | tf_op jit(solution)/shard_map/ppermute | solution.py:38
  168.2 6.3 %collective-permute-start.26 = (bf16[128,1536]{1,0:T(8,128)(2,1)S(1)}, bf16[128,1536]{1,0:T(8,128)(2,1)S(1)}, u32[]{:S(2)}, u32[]{:S(2)}) collective-permute-start(bf16[128,1536]{1,0:T(8,128)(2,1)S(1)} %copy-done.6), channel_id=1, source_target_pairs={{0,1},{1,0},{2,3},{3,2},{4,5},{5,4},{6,7},{7,6},{8,9},{9,8},{10,11... | collective-permute-start | bytes 1179656 | tf_op jit(solution)/shard_map/ppermute | solution.py:38
  169.1 12.0 %collective-permute-start.24 = (bf16[2,128,1536]{2,1,0:T(8,128)(2,1)S(1)}, bf16[2,128,1536]{2,1,0:T(8,128)(2,1)S(1)}, u32[]{:S(2)}, u32[]{:S(2)}) collective-permute-start(bf16[2,128,1536]{2,1,0:T(8,128)(2,1)S(1)} %get-tuple-element.93), channel_id=1, source_target_pairs={{0,4},{1,3},{2,6},{3,1},{4,0},{5,7},{6,2},{7,5},{8,12},{9,11},{10,... | collective-permute-start | bytes 2359304 | tf_op jit(solution)/shard_map/ppermute | solution.py:32
  182.5 7.8 %collective-permute-start.38 = (bf16[1,128,1536]{2,1,0:T(8,128)(2,1)S(1)}, bf16[1,128,1536]{2,1,0:T(8,128)(2,1)S(1)}, u32[]{:S(2)}, u32[]{:S(2)}) collective-permute-start(bf16[1,128,1536]{2,1,0:T(8,128)(2,1)S(1)} %get-tuple-element.99), channel_id=1, source_target_pairs={{0,2},{1,5},{2,0},{3,7},{4,6},{5,1},{6,4},{7,3},{8,10},{9,13},{10,... | collective-permute-start | bytes 1179656 | tf_op jit(solution)/shard_map/ppermute | solution.py:32
  191.3 21.2 %collective-permute-start.35 = (bf16[2,128,1536]{2,1,0:T(8,128)(2,1)S(1)}, bf16[2,128,1536]{2,1,0:T(8,128)(2,1)}, u32[]{:S(2)}, u32[]{:S(2)}) collective-permute-start(bf16[2,128,1536]{2,1,0:T(8,128)(2,1)S(1)} %get-tuple-element.102), channel_id=1, source_target_pairs={{0,4},{1,3},{2,6},{3,1},{4,0},{5,7},{6,2},{7,5},{8,12},{9,11},{10,... | collective-permute-start | bytes 2359304 | tf_op jit(solution)/shard_map/ppermute | solution.py:32
  192.8 51.0 %collective-permute-start.49 = (bf16[1536,640]{1,0:T(8,128)(2,1)}, bf16[1536,640]{1,0:T(8,128)(2,1)}, u32[]{:S(2)}, u32[]{:S(2)}) collective-permute-start(bf16[1536,640]{1,0:T(8,128)(2,1)} %all-gather.2.cloned.1.call-done.refs_10_.refs_19_.refs_4_), channel_id=1, source_target_pairs={{0,1},{1,0},{2,3},{3,2},{4,5},{5,4},{6,7},{7,6},{8,9},{9,8},{10,11... | collective-permute-start | bytes 5898248 | tf_op jit(solution)/shard_map/ppermute | solution.py:38
  199.8 76.8 %all-to-all-start.3 = ((bf16[4,384,768]{2,1,0:T(8,128)(2,1)}), bf16[4,384,768]{2,1,0:T(8,128)(2,1)S(1)}, u32[]{:S(2)}, u32[]{:S(2)}) async-start(bf16[4,384,768]{2,1,0:T(8,128)(2,1)} %bitcast.25), calls=%async_computation.3 | async-start | bytes 4718592 | tf_op jit(solution)/shard_map/all_to_all | solution.py:1011
  206.3 88.1 %reduce-scatter.3.cloned.1.call-start = ((), (), s32[]{:S(2)}) async-start(), calls=%async_computation.9 | async-start | bytes 2457600 | tf_op jit(solution)/shard_map/reduce_scatter | solution.py:1073
  207.8 10.5 %collective-permute-start.41 = (bf16[64,1536]{1,0:T(8,128)(2,1)S(1)}, bf16[64,1536]{1,0:T(8,128)(2,1)S(1)}, u32[]{:S(2)}, u32[]{:S(2)}) collective-permute-start(bf16[64,1536]{1,0:T(8,128)(2,1)S(1)} %get-tuple-element.108.refs_2_.refs_9_), channel_id=1, source_target_pairs={{0,4},{1,3},{2,6},{3,1},{4,0},{5,7},{6,2},{7,5},{8,12},{9,11},{10,... | collective-permute-start | bytes 589832 | tf_op jit(solution)/shard_map/ppermute | solution.py:32
  208.3 10.0 %collective-permute-start.43 = (bf16[64,1536]{1,0:T(8,128)(2,1)S(1)}, bf16[64,1536]{1,0:T(8,128)(2,1)S(1)}, u32[]{:S(2)}, u32[]{:S(2)}) collective-permute-start(bf16[64,1536]{1,0:T(8,128)(2,1)S(1)} %get-tuple-element.108.refs_2_.refs_9_), channel_id=1, source_target_pairs={{0,1},{1,0},{2,3},{3,2},{4,5},{5,4},{6,7},{7,6},{8,9},{9,8},{10,11... | collective-permute-start | bytes 589832 | tf_op jit(solution)/shard_map/ppermute | solution.py:38
  212.5 7.8 %collective-permute-start.42 = (bf16[64,1536]{1,0:T(8,128)(2,1)S(1)}, bf16[64,1536]{1,0:T(8,128)(2,1)S(1)}, u32[]{:S(2)}, u32[]{:S(2)}) collective-permute-start(bf16[64,1536]{1,0:T(8,128)(2,1)S(1)} %collective-permute-done.40.refs_3_.refs_10_), channel_id=1, source_target_pairs={{0,4},{1,3},{2,6},{3,1},{4,0},{5,7},{6,2},{7,5},{8,12},{9,11},{10,... | collective-permute-start | bytes 589832 | tf_op jit(solution)/shard_map/ppermute | solution.py:32
  215.7 16.1 %collective-permute-start.36 = (bf16[1,128,1536]{2,1,0:T(8,128)(2,1)S(1)}, bf16[1,128,1536]{2,1,0:T(8,128)(2,1)S(1)}, u32[]{:S(2)}, u32[]{:S(2)}) collective-permute-start(bf16[1,128,1536]{2,1,0:T(8,128)(2,1)S(1)} %get-tuple-element.104), channel_id=1, source_target_pairs={{0,2},{1,5},{2,0},{3,7},{4,6},{5,1},{6,4},{7,3},{8,10},{9,13},{10,... | collective-permute-start | bytes 1179656 | tf_op jit(solution)/shard_map/ppermute | solution.py:32
  231.6 13.7 %collective-permute-start.47 = (bf16[4,8,32,384]{3,2,1,0:T(8,128)(2,1)}, bf16[4,8,32,384]{3,2,1,0:T(8,128)(2,1)}, u32[]{:S(2)}, u32[]{:S(2)}) collective-permute-start(bf16[4,8,32,384]{3,2,1,0:T(8,128)(2,1)} %get-tuple-element.118), channel_id=1, source_target_pairs={{0,1},{1,0},{2,3},{3,2},{4,5},{5,4},{6,7},{7,6},{8,9},{9,8},{10,11... | collective-permute-start | bytes 2359304 | tf_op jit(solution)/shard_map/ppermute | solution.py:38
  253.8 25.0 %collective-permute-start.50 = (bf16[2,320,1536]{2,1,0:T(8,128)(2,1)}, bf16[2,320,1536]{2,1,0:T(8,128)(2,1)}, u32[]{:S(2)}, u32[]{:S(2)}) collective-permute-start(bf16[2,320,1536]{2,1,0:T(8,128)(2,1)} %get-tuple-element.121), channel_id=1, source_target_pairs={{0,4},{1,3},{2,6},{3,1},{4,0},{5,7},{6,2},{7,5},{8,12},{9,11},{10,... | collective-permute-start | bytes 5898248 | tf_op jit(solution)/shard_map/ppermute | solution.py:32
  255.3 19.6 %collective-permute-start.37 = (bf16[64,1536]{1,0:T(8,128)(2,1)S(1)}, bf16[64,1536]{1,0:T(8,128)(2,1)S(1)}, u32[]{:S(2)}, u32[]{:S(2)}) collective-permute-start(bf16[64,1536]{1,0:T(8,128)(2,1)S(1)} %shard_map.234), channel_id=1, source_target_pairs={{0,8},{8,0},{16,24},{24,16},{1,9},{9,1},{17,25},{25,17},{2,10},{10... | collective-permute-start | bytes 589832 | tf_op jit(solution)/shard_map/ppermute | solution.py:38
  278.8 20.7 %all-to-all-start.4 = ((bf16[8,48,1536]{2,1,0:T(8,128)(2,1)}), bf16[8,48,1536]{2,1,0:T(8,128)(2,1)S(1)}, u32[]{:S(2)}, u32[]{:S(2)}) async-start(bf16[8,48,1536]{2,1,0:T(8,128)(2,1)} %bitcast.27), calls=%async_computation.4 | async-start | bytes 2359296 | tf_op jit(solution)/shard_map/all_to_all | solution.py:1016
  282.6 38.3 %reduce-scatter.5.cloned.1.call-start = ((), (), s32[]{:S(2)}) async-start(), calls=%async_computation.10 | async-start | bytes 737280 | tf_op jit(solution)/shard_map/reduce_scatter | solution.py:1126
  286.4 25.3 %collective-permute-start.51 = (bf16[1,320,1536]{2,1,0:T(8,128)(2,1)}, bf16[1,320,1536]{2,1,0:T(8,128)(2,1)S(1)}, u32[]{:S(2)}, u32[]{:S(2)}) collective-permute-start(bf16[1,320,1536]{2,1,0:T(8,128)(2,1)} %get-tuple-element.125), channel_id=1, source_target_pairs={{0,2},{1,5},{2,0},{3,7},{4,6},{5,1},{6,4},{7,3},{8,10},{9,13},{10,... | collective-permute-start | bytes 2949128 | tf_op jit(solution)/shard_map/ppermute | solution.py:32
  299.5 18.8 %all-to-all-start.5 = ((bf16[8,48,640]{2,1,0:T(8,128)(2,1)}), bf16[8,48,640]{2,1,0:T(8,128)(2,1)S(1)}, u32[]{:S(2)}, u32[]{:S(2)}) async-start(bf16[8,48,640]{2,1,0:T(8,128)(2,1)} %bitcast.68), calls=%async_computation.6 | async-start | bytes 983040 | tf_op jit(solution)/shard_map/all_to_all | solution.py:1118
  (66 other events, 449.6 us)
Sparse Core Ops, SparseCore 0:
  33.1 48.3 all-gather.1
  243.5 50.8 reduce-scatter.2
  296.7 20.3 reduce-scatter.4
where the time goes:
time: 333 us; the launch traced here: 329 us
  waiting for transfers between devices  129 us (39%)
  Pallas kernels  92.8 us (28%)
  starting transfers between devices  69.8 us (21%)
  between operations  14.8 us (4%)
  local copies, waits for them, and re-layouts  14.5 us (4%)
  other arithmetic  8 us (2%)
    pallas_call x25, Pallas kernels, run(): pl.pallas_call(whole, out_shape=[jax.ShapeDtypeStruct(shape, kind) for sh...  92.8 us
    ppermute x20, waiting for transfers between devices, hop(): lax.ppermute(array, 'blk', [(i, i ^ hop_bit(j, i % 2)) for i in range(lax...  61.7 us
    ppermute x33, waiting for transfers between devices, swap(): lax.ppermute(array, axis, [(i, i ^ bit) for i in range(lax.axis_size(axis...  52.9 us
    ppermute x20, starting transfers between devices, hop(): lax.ppermute(array, 'blk', [(i, i ^ hop_bit(j, i % 2)) for i in range(lax...  29.5 us
    ppermute x33, starting transfers between devices, swap(): lax.ppermute(array, axis, [(i, i ^ bit) for i in range(lax.axis_size(axis...  13.5 us
    unnamed x106, local copies, waits for them, and re-layouts  12.9 us
  transfers between devices with their start and end apart: 62, of which 28 were waited for; matrix products, arithmetic and copies ran while one was open for 2% of the time, Pallas kernels for 27%

commit v1 on v0

--- a/solution.py
+++ b/solution.py
@@ -1104,16 +1104,16 @@
     rank = lax.axis_index("blk") % ring
     pieces = [lax.dynamic_index_in_dim(pieces, rank ^ r, 0, False) for r in range(ring)]
     out_rows = jnp.concatenate(pieces, 0).reshape(nd * own, width)
-    media_grad, latents_grad = call(
-        final_kernel, [((block_m, width), F32, "d"), ((block_l, width), F32, "d")], "ddddd", cost=5
-    )(*scatter(parts, [lambda sent: (ffn_rows, resampled), lambda sent: (ffn_slots, out_rows)]), media_flat, lat_flat, mixed_grad)
-
     in_grad, down_grad, ffn_gain_grad = call(
         finish_ffn_kernel,
         [((own, hidden_width), F32, "d")] * 2 + [((own, 128), F32, "d")],
         "ddd",
         cost=3,
     )(ffn_slots, in_weight, gains)
+
+    media_grad, latents_grad = call(
+        final_kernel, [((block_m, width), F32, "d"), ((block_l, width), F32, "d")], "ddddd", cost=5
+    )(*scatter(parts, [lambda sent: (ffn_rows, resampled), lambda sent: (ffn_slots, out_rows)]), after(media_flat, in_grad), lat_flat, mixed_grad)
 
     attn_slots = lax.all_to_all(attn_sum.reshape(nb, own, -1), "blk", 0, 0, tiled=True)
     query_grad, kv_grad, gain_grads = call(

time: 333 us -> 333 us (level)
  no operation moved by 1% of the time
where the time goes in v1:
time: 333 us; the launch traced here: 329 us
  waiting for transfers between devices  129 us (39%)
  Pallas kernels  92.8 us (28%)
  starting transfers between devices  69.8 us (21%)
  between operations  14.8 us (4%)
  local copies, waits for them, and re-layouts  14.5 us (4%)
  other arithmetic  8 us (2%)
    pallas_call x25, Pallas kernels, run(): pl.pallas_call(whole, out_shape=[jax.ShapeDtypeStruct(shape, kind) for sh...  92.8 us
    ppermute x20, waiting for transfers between devices, hop(): lax.ppermute(array, 'blk', [(i, i ^ hop_bit(j, i % 2)) for i in range(lax...  61.7 us
    ppermute x33, waiting for transfers between devices, swap(): lax.ppermute(array, axis, [(i, i ^ bit) for i in range(lax.axis_size(axis...  52.9 us
    ppermute x20, starting transfers between devices, hop(): lax.ppermute(array, 'blk', [(i, i ^ hop_bit(j, i % 2)) for i in range(lax...  29.5 us
    ppermute x33, starting transfers between devices, swap(): lax.ppermute(array, axis, [(i, i ^ bit) for i in range(lax.axis_size(axis...  13.5 us
    unnamed x106, local copies, waits for them, and re-layouts  12.9 us
  transfers between devices with their start and end apart: 62, of which 28 were waited for; matrix products, arithmetic and copies ran while one was open for 2% of the time, Pallas kernels for 27%

profile of v1, /device:TPU:0, one launch (start us, length us, event | category | flops | bytes accessed | tf_op | source)
XLA Modules:
  0.0 329.3 jit_solution(4144627769639667619)
XLA Ops:
  11.3 5.2 %all-to-all-start = ((bf16[8,48,640]{2,1,0:T(8,128)(2,1)}), bf16[8,48,640]{2,1,0:T(8,128)(2,1)S(1)}, u32[]{:S(2)}, u32[]{:S(2)}) async-start(bf16[8,48,640]{2,1,0:T(8,128)(2,1)} %shard_map.221), calls=%async_computation | async-start | bytes 983040 | tf_op jit(solution)/shard_map/all_to_all | solution.py:843
  18.1 2.6 collective-permute-start.8
  22.1 2.0 collective-permute-start
  25.5 6.6 %collective-permute-done.8 = bf16[48,1536]{1,0:T(8,128)(2,1)S(1)} collective-permute-done((bf16[48,1536]{1,0:T(8,128)(2,1)S(1)}, bf16[48,1536]{1,0:T(8,128)(2,1)S(1)}, u32[]{:S(2)}, u32[]{:S(2)}) %collective-permute-start.8) | collective-permute-done | bytes 147488 | tf_op jit(solution)/shard_map/ppermute | solution.py:38
  33.0 2.0 collective-permute-start.1
  35.0 3.4 %collective-permute-done.refs_3_.refs_2_ = bf16[320,1536]{1,0:T(8,128)(2,1)} collective-permute-done((bf16[320,1536]{1,0:T(8,128)(2,1)S(1)}, bf16[320,1536]{1,0:T(8,128)(2,1)}, u32[]{:S(2)}, u32[]{:S(2)}) %collective-permute-start) | collective-permute-done | bytes 983072 | tf_op jit(solution)/shard_map/ppermute | solution.py:32
  38.4 2.6 collective-permute-start.2
  41.0 2.6 shard_map.227
  43.6 3.7 %all-to-all-start.1 = ((bf16[8,48,1536]{2,1,0:T(8,128)(2,1)}), bf16[8,48,1536]{2,1,0:T(8,128)(2,1)S(1)}, u32[]{:S(2)}, u32[]{:S(2)}) async-start(bf16[8,48,1536]{2,1,0:T(8,128)(2,1)} %shard_map.227), calls=%async_computation.1 | async-start | bytes 2359296 | tf_op jit(solution)/shard_map/all_to_all | solution.py:858
  48.3 15.3 %collective-permute-done.2.refs_5_.refs_4_ = bf16[320,1536]{1,0:T(8,128)(2,1)} collective-permute-done((bf16[320,1536]{1,0:T(8,128)(2,1)}, bf16[320,1536]{1,0:T(8,128)(2,1)}, u32[]{:S(2)}, u32[]{:S(2)}) %collective-permute-start.2) | collective-permute-done | bytes 983072 | tf_op jit(solution)/shard_map/ppermute | solution.py:32
  65.6 3.2 collective-permute-done.10
  68.8 2.7 all-to-all-done.1
  75.7 5.8 %all-gather.2.cloned.1.call-done.refs_10_.refs_19_.refs_4_ = bf16[1536,640]{1,0:T(8,128)(2,1)} async-done(((bf16[384,640]{1,0:T(8,128)(2,1)}), bf16[1536,640]{1,0:T(8,128)(2,1)}) %all-gather.2.cloned.1.call-update) | async-done | bytes 1966096 | tf_op jit(solution)/shard_map/all_gather | solution.py:844
  81.4 4.2 %all-to-all-start.2 = ((bf16[4,384,768]{2,1,0:T(8,128)(2,1)}), bf16[4,384,768]{2,1,0:T(8,128)(2,1)S(1)}, u32[]{:S(2)}, u32[]{:S(2)}) async-start(bf16[4,384,768]{2,1,0:T(8,128)(2,1)} %pad_maximum_fusion), calls=%async_computation.2 | async-start | bytes 4718592 | tf_op jit(solution)/shard_map/all_to_all | solution.py:863
  85.7 12.5 %shard_map.223 = (bf16[8,8,32,384]{3,2,1,0:T(8,128)(2,1)}, f32[8,8,8,640]{3,2,1,0:T(8,128)}, f32[8,8,8,256]{3,2,1,0:T(8,128)}, f32[8,128,128]{2,1,0:T(8,128)}, b...) custom-call(s32[10]{0:T(128)} %pad_add_fusion.refs_0_, s32[8]{0:T(128)} %refs_1_.9, bf16[320,1536]{1,0:T(8,128)(2,1)} %copy-done.1, ...), custom_call_target="tpu_custom_call" | custom-call | flops 12650000384 | bytes 39600000 | tf_op jit(solution)/shard_map/pallas_call | solution.py:122
  100.8 3.8 %shard_map.224 = (bf16[2,64,1536]{2,1,0:T(8,128)(2,1)S(1)}, bf16[2,64,1536]{2,1,0:T(8,128)(2,1)S(1)}) custom-call(s32[10]{0:T(128)S(1)} %copy-done.15, bf16[8,64,256]{2,1,0:T(8,128)(2,1)S(1)} %copy-done.10, bf16[4,64,256]{2,1,0:T(8,128)(2,1)S(1)} %collective-permute-done.13.refs_2_, bf16[4,48,1536]{2,1,0:T(8,128)(2,1)S(1)} %pad_maximum_fusion.1.refs_3_.refs_10_, ...), custom_call_target="tpu_custom_call" | custom-call | flops 3449999872 | bytes 10800000 | tf_op jit(solution)/shard_map/pallas_call | solution.py:122
  106.3 6.1 %collective-permute-done.15.refs_1_ = bf16[2,64,1536]{2,1,0:T(8,128)(2,1)S(1)} collective-permute-done((bf16[2,64,1536]{2,1,0:T(8,128)(2,1)S(1)}, bf16[2,64,1536]{2,1,0:T(8,128)(2,1)S(1)}, u32[]{:S(2)}, u32[]{:S(2)}) %collective-permute-start.15) | collective-permute-done | bytes 393248 | tf_op jit(solution)/shard_map/ppermute | solution.py:32
  115.7 4.2 %collective-permute-done.17 = bf16[1,64,1536]{2,1,0:T(8,128)(2,1)S(1)} collective-permute-done((bf16[1,64,1536]{2,1,0:T(8,128)(2,1)S(1)}, bf16[1,64,1536]{2,1,0:T(8,128)(2,1)S(1)}, u32[]{:S(2)}, u32[]{:S(2)}) %collective-permute-start.17) | collective-permute-done | bytes 196640 | tf_op jit(solution)/shard_map/ppermute | solution.py:32
  122.1 2.1 collective-permute-start.18
  124.3 3.1 collective-permute-done.18
  127.5 12.6 %collective-permute-done.19 = bf16[32,1536]{1,0:T(8,128)(2,1)S(1)} collective-permute-done((bf16[32,1536]{1,0:T(8,128)(2,1)S(1)}, bf16[32,1536]{1,0:T(8,128)(2,1)S(1)}, u32[]{:S(2)}, u32[]{:S(2)}) %collective-permute-start.19) | collective-permute-done | bytes 98336 | tf_op jit(solution)/shard_map/ppermute | solution.py:38
  143.0 4.8 %collective-permute-done.20.refs_1_ = bf16[128,1536]{1,0:T(8,128)(2,1)S(1)} collective-permute-done((bf16[128,1536]{1,0:T(8,128)(2,1)S(1)}, bf16[128,1536]{1,0:T(8,128)(2,1)S(1)}, u32[]{:S(2)}, u32[]{:S(2)}) %collective-permute-start.20) | collective-permute-done | bytes 393248 | tf_op jit(solution)/shard_map/ppermute | solution.py:32
  152.1 6.0 %collective-permute-done.22.refs_3_ = bf16[128,1536]{1,0:T(8,128)(2,1)S(1)} collective-permute-done((bf16[128,1536]{1,0:T(8,128)(2,1)}, bf16[128,1536]{1,0:T(8,128)(2,1)S(1)}, u32[]{:S(2)}, u32[]{:S(2)}) %collective-permute-start.22) | collective-permute-done | bytes 393248 | tf_op jit(solution)/shard_map/ppermute | solution.py:32
  160.6 7.4 %shard_map.228 = (bf16[512,384]{1,0:T(8,128)(2,1)S(1)}, bf16[512,384]{1,0:T(8,128)(2,1)S(1)}, bf16[512,384]{1,0:T(8,128)(2,1)S(1)}, bf16[512,384]{1,0:T(8,128)(2...) custom-call(bf16[128,1536]{1,0:T(8,128)(2,1)S(1)} %constant_dynamic-update-slice_fusion.refs_0_, ...), custom_call_target="tpu_custom_call" | custom-call | flops 1150000000 | bytes 3600000 | tf_op jit(solution)/shard_map/pallas_call | solution.py:122
  170.6 3.9 %shard_map.229.refs_10_ = bf16[1536,384]{1,0:T(8,128)(2,1)S(1)} custom-call(bf16[128,1536]{1,0:T(8,128)(2,1)S(1)} %pad_maximum_fusion.3.refs_4_.refs_0_, bf16[128,1536]{1,0:T(8,128)(2,1)} %collective-permute-done.11.refs_5_.refs_1_, bf16[128,1536]{1,0:T(8,128)(2,1)} %collective-permute-done.12.refs_6_.refs_2_, bf16[128,1536]{1,0:T(8,128)(2,1)S(1)} %copy-done.4, ...), custom_call_target="tpu_custom_call" | custom-call | flops 4600000000 | bytes 14400000 | tf_op jit(solution)/shard_map/pallas_call | solution.py:122
  174.5 5.5 %shard_map.230 = bf16[1536,768]{1,0:T(8,128)(2,1)} custom-call(bf16[128,1536]{1,0:T(8,128)(2,1)S(1)} %constant_dynamic-update-slice_fusion.refs_0_, bf16[128,1536]{1,0:T(8,128)(2,1)S(1)} %copy-done.6, bf16[128,1536]{1,0:T(8,128)(2,1)S(1)} %copy-done.9, bf16[128,1536]{1,0:T(8,128)(2,1)S(1)} %collective-permute-done.22.refs_3_, ...), custom_call_target="tpu_custom_call" | custom-call | flops 4600000000 | bytes 14400000 | tf_op jit(solution)/shard_map/pallas_call | solution.py:122
  183.3 2.0 shard_map.232
  185.3 5.0 %collective-permute-done.38 = bf16[1,128,1536]{2,1,0:T(8,128)(2,1)S(1)} collective-permute-done((bf16[1,128,1536]{2,1,0:T(8,128)(2,1)S(1)}, bf16[1,128,1536]{2,1,0:T(8,128)(2,1)S(1)}, u32[]{:S(2)}, u32[]{:S(2)}) %collective-permute-start.38) | collective-permute-done | bytes 393248 | tf_op jit(solution)/shard_map/ppermute | solution.py:32
  192.8 4.1 %collective-permute-done.39.refs_2_ = bf16[64,1536]{1,0:T(8,128)(2,1)S(1)} collective-permute-done((bf16[64,1536]{1,0:T(8,128)(2,1)S(1)}, bf16[64,1536]{1,0:T(8,128)(2,1)S(1)}, u32[]{:S(2)}, u32[]{:S(2)}) %collective-permute-start.39) | collective-permute-done | bytes 196640 | tf_op jit(solution)/shard_map/ppermute | solution.py:38
  196.9 2.1 shard_map.237
  199.8 6.5 %all-to-all-start.3 = ((bf16[4,384,768]{2,1,0:T(8,128)(2,1)}), bf16[4,384,768]{2,1,0:T(8,128)(2,1)S(1)}, u32[]{:S(2)}, u32[]{:S(2)}) async-start(bf16[4,384,768]{2,1,0:T(8,128)(2,1)} %bitcast.25), calls=%async_computation.3 | async-start | bytes 4718592 | tf_op jit(solution)/shard_map/all_to_all | solution.py:1011
  208.3 4.1 %collective-permute-done.40.refs_3_.refs_10_ = bf16[64,1536]{1,0:T(8,128)(2,1)S(1)} collective-permute-done((bf16[64,1536]{1,0:T(8,128)(2,1)S(1)}, bf16[64,1536]{1,0:T(8,128)(2,1)S(1)}, u32[]{:S(2)}, u32[]{:S(2)}) %collective-permute-start.40) | collective-permute-done | bytes 196640 | tf_op jit(solution)/shard_map/ppermute | solution.py:32
  213.7 2.0 shard_map.233
  215.7 2.5 collective-permute-start.36
  222.4 9.2 %shard_map.238 = (bf16[8,8,32,384]{3,2,1,0:T(8,128)(2,1)}, bf16[512,640]{1,0:T(8,128)(2,1)}, bf16[4,8,32,384]{3,2,1,0:T(8,128)(2,1)}, bf16[4,64,640]{2,1,0:T(8,128)(2,1)}) custom-call(s32[10]{0:T(128)} %pad_add_fusion.refs_0_, s32[8]{0:T(128)} %refs_1_.9, bf16[64,1536]{1,0:T(8,128)(2,1)} %copy-done.2, bf16[64,1536]{1,0:T(8,128)(2,1)} %copy-done.36, ...), custom_call_target="tpu_custom_call" | custom-call | flops 1150000000 | bytes 3600000 | tf_op jit(solution)/shard_map/pallas_call | solution.py:122
  231.8 11.6 %shard_map.239 = (bf16[1536,640]{1,0:T(8,128)(2,1)}, bf16[2,48,1536]{2,1,0:T(8,128)(2,1)}, bf16[1,2,48,1536]{3,2,1,0:T(8,128)(2,1)}) custom-call(s32[10]{0:T(128)} %pad_add_fusion.refs_0_, bf16[320,1536]{1,0:T(8,128)(2,1)} %copy-done.1, bf16[320,1536]{1,0:T(8,128)(2,1)} %collective-permute-done.refs_3_.refs_2_, ...), custom_call_target="tpu_custom_call" | custom-call | flops 1150000000 | bytes 3600000 | tf_op jit(solution)/shard_map/pallas_call | solution.py:122
  246.0 7.8 %shard_map.240 = (bf16[2,320,1536]{2,1,0:T(8,128)(2,1)}, bf16[2,320,1536]{2,1,0:T(8,128)(2,1)}) custom-call(bf16[8,8,32,384]{3,2,1,0:T(8,128)(2,1)} %get-tuple-element.118.refs_17_.refs_0_, bf16[512,640]{1,0:T(8,128)(2,1)} %get-tuple-element.116.refs_18_.refs_1_, bf16[4,8,32,384]{3,2,1,0:T(8,128)(2,1)} %collective-permute-done.47.refs_2_, ...), custom_call_target="tpu_custom_call" | custom-call | flops 1150000000 | bytes 3600000 | tf_op jit(solution)/shard_map/pallas_call | solution.py:122
  255.3 2.1 collective-permute-start.37
  257.4 17.5 %collective-permute-done.37.refs_2_ = bf16[64,1536]{1,0:T(8,128)(2,1)S(1)} collective-permute-done((bf16[64,1536]{1,0:T(8,128)(2,1)S(1)}, bf16[64,1536]{1,0:T(8,128)(2,1)S(1)}, u32[]{:S(2)}, u32[]{:S(2)}) %collective-permute-start.37) | collective-permute-done | bytes 196640 | tf_op jit(solution)/shard_map/ppermute | solution.py:38
  278.8 3.8 %all-to-all-start.4 = ((bf16[8,48,1536]{2,1,0:T(8,128)(2,1)}), bf16[8,48,1536]{2,1,0:T(8,128)(2,1)S(1)}, u32[]{:S(2)}, u32[]{:S(2)}) async-start(bf16[8,48,1536]{2,1,0:T(8,128)(2,1)} %bitcast.27), calls=%async_computation.4 | async-start | bytes 2359296 | tf_op jit(solution)/shard_map/all_to_all | solution.py:1016
  282.7 2.7 shard_map.242
  286.4 2.3 collective-permute-start.51
  294.4 5.1 %all-to-all-done.4.refs_0_ = bf16[8,48,1536]{2,1,0:T(8,128)(2,1)S(1)} async-done(((bf16[8,48,1536]{2,1,0:T(8,128)(2,1)}), bf16[8,48,1536]{2,1,0:T(8,128)(2,1)S(1)}, u32[]{:S(2)}, u32[]{:S(2)}) %all-to-all-start.4) | async-done | bytes 1179680 | tf_op jit(solution)/shard_map/all_to_all | solution.py:1016
  299.5 3.5 %all-to-all-start.5 = ((bf16[8,48,640]{2,1,0:T(8,128)(2,1)}), bf16[8,48,640]{2,1,0:T(8,128)(2,1)S(1)}, u32[]{:S(2)}, u32[]{:S(2)}) async-start(bf16[8,48,640]{2,1,0:T(8,128)(2,1)} %bitcast.68), calls=%async_computation.6 | async-start | bytes 983040 | tf_op jit(solution)/shard_map/all_to_all | solution.py:1118
  303.1 8.7 %collective-permute-done.51 = bf16[1,320,1536]{2,1,0:T(8,128)(2,1)S(1)} collective-permute-done((bf16[1,320,1536]{2,1,0:T(8,128)(2,1)}, bf16[1,320,1536]{2,1,0:T(8,128)(2,1)S(1)}, u32[]{:S(2)}, u32[]{:S(2)}) %collective-permute-start.51) | collective-permute-done | bytes 983072 | tf_op jit(solution)/shard_map/ppermute | solution.py:32
  311.7 2.3 shard_map.243
  314.6 3.7 %shard_map.244 = (f32[256,1536]{1,0:T(8,128)}, f32[64,1536]{1,0:T(8,128)}) custom-call(bf16[320,1536]{1,0:T(8,128)(2,1)S(1)} %bitcast.59, bf16[320,1536]{1,0:T(8,128)(2,1)S(1)} %bitcast.48, bf16[256,1536]{1,0:T(8,128)(2,1)S(1)} %bitcast.50, bf16[64,1536]{1,0:T(8,128)(2,1)S(1)} %bitcast.57, f32[64,1536]{1,0:T(8,128)S(1)} %copy-done.34), custom_call_target="tpu_custom_call" | custom-call | flops 5750000128 | bytes 18000000 | tf_op jit(solution)/shard_map/pallas_call | solution.py:122
  318.3 1.9 shard_map.245
  (226 shorter events, 70.4 us)
Async XLA Ops:
  11.3 20.8 %all-to-all-start = ((bf16[8,48,640]{2,1,0:T(8,128)(2,1)}), bf16[8,48,640]{2,1,0:T(8,128)(2,1)S(1)}, u32[]{:S(2)}, u32[]{:S(2)}) async-start(bf16[8,48,640]{2,1,0:T(8,128)(2,1)} %shard_map.221), calls=%async_computation | async-start | bytes 983040 | tf_op jit(solution)/shard_map/all_to_all | solution.py:843
  16.4 65.0 %all-gather.2.cloned.1.call-start = ((), (), s32[]{:S(2)}) async-start(), calls=%async_computation.8 | async-start | bytes 2457600 | tf_op jit(solution)/shard_map/all_gather | solution.py:844
  16.5 9.0 %collective-permute-start.7 = (bf16[48,1536]{1,0:T(8,128)(2,1)S(1)}, bf16[48,1536]{1,0:T(8,128)(2,1)S(1)}, u32[]{:S(2)}, u32[]{:S(2)}) collective-permute-start(bf16[48,1536]{1,0:T(8,128)(2,1)S(1)} %copy-done.45), channel_id=1, source_target_pairs={{0,8},{8,0},{16,24},{24,16},{1,9},{9,1},{17,25},{25,17},{2,10},{10... | collective-permute-start | bytes 442376 | tf_op jit(solution)/shard_map/ppermute | solution.py:38
  18.1 14.0 %collective-permute-start.8 = (bf16[48,1536]{1,0:T(8,128)(2,1)S(1)}, bf16[48,1536]{1,0:T(8,128)(2,1)S(1)}, u32[]{:S(2)}, u32[]{:S(2)}) collective-permute-start(bf16[48,1536]{1,0:T(8,128)(2,1)S(1)} %copy-done.45), channel_id=1, source_target_pairs={{0,16},{8,24},{16,0},{24,8},{1,17},{9,25},{17,1},{25,9},{2,18},{10... | collective-permute-start | bytes 442376 | tf_op jit(solution)/shard_map/ppermute | solution.py:38
  20.7 11.4 %collective-permute-start.9 = (bf16[48,1536]{1,0:T(8,128)(2,1)S(1)}, bf16[48,1536]{1,0:T(8,128)(2,1)S(1)}, u32[]{:S(2)}, u32[]{:S(2)}) collective-permute-start(bf16[48,1536]{1,0:T(8,128)(2,1)S(1)} %copy-done.45), channel_id=1, source_target_pairs={{0,24},{8,16},{16,8},{24,0},{1,25},{9,17},{17,9},{25,1},{2,26},{10... | collective-permute-start | bytes 442376 | tf_op jit(solution)/shard_map/ppermute | solution.py:38
  22.1 16.2 %collective-permute-start = (bf16[320,1536]{1,0:T(8,128)(2,1)S(1)}, bf16[320,1536]{1,0:T(8,128)(2,1)}, u32[]{:S(2)}, u32[]{:S(2)}) collective-permute-start(bf16[320,1536]{1,0:T(8,128)(2,1)S(1)} %shard_map.222.refs_2_.refs_1_), channel_id=1, source_target_pairs={{0,2},{1,5},{2,0},{3,7},{4,6},{5,1},{6,4},{7,3},{8,10},{9,13},{10,... | collective-permute-start | bytes 2949128 | tf_op jit(solution)/shard_map/ppermute | solution.py:32
  33.0 15.0 %collective-permute-start.1 = (bf16[320,1536]{1,0:T(8,128)(2,1)S(1)}, bf16[320,1536]{1,0:T(8,128)(2,1)}, u32[]{:S(2)}, u32[]{:S(2)}) collective-permute-start(bf16[320,1536]{1,0:T(8,128)(2,1)S(1)} %shard_map.222.refs_2_.refs_1_), channel_id=1, source_target_pairs={{0,4},{1,3},{2,6},{3,1},{4,0},{5,7},{6,2},{7,5},{8,12},{9,11},{10,... | collective-permute-start | bytes 2949128 | tf_op jit(solution)/shard_map/ppermute | solution.py:32
  38.4 25.2 %collective-permute-start.2 = (bf16[320,1536]{1,0:T(8,128)(2,1)}, bf16[320,1536]{1,0:T(8,128)(2,1)}, u32[]{:S(2)}, u32[]{:S(2)}) collective-permute-start(bf16[320,1536]{1,0:T(8,128)(2,1)} %collective-permute-done.refs_3_.refs_2_), channel_id=1, source_target_pairs={{0,4},{1,3},{2,6},{3,1},{4,0},{5,7},{6,2},{7,5},{8,12},{9,11},{10,... | collective-permute-start | bytes 2949128 | tf_op jit(solution)/shard_map/ppermute | solution.py:32
  43.6 27.9 %all-to-all-start.1 = ((bf16[8,48,1536]{2,1,0:T(8,128)(2,1)}), bf16[8,48,1536]{2,1,0:T(8,128)(2,1)S(1)}, u32[]{:S(2)}, u32[]{:S(2)}) async-start(bf16[8,48,1536]{2,1,0:T(8,128)(2,1)} %shard_map.227), calls=%async_computation.1 | async-start | bytes 2359296 | tf_op jit(solution)/shard_map/all_to_all | solution.py:858
  47.3 26.0 %collective-permute-start.3 = (bf16[320,1536]{1,0:T(8,128)(2,1)S(1)}, bf16[320,1536]{1,0:T(8,128)(2,1)}, u32[]{:S(2)}, u32[]{:S(2)}) collective-permute-start(bf16[320,1536]{1,0:T(8,128)(2,1)S(1)} %shard_map.222.refs_2_.refs_1_), channel_id=1, source_target_pairs={{0,1},{1,0},{2,3},{3,2},{4,5},{5,4},{6,7},{7,6},{8,9},{9,8},{10,11... | collective-permute-start | bytes 2949128 | tf_op jit(solution)/shard_map/ppermute | solution.py:38
  47.7 21.0 %collective-permute-start.10 = (bf16[64,1536]{1,0:T(8,128)(2,1)S(1)}, bf16[64,1536]{1,0:T(8,128)(2,1)S(1)}, u32[]{:S(2)}, u32[]{:S(2)}) collective-permute-start(bf16[64,1536]{1,0:T(8,128)(2,1)S(1)} %bitcast.45), channel_id=1, source_target_pairs={{0,8},{8,0},{16,24},{24,16},{1,9},{9,1},{17,25},{25,17},{2,10},{10... | collective-permute-start | bytes 589832 | tf_op jit(solution)/shard_map/ppermute | solution.py:38
  47.7 25.6 %collective-permute-start.4 = (bf16[320,1536]{1,0:T(8,128)(2,1)}, bf16[320,1536]{1,0:T(8,128)(2,1)}, u32[]{:S(2)}, u32[]{:S(2)}) collective-permute-start(bf16[320,1536]{1,0:T(8,128)(2,1)} %collective-permute-done.refs_3_.refs_2_), channel_id=1, source_target_pairs={{0,1},{1,0},{2,3},{3,2},{4,5},{5,4},{6,7},{7,6},{8,9},{9,8},{10,11... | collective-permute-start | bytes 2949128 | tf_op jit(solution)/shard_map/ppermute | solution.py:38
  48.0 25.3 %collective-permute-start.5 = (bf16[320,1536]{1,0:T(8,128)(2,1)}, bf16[320,1536]{1,0:T(8,128)(2,1)}, u32[]{:S(2)}, u32[]{:S(2)}) collective-permute-start(bf16[320,1536]{1,0:T(8,128)(2,1)} %collective-permute-done.1.refs_4_.refs_3_), channel_id=1, source_target_pairs={{0,1},{1,0},{2,3},{3,2},{4,5},{5,4},{6,7},{7,6},{8,9},{9,8},{10,11... | collective-permute-start | bytes 2949128 | tf_op jit(solution)/shard_map/ppermute | solution.py:38
  63.6 9.8 %collective-permute-start.6 = (bf16[320,1536]{1,0:T(8,128)(2,1)}, bf16[320,1536]{1,0:T(8,128)(2,1)}, u32[]{:S(2)}, u32[]{:S(2)}) collective-permute-start(bf16[320,1536]{1,0:T(8,128)(2,1)} %collective-permute-done.2.refs_5_.refs_4_), channel_id=1, source_target_pairs={{0,1},{1,0},{2,3},{3,2},{4,5},{5,4},{6,7},{7,6},{8,9},{9,8},{10,11... | collective-permute-start | bytes 2949128 | tf_op jit(solution)/shard_map/ppermute | solution.py:38
  68.7 31.1 %collective-permute-start.14 = (bf16[4,48,1536]{2,1,0:T(8,128)(2,1)S(1)}, bf16[4,48,1536]{2,1,0:T(8,128)(2,1)}, u32[]{:S(2)}, u32[]{:S(2)}) collective-permute-start(bf16[4,48,1536]{2,1,0:T(8,128)(2,1)S(1)} %pad_maximum_fusion.1.refs_3_.refs_10_), channel_id=1, source_target_pairs={{0,1},{1,0},{2,3},{3,2},{4,5},{5,4},{6,7},{7,6},{8,9},{9,8},{10,11... | collective-permute-start | bytes 1769480 | tf_op jit(solution)/shard_map/ppermute | solution.py:38
  73.3 24.9 %collective-permute-start.11 = (bf16[128,1536]{1,0:T(8,128)(2,1)S(1)}, bf16[128,1536]{1,0:T(8,128)(2,1)}, u32[]{:S(2)}, u32[]{:S(2)}) collective-permute-start(bf16[128,1536]{1,0:T(8,128)(2,1)S(1)} %pad_maximum_fusion.3.refs_4_.refs_0_), channel_id=1, source_target_pairs={{0,2},{1,5},{2,0},{3,7},{4,6},{5,1},{6,4},{7,3},{8,10},{9,13},{10,... | collective-permute-start | bytes 1179656 | tf_op jit(solution)/shard_map/ppermute | solution.py:32
  74.2 24.0 %collective-permute-start.12 = (bf16[128,1536]{1,0:T(8,128)(2,1)S(1)}, bf16[128,1536]{1,0:T(8,128)(2,1)}, u32[]{:S(2)}, u32[]{:S(2)}) collective-permute-start(bf16[128,1536]{1,0:T(8,128)(2,1)S(1)} %pad_maximum_fusion.3.refs_4_.refs_0_), channel_id=1, source_target_pairs={{0,4},{1,3},{2,6},{3,1},{4,0},{5,7},{6,2},{7,5},{8,12},{9,11},{10,... | collective-permute-start | bytes 1179656 | tf_op jit(solution)/shard_map/ppermute | solution.py:32
  81.4 68.7 %all-to-all-start.2 = ((bf16[4,384,768]{2,1,0:T(8,128)(2,1)}), bf16[4,384,768]{2,1,0:T(8,128)(2,1)S(1)}, u32[]{:S(2)}, u32[]{:S(2)}) async-start(bf16[4,384,768]{2,1,0:T(8,128)(2,1)} %pad_maximum_fusion), calls=%async_computation.2 | async-start | bytes 4718592 | tf_op jit(solution)/shard_map/all_to_all | solution.py:863
  98.3 8.1 %collective-permute-start.16 = (bf16[128,1536]{1,0:T(8,128)(2,1)}, bf16[128,1536]{1,0:T(8,128)(2,1)S(1)}, u32[]{:S(2)}, u32[]{:S(2)}) collective-permute-start(bf16[128,1536]{1,0:T(8,128)(2,1)} %collective-permute-done.11.refs_5_.refs_1_), channel_id=1, source_target_pairs={{0,4},{1,3},{2,6},{3,1},{4,0},{5,7},{6,2},{7,5},{8,12},{9,11},{10,... | collective-permute-start | bytes 1179656 | tf_op jit(solution)/shard_map/ppermute | solution.py:32
  104.6 7.8 %collective-permute-start.15 = (bf16[2,64,1536]{2,1,0:T(8,128)(2,1)S(1)}, bf16[2,64,1536]{2,1,0:T(8,128)(2,1)S(1)}, u32[]{:S(2)}, u32[]{:S(2)}) collective-permute-start(bf16[2,64,1536]{2,1,0:T(8,128)(2,1)S(1)} %get-tuple-element.83), channel_id=1, source_target_pairs={{0,4},{1,3},{2,6},{3,1},{4,0},{5,7},{6,2},{7,5},{8,12},{9,11},{10,... | collective-permute-start | bytes 1179656 | tf_op jit(solution)/shard_map/ppermute | solution.py:32
  124.2 15.8 %collective-permute-start.19 = (bf16[32,1536]{1,0:T(8,128)(2,1)S(1)}, bf16[32,1536]{1,0:T(8,128)(2,1)S(1)}, u32[]{:S(2)}, u32[]{:S(2)}) collective-permute-start(bf16[32,1536]{1,0:T(8,128)(2,1)S(1)} %get-tuple-element.147), channel_id=1, source_target_pairs={{0,8},{8,0},{16,24},{24,16},{1,9},{9,1},{17,25},{25,17},{2,10},{10... | collective-permute-start | bytes 294920 | tf_op jit(solution)/shard_map/ppermute | solution.py:38
  140.0 7.8 %collective-permute-start.20 = (bf16[128,1536]{1,0:T(8,128)(2,1)S(1)}, bf16[128,1536]{1,0:T(8,128)(2,1)S(1)}, u32[]{:S(2)}, u32[]{:S(2)}) collective-permute-start(bf16[128,1536]{1,0:T(8,128)(2,1)S(1)} %constant_dynamic-update-slice_fusion.refs_0_), channel_id=1, source_target_pairs={{0,2},{1,5},{2,0},{3,7},{4,6},{5,1},{6,4},{7,3},{8,10},{9,13},{10,... | collective-permute-start | bytes 1179656 | tf_op jit(solution)/shard_map/ppermute | solution.py:32
  141.6 7.8 %collective-permute-start.21 = (bf16[128,1536]{1,0:T(8,128)(2,1)S(1)}, bf16[128,1536]{1,0:T(8,128)(2,1)S(1)}, u32[]{:S(2)}, u32[]{:S(2)}) collective-permute-start(bf16[128,1536]{1,0:T(8,128)(2,1)S(1)} %constant_dynamic-update-slice_fusion.refs_0_), channel_id=1, source_target_pairs={{0,4},{1,3},{2,6},{3,1},{4,0},{5,7},{6,2},{7,5},{8,12},{9,11},{10,... | collective-permute-start | bytes 1179656 | tf_op jit(solution)/shard_map/ppermute | solution.py:32
  150.1 8.0 %collective-permute-start.23 = (bf16[1536,768]{1,0:T(8,128)(2,1)S(1)}, bf16[1536,768]{1,0:T(8,128)(2,1)S(1)}, u32[]{:S(2)}, u32[]{:S(2)}) collective-permute-start(bf16[1536,768]{1,0:T(8,128)(2,1)S(1)} %bitcast.42), channel_id=1, source_target_pairs={{0,1},{1,0},{2,3},{3,2},{4,5},{5,4},{6,7},{7,6},{8,9},{9,8},{10,11... | collective-permute-start | bytes 7077896 | tf_op jit(solution)/shard_map/ppermute | solution.py:38
  150.1 8.0 %collective-permute-start.22 = (bf16[128,1536]{1,0:T(8,128)(2,1)}, bf16[128,1536]{1,0:T(8,128)(2,1)S(1)}, u32[]{:S(2)}, u32[]{:S(2)}) collective-permute-start(bf16[128,1536]{1,0:T(8,128)(2,1)} %copy-done.5), channel_id=1, source_target_pairs={{0,4},{1,3},{2,6},{3,1},{4,0},{5,7},{6,2},{7,5},{8,12},{9,11},{10,... | collective-permute-start | bytes 1179656 | tf_op jit(solution)/shard_map/ppermute | solution.py:32
  151.6 16.5 %collective-permute-start.30 = (bf16[128,1536]{1,0:T(8,128)(2,1)S(1)}, bf16[128,1536]{1,0:T(8,128)(2,1)S(1)}, u32[]{:S(2)}, u32[]{:S(2)}) collective-permute-start(bf16[128,1536]{1,0:T(8,128)(2,1)S(1)} %pad_maximum_fusion.3.refs_4_.refs_0_), channel_id=1, source_target_pairs={{0,1},{1,0},{2,3},{3,2},{4,5},{5,4},{6,7},{7,6},{8,9},{9,8},{10,11... | collective-permute-start | bytes 1179656 | tf_op jit(solution)/shard_map/ppermute | solution.py:38
  151.6 16.6 %collective-permute-start.31 = (bf16[128,1536]{1,0:T(8,128)(2,1)}, bf16[128,1536]{1,0:T(8,128)(2,1)S(1)}, u32[]{:S(2)}, u32[]{:S(2)}) collective-permute-start(bf16[128,1536]{1,0:T(8,128)(2,1)} %collective-permute-done.11.refs_5_.refs_1_), channel_id=1, source_target_pairs={{0,1},{1,0},{2,3},{3,2},{4,5},{5,4},{6,7},{7,6},{8,9},{9,8},{10,11... | collective-permute-start | bytes 1179656 | tf_op jit(solution)/shard_map/ppermute | solution.py:38
  152.1 16.5 %collective-permute-start.32 = (bf16[128,1536]{1,0:T(8,128)(2,1)}, bf16[128,1536]{1,0:T(8,128)(2,1)S(1)}, u32[]{:S(2)}, u32[]{:S(2)}) collective-permute-start(bf16[128,1536]{1,0:T(8,128)(2,1)} %collective-permute-done.12.refs_6_.refs_2_), channel_id=1, source_target_pairs={{0,1},{1,0},{2,3},{3,2},{4,5},{5,4},{6,7},{7,6},{8,9},{9,8},{10,11... | collective-permute-start | bytes 1179656 | tf_op jit(solution)/shard_map/ppermute | solution.py:38
  158.1 10.6 %collective-permute-start.33 = (bf16[128,1536]{1,0:T(8,128)(2,1)S(1)}, bf16[128,1536]{1,0:T(8,128)(2,1)S(1)}, u32[]{:S(2)}, u32[]{:S(2)}) collective-permute-start(bf16[128,1536]{1,0:T(8,128)(2,1)S(1)} %copy-done.4), channel_id=1, source_target_pairs={{0,1},{1,0},{2,3},{3,2},{4,5},{5,4},{6,7},{7,6},{8,9},{9,8},{10,11... | collective-permute-start | bytes 1179656 | tf_op jit(solution)/shard_map/ppermute | solution.py:38
  158.1 11.0 %collective-permute-start.25 = (bf16[128,1536]{1,0:T(8,128)(2,1)S(1)}, bf16[128,1536]{1,0:T(8,128)(2,1)S(1)}, u32[]{:S(2)}, u32[]{:S(2)}) collective-permute-start(bf16[128,1536]{1,0:T(8,128)(2,1)S(1)} %constant_dynamic-update-slice_fusion.refs_0_), channel_id=1, source_target_pairs={{0,1},{1,0},{2,3},{3,2},{4,5},{5,4},{6,7},{7,6},{8,9},{9,8},{10,11... | collective-permute-start | bytes 1179656 | tf_op jit(solution)/shard_map/ppermute | solution.py:38
  168.2 6.3 %collective-permute-start.26 = (bf16[128,1536]{1,0:T(8,128)(2,1)S(1)}, bf16[128,1536]{1,0:T(8,128)(2,1)S(1)}, u32[]{:S(2)}, u32[]{:S(2)}) collective-permute-start(bf16[128,1536]{1,0:T(8,128)(2,1)S(1)} %copy-done.6), channel_id=1, source_target_pairs={{0,1},{1,0},{2,3},{3,2},{4,5},{5,4},{6,7},{7,6},{8,9},{9,8},{10,11... | collective-permute-start | bytes 1179656 | tf_op jit(solution)/shard_map/ppermute | solution.py:38
  169.1 12.0 %collective-permute-start.24 = (bf16[2,128,1536]{2,1,0:T(8,128)(2,1)S(1)}, bf16[2,128,1536]{2,1,0:T(8,128)(2,1)S(1)}, u32[]{:S(2)}, u32[]{:S(2)}) collective-permute-start(bf16[2,128,1536]{2,1,0:T(8,128)(2,1)S(1)} %get-tuple-element.94), channel_id=1, source_target_pairs={{0,4},{1,3},{2,6},{3,1},{4,0},{5,7},{6,2},{7,5},{8,12},{9,11},{10,... | collective-permute-start | bytes 2359304 | tf_op jit(solution)/shard_map/ppermute | solution.py:32
  182.5 7.8 %collective-permute-start.38 = (bf16[1,128,1536]{2,1,0:T(8,128)(2,1)S(1)}, bf16[1,128,1536]{2,1,0:T(8,128)(2,1)S(1)}, u32[]{:S(2)}, u32[]{:S(2)}) collective-permute-start(bf16[1,128,1536]{2,1,0:T(8,128)(2,1)S(1)} %get-tuple-element.100), channel_id=1, source_target_pairs={{0,2},{1,5},{2,0},{3,7},{4,6},{5,1},{6,4},{7,3},{8,10},{9,13},{10,... | collective-permute-start | bytes 1179656 | tf_op jit(solution)/shard_map/ppermute | solution.py:32
  191.3 21.2 %collective-permute-start.35 = (bf16[2,128,1536]{2,1,0:T(8,128)(2,1)S(1)}, bf16[2,128,1536]{2,1,0:T(8,128)(2,1)}, u32[]{:S(2)}, u32[]{:S(2)}) collective-permute-start(bf16[2,128,1536]{2,1,0:T(8,128)(2,1)S(1)} %get-tuple-element.103), channel_id=1, source_target_pairs={{0,4},{1,3},{2,6},{3,1},{4,0},{5,7},{6,2},{7,5},{8,12},{9,11},{10,... | collective-permute-start | bytes 2359304 | tf_op jit(solution)/shard_map/ppermute | solution.py:32
  192.8 51.0 %collective-permute-start.49 = (bf16[1536,640]{1,0:T(8,128)(2,1)}, bf16[1536,640]{1,0:T(8,128)(2,1)}, u32[]{:S(2)}, u32[]{:S(2)}) collective-permute-start(bf16[1536,640]{1,0:T(8,128)(2,1)} %all-gather.2.cloned.1.call-done.refs_10_.refs_19_.refs_4_), channel_id=1, source_target_pairs={{0,1},{1,0},{2,3},{3,2},{4,5},{5,4},{6,7},{7,6},{8,9},{9,8},{10,11... | collective-permute-start | bytes 5898248 | tf_op jit(solution)/shard_map/ppermute | solution.py:38
  199.8 76.8 %all-to-all-start.3 = ((bf16[4,384,768]{2,1,0:T(8,128)(2,1)}), bf16[4,384,768]{2,1,0:T(8,128)(2,1)S(1)}, u32[]{:S(2)}, u32[]{:S(2)}) async-start(bf16[4,384,768]{2,1,0:T(8,128)(2,1)} %bitcast.25), calls=%async_computation.3 | async-start | bytes 4718592 | tf_op jit(solution)/shard_map/all_to_all | solution.py:1011
  206.3 88.1 %reduce-scatter.3.cloned.1.call-start = ((), (), s32[]{:S(2)}) async-start(), calls=%async_computation.9 | async-start | bytes 2457600 | tf_op jit(solution)/shard_map/reduce_scatter | solution.py:1073
  207.8 10.5 %collective-permute-start.41 = (bf16[64,1536]{1,0:T(8,128)(2,1)S(1)}, bf16[64,1536]{1,0:T(8,128)(2,1)S(1)}, u32[]{:S(2)}, u32[]{:S(2)}) collective-permute-start(bf16[64,1536]{1,0:T(8,128)(2,1)S(1)} %get-tuple-element.109.refs_2_.refs_9_), channel_id=1, source_target_pairs={{0,4},{1,3},{2,6},{3,1},{4,0},{5,7},{6,2},{7,5},{8,12},{9,11},{10,... | collective-permute-start | bytes 589832 | tf_op jit(solution)/shard_map/ppermute | solution.py:32
  208.3 10.0 %collective-permute-start.43 = (bf16[64,1536]{1,0:T(8,128)(2,1)S(1)}, bf16[64,1536]{1,0:T(8,128)(2,1)S(1)}, u32[]{:S(2)}, u32[]{:S(2)}) collective-permute-start(bf16[64,1536]{1,0:T(8,128)(2,1)S(1)} %get-tuple-element.109.refs_2_.refs_9_), channel_id=1, source_target_pairs={{0,1},{1,0},{2,3},{3,2},{4,5},{5,4},{6,7},{7,6},{8,9},{9,8},{10,11... | collective-permute-start | bytes 589832 | tf_op jit(solution)/shard_map/ppermute | solution.py:38
  212.5 7.8 %collective-permute-start.42 = (bf16[64,1536]{1,0:T(8,128)(2,1)S(1)}, bf16[64,1536]{1,0:T(8,128)(2,1)S(1)}, u32[]{:S(2)}, u32[]{:S(2)}) collective-permute-start(bf16[64,1536]{1,0:T(8,128)(2,1)S(1)} %collective-permute-done.40.refs_3_.refs_10_), channel_id=1, source_target_pairs={{0,4},{1,3},{2,6},{3,1},{4,0},{5,7},{6,2},{7,5},{8,12},{9,11},{10,... | collective-permute-start | bytes 589832 | tf_op jit(solution)/shard_map/ppermute | solution.py:32
  215.7 16.1 %collective-permute-start.36 = (bf16[1,128,1536]{2,1,0:T(8,128)(2,1)S(1)}, bf16[1,128,1536]{2,1,0:T(8,128)(2,1)S(1)}, u32[]{:S(2)}, u32[]{:S(2)}) collective-permute-start(bf16[1,128,1536]{2,1,0:T(8,128)(2,1)S(1)} %get-tuple-element.105), channel_id=1, source_target_pairs={{0,2},{1,5},{2,0},{3,7},{4,6},{5,1},{6,4},{7,3},{8,10},{9,13},{10,... | collective-permute-start | bytes 1179656 | tf_op jit(solution)/shard_map/ppermute | solution.py:32
  231.6 13.7 %collective-permute-start.47 = (bf16[4,8,32,384]{3,2,1,0:T(8,128)(2,1)}, bf16[4,8,32,384]{3,2,1,0:T(8,128)(2,1)}, u32[]{:S(2)}, u32[]{:S(2)}) collective-permute-start(bf16[4,8,32,384]{3,2,1,0:T(8,128)(2,1)} %get-tuple-element.119), channel_id=1, source_target_pairs={{0,1},{1,0},{2,3},{3,2},{4,5},{5,4},{6,7},{7,6},{8,9},{9,8},{10,11... | collective-permute-start | bytes 2359304 | tf_op jit(solution)/shard_map/ppermute | solution.py:38
  253.8 25.0 %collective-permute-start.50 = (bf16[2,320,1536]{2,1,0:T(8,128)(2,1)}, bf16[2,320,1536]{2,1,0:T(8,128)(2,1)}, u32[]{:S(2)}, u32[]{:S(2)}) collective-permute-start(bf16[2,320,1536]{2,1,0:T(8,128)(2,1)} %get-tuple-element.122), channel_id=1, source_target_pairs={{0,4},{1,3},{2,6},{3,1},{4,0},{5,7},{6,2},{7,5},{8,12},{9,11},{10,... | collective-permute-start | bytes 5898248 | tf_op jit(solution)/shard_map/ppermute | solution.py:32
  255.3 19.6 %collective-permute-start.37 = (bf16[64,1536]{1,0:T(8,128)(2,1)S(1)}, bf16[64,1536]{1,0:T(8,128)(2,1)S(1)}, u32[]{:S(2)}, u32[]{:S(2)}) collective-permute-start(bf16[64,1536]{1,0:T(8,128)(2,1)S(1)} %shard_map.234), channel_id=1, source_target_pairs={{0,8},{8,0},{16,24},{24,16},{1,9},{9,1},{17,25},{25,17},{2,10},{10... | collective-permute-start | bytes 589832 | tf_op jit(solution)/shard_map/ppermute | solution.py:38
  278.8 20.7 %all-to-all-start.4 = ((bf16[8,48,1536]{2,1,0:T(8,128)(2,1)}), bf16[8,48,1536]{2,1,0:T(8,128)(2,1)S(1)}, u32[]{:S(2)}, u32[]{:S(2)}) async-start(bf16[8,48,1536]{2,1,0:T(8,128)(2,1)} %bitcast.27), calls=%async_computation.4 | async-start | bytes 2359296 | tf_op jit(solution)/shard_map/all_to_all | solution.py:1016
  282.6 38.3 %reduce-scatter.5.cloned.1.call-start = ((), (), s32[]{:S(2)}) async-start(), calls=%async_computation.10 | async-start | bytes 737280 | tf_op jit(solution)/shard_map/reduce_scatter | solution.py:1126
  286.4 25.3 %collective-permute-start.51 = (bf16[1,320,1536]{2,1,0:T(8,128)(2,1)}, bf16[1,320,1536]{2,1,0:T(8,128)(2,1)S(1)}, u32[]{:S(2)}, u32[]{:S(2)}) collective-permute-start(bf16[1,320,1536]{2,1,0:T(8,128)(2,1)} %get-tuple-element.126), channel_id=1, source_target_pairs={{0,2},{1,5},{2,0},{3,7},{4,6},{5,1},{6,4},{7,3},{8,10},{9,13},{10,... | collective-permute-start | bytes 2949128 | tf_op jit(solution)/shard_map/ppermute | solution.py:32
  299.5 18.8 %all-to-all-start.5 = ((bf16[8,48,640]{2,1,0:T(8,128)(2,1)}), bf16[8,48,640]{2,1,0:T(8,128)(2,1)S(1)}, u32[]{:S(2)}, u32[]{:S(2)}) async-start(bf16[8,48,640]{2,1,0:T(8,128)(2,1)} %bitcast.68), calls=%async_computation.6 | async-start | bytes 983040 | tf_op jit(solution)/shard_map/all_to_all | solution.py:1118
  (66 other events, 449.6 us)
Sparse Core Ops, SparseCore 0:
  33.1 48.3 all-gather.1
  243.5 50.8 reduce-scatter.2
  296.7 20.3 reduce-scatter.4

commit v2 on v1

--- a/solution.py
+++ b/solution.py
@@ -860,7 +860,7 @@
     by_plane = jnp.stack(
         [ffn_mine[:, d % 2 * 2 * part : (d % 2 + 1) * 2 * part] for d in range(nd)]
     )
-    ffn_w = lax.all_to_all(after(by_plane, *slots, attn_w, cot_pair), "dp", 0, 0, tiled=True)
+    ffn_w = lax.all_to_all(after(by_plane, *slots, cot_pair), "dp", 0, 0, tiled=True)
     ffn_w = ffn_w.reshape(width, 2 * part)
 
     if quick:
@@ -921,7 +921,7 @@
     in_kind = gather_kind(
         jnp.concatenate([ffn_in, swap(ffn_in[:mid], 1, "dp"), swap(ffn_in[mid:], 1, "dp")], 0)
     )
-    ffn_far = swap(after(ffn_w, *in_kind[1:3]), 1)
+    ffn_far = swap(after(ffn_w, *in_kind[1:2]), 1)
     if part % 128:
         ffn_sides = [
             jnp.concatenate([ffn_w[:, i * part : (i + 1) * part], ffn_far[:, i * part : (i + 1) * part]], 1)
@@ -1108,7 +1108,7 @@
         finish_ffn_kernel,
         [((own, hidden_width), F32, "d")] * 2 + [((own, 128), F32, "d")],
         "ddd",
-        cost=3,
+        cost=8,
     )(ffn_slots, in_weight, gains)
 
     media_grad, latents_grad = call(

time: 333 us -> 323 us (0.970)
  waiting for transfers between devices: 129 us -> 123 us
  local copies, waits for them, and re-layouts: 14.5 us -> 10.6 us
    ppermute x33, waiting for transfers between devices: 52.9 us -> 39.9 us  [swap(): lax.ppermute(array, axis, [(i, i ^ bit) for i in range(lax.axis_size(axis...]
    ppermute x20, waiting for transfers between devices: 61.7 us -> 72.5 us  [hop(): lax.ppermute(array, 'blk', [(i, i ^ hop_bit(j, i % 2)) for i in range(lax...]
    all_to_all x1, waiting for transfers between devices: 0.01 us -> 6.47 us  [body(): lax.all_to_all(after(made['both'], branch).reshape(nd, plane, 2 * part),...]
    all_gather x1, waiting for transfers between devices: 5.79 us -> 0.38 us  [body(): attn_w = lax.all_gather(after(mine, *out_near), 'dp', axis=0, tiled=True)]
    all_to_all x1, waiting for transfers between devices: 5.08 us -> 0.01 us  [body(): lax.all_to_all(ffn_rows.reshape(nb, own, 4 * part), 'blk', 0, 0, tiled=True)]
    unnamed x106 -> x94, local copies, waits for them, and re-layouts: 12.9 us -> 9.02 us
  transfers between devices with their start and end apart: 62 -> 62, of which waited for: 28 -> 28; matrix products, arithmetic and copies ran while one was open for 2% -> 2% of each run, Pallas kernels for 27% -> 28%
where the time goes in v2:
time: 323 us; the launch traced here: 319 us
  waiting for transfers between devices  123 us (38%)
  Pallas kernels  92.3 us (29%)
  starting transfers between devices  71.5 us (22%)
  between operations  14.8 us (5%)
  local copies, waits for them, and re-layouts  10.6 us (3%)
  other arithmetic  6.82 us (2%)
    pallas_call x25, Pallas kernels, run(): pl.pallas_call(whole, out_shape=[jax.ShapeDtypeStruct(shape, kind) for sh...  92.3 us
    ppermute x20, waiting for transfers between devices, hop(): lax.ppermute(array, 'blk', [(i, i ^ hop_bit(j, i % 2)) for i in range(lax...  72.5 us
    ppermute x33, waiting for transfers between devices, swap(): lax.ppermute(array, axis, [(i, i ^ bit) for i in range(lax.axis_size(axis...  39.9 us
    ppermute x20, starting transfers between devices, hop(): lax.ppermute(array, 'blk', [(i, i ^ hop_bit(j, i % 2)) for i in range(lax...  31.6 us
    ppermute x33, starting transfers between devices, swap(): lax.ppermute(array, axis, [(i, i ^ bit) for i in range(lax.axis_size(axis...  14.1 us
    unnamed x94, local copies, waits for them, and re-layouts  9.02 us
    all_to_all x1, waiting for transfers between devices, body(): lax.all_to_all(after(made['both'], branch).reshape(nd, plane, 2 * part),...  6.47 us
  transfers between devices with their start and end apart: 62, of which 28 were waited for; matrix products, arithmetic and copies ran while one was open for 2% of the time, Pallas kernels for 28%

profile of v2, /device:TPU:0, one launch (start us, length us, event | category | flops | bytes accessed | tf_op | source)
XLA Modules:
  0.0 319.3 jit_solution(11981931538876128815)
XLA Ops:
  11.3 5.2 %all-to-all-start = ((bf16[8,48,640]{2,1,0:T(8,128)(2,1)}), bf16[8,48,640]{2,1,0:T(8,128)(2,1)S(1)}, u32[]{:S(2)}, u32[]{:S(2)}) async-start(bf16[8,48,640]{2,1,0:T(8,128)(2,1)} %shard_map.221), calls=%async_computation | async-start | bytes 983040 | tf_op jit(solution)/shard_map/all_to_all | solution.py:843
  18.1 2.6 collective-permute-start.8
  22.1 2.0 collective-permute-start
  25.5 6.6 %collective-permute-done.8 = bf16[48,1536]{1,0:T(8,128)(2,1)S(1)} collective-permute-done((bf16[48,1536]{1,0:T(8,128)(2,1)S(1)}, bf16[48,1536]{1,0:T(8,128)(2,1)S(1)}, u32[]{:S(2)}, u32[]{:S(2)}) %collective-permute-start.8) | collective-permute-done | bytes 147488 | tf_op jit(solution)/shard_map/ppermute | solution.py:38
  33.0 2.0 collective-permute-start.1
  35.0 3.4 %collective-permute-done.refs_3_.refs_2_ = bf16[320,1536]{1,0:T(8,128)(2,1)} collective-permute-done((bf16[320,1536]{1,0:T(8,128)(2,1)S(1)}, bf16[320,1536]{1,0:T(8,128)(2,1)}, u32[]{:S(2)}, u32[]{:S(2)}) %collective-permute-start) | collective-permute-done | bytes 983072 | tf_op jit(solution)/shard_map/ppermute | solution.py:32
  38.4 2.6 collective-permute-start.2
  41.0 2.6 shard_map.227
  43.6 3.7 %all-to-all-start.1 = ((bf16[8,48,1536]{2,1,0:T(8,128)(2,1)}), bf16[8,48,1536]{2,1,0:T(8,128)(2,1)S(1)}, u32[]{:S(2)}, u32[]{:S(2)}) async-start(bf16[8,48,1536]{2,1,0:T(8,128)(2,1)} %shard_map.227), calls=%async_computation.1 | async-start | bytes 2359296 | tf_op jit(solution)/shard_map/all_to_all | solution.py:858
  48.3 15.3 %collective-permute-done.2.refs_5_.refs_4_ = bf16[320,1536]{1,0:T(8,128)(2,1)} collective-permute-done((bf16[320,1536]{1,0:T(8,128)(2,1)}, bf16[320,1536]{1,0:T(8,128)(2,1)}, u32[]{:S(2)}, u32[]{:S(2)}) %collective-permute-start.2) | collective-permute-done | bytes 983072 | tf_op jit(solution)/shard_map/ppermute | solution.py:32
  65.6 3.2 collective-permute-done.10
  68.8 2.7 all-to-all-done.1
  75.6 5.4 %all-to-all-start.2 = ((bf16[4,384,768]{2,1,0:T(8,128)(2,1)}), bf16[4,384,768]{2,1,0:T(8,128)(2,1)S(1)}, u32[]{:S(2)}, u32[]{:S(2)}) async-start(bf16[4,384,768]{2,1,0:T(8,128)(2,1)} %pad_maximum_fusion), calls=%async_computation.2 | async-start | bytes 4718592 | tf_op jit(solution)/shard_map/all_to_all | solution.py:863
  81.4 12.4 %shard_map.223 = (bf16[8,8,32,384]{3,2,1,0:T(8,128)(2,1)}, f32[8,8,8,640]{3,2,1,0:T(8,128)}, f32[8,8,8,256]{3,2,1,0:T(8,128)}, f32[8,128,128]{2,1,0:T(8,128)}, b...) custom-call(s32[10]{0:T(128)} %pad_add_fusion.refs_0_, s32[8]{0:T(128)} %refs_1_.9, bf16[320,1536]{1,0:T(8,128)(2,1)} %copy-done.1, ...), custom_call_target="tpu_custom_call" | custom-call | flops 12650000384 | bytes 39600000 | tf_op jit(solution)/shard_map/pallas_call | solution.py:122
  96.5 3.8 %shard_map.224 = (bf16[2,64,1536]{2,1,0:T(8,128)(2,1)S(1)}, bf16[2,64,1536]{2,1,0:T(8,128)(2,1)S(1)}) custom-call(s32[10]{0:T(128)S(1)} %copy-done.10, bf16[8,64,256]{2,1,0:T(8,128)(2,1)S(1)} %copy-done.5, bf16[4,64,256]{2,1,0:T(8,128)(2,1)S(1)} %collective-permute-done.13.refs_2_, bf16[4,48,1536]{2,1,0:T(8,128)(2,1)S(1)} %pad_maximum_fusion.1.refs_3_.refs_10_, ...), custom_call_target="tpu_custom_call" | custom-call | flops 3449999872 | bytes 10800000 | tf_op jit(solution)/shard_map/pallas_call | solution.py:122
  102.0 6.1 %collective-permute-done.15.refs_1_ = bf16[2,64,1536]{2,1,0:T(8,128)(2,1)S(1)} collective-permute-done((bf16[2,64,1536]{2,1,0:T(8,128)(2,1)S(1)}, bf16[2,64,1536]{2,1,0:T(8,128)(2,1)S(1)}, u32[]{:S(2)}, u32[]{:S(2)}) %collective-permute-start.15) | collective-permute-done | bytes 393248 | tf_op jit(solution)/shard_map/ppermute | solution.py:32
  111.7 3.9 %collective-permute-done.17 = bf16[1,64,1536]{2,1,0:T(8,128)(2,1)S(1)} collective-permute-done((bf16[1,64,1536]{2,1,0:T(8,128)(2,1)S(1)}, bf16[1,64,1536]{2,1,0:T(8,128)(2,1)S(1)}, u32[]{:S(2)}, u32[]{:S(2)}) %collective-permute-start.17) | collective-permute-done | bytes 196640 | tf_op jit(solution)/shard_map/ppermute | solution.py:32
  120.0 3.9 %collective-permute-done.18 = bf16[32,1536]{1,0:T(8,128)(2,1)S(1)} collective-permute-done((bf16[32,1536]{1,0:T(8,128)(2,1)S(1)}, bf16[32,1536]{1,0:T(8,128)(2,1)S(1)}, u32[]{:S(2)}, u32[]{:S(2)}) %collective-permute-start.18) | collective-permute-done | bytes 98336 | tf_op jit(solution)/shard_map/ppermute | solution.py:38
  123.9 11.3 %collective-permute-done.19 = bf16[32,1536]{1,0:T(8,128)(2,1)S(1)} collective-permute-done((bf16[32,1536]{1,0:T(8,128)(2,1)S(1)}, bf16[32,1536]{1,0:T(8,128)(2,1)S(1)}, u32[]{:S(2)}, u32[]{:S(2)}) %collective-permute-start.19) | collective-permute-done | bytes 98336 | tf_op jit(solution)/shard_map/ppermute | solution.py:38
  136.7 6.4 %collective-permute-done.20.refs_1_ = bf16[128,1536]{1,0:T(8,128)(2,1)} collective-permute-done((bf16[128,1536]{1,0:T(8,128)(2,1)S(1)}, bf16[128,1536]{1,0:T(8,128)(2,1)}, u32[]{:S(2)}, u32[]{:S(2)}) %collective-permute-start.20) | collective-permute-done | bytes 393248 | tf_op jit(solution)/shard_map/ppermute | solution.py:32
  145.6 5.2 %collective-permute-done.21.refs_2_ = bf16[128,1536]{1,0:T(8,128)(2,1)S(1)} collective-permute-done((bf16[128,1536]{1,0:T(8,128)(2,1)S(1)}, bf16[128,1536]{1,0:T(8,128)(2,1)S(1)}, u32[]{:S(2)}, u32[]{:S(2)}) %collective-permute-start.21) | collective-permute-done | bytes 393248 | tf_op jit(solution)/shard_map/ppermute | solution.py:32
  150.9 4.2 %collective-permute-done.22.refs_3_ = bf16[128,1536]{1,0:T(8,128)(2,1)S(1)} collective-permute-done((bf16[128,1536]{1,0:T(8,128)(2,1)}, bf16[128,1536]{1,0:T(8,128)(2,1)S(1)}, u32[]{:S(2)}, u32[]{:S(2)}) %collective-permute-start.22) | collective-permute-done | bytes 393248 | tf_op jit(solution)/shard_map/ppermute | solution.py:32
  155.6 7.2 %shard_map.228 = (bf16[512,384]{1,0:T(8,128)(2,1)S(1)}, bf16[512,384]{1,0:T(8,128)(2,1)S(1)}, bf16[512,384]{1,0:T(8,128)(2,1)S(1)}, bf16[512,384]{1,0:T(8,128)(2...) custom-call(bf16[128,1536]{1,0:T(8,128)(2,1)S(1)} %constant_dynamic-update-slice_fusion.refs_0_, ...), custom_call_target="tpu_custom_call" | custom-call | flops 1150000000 | bytes 3600000 | tf_op jit(solution)/shard_map/pallas_call | solution.py:122
  165.4 3.9 %shard_map.229.refs_10_ = bf16[1536,384]{1,0:T(8,128)(2,1)S(1)} custom-call(bf16[128,1536]{1,0:T(8,128)(2,1)S(1)} %pad_maximum_fusion.3.refs_4_.refs_0_, bf16[128,1536]{1,0:T(8,128)(2,1)} %collective-permute-done.11.refs_5_.refs_1_, bf16[128,1536]{1,0:T(8,128)(2,1)} %collective-permute-done.12.refs_6_.refs_2_, bf16[128,1536]{1,0:T(8,128)(2,1)S(1)} %copy-done.4, ...), custom_call_target="tpu_custom_call" | custom-call | flops 4600000000 | bytes 14400000 | tf_op jit(solution)/shard_map/pallas_call | solution.py:122
  169.3 5.3 %shard_map.230 = bf16[1536,768]{1,0:T(8,128)(2,1)} custom-call(bf16[128,1536]{1,0:T(8,128)(2,1)S(1)} %constant_dynamic-update-slice_fusion.refs_0_, bf16[128,1536]{1,0:T(8,128)(2,1)} %collective-permute-done.20.refs_1_, bf16[128,1536]{1,0:T(8,128)(2,1)S(1)} %collective-permute-done.21.refs_2_, bf16[128,1536]{1,0:T(8,128)(2,1)S(1)} %collective-permute-done.22.refs_3_, ...), custom_call_target="tpu_custom_call" | custom-call | flops 4600000000 | bytes 14400000 | tf_op jit(solution)/shard_map/pallas_call | solution.py:122
  178.9 2.0 shard_map.232
  182.1 5.8 %collective-permute-done.38 = bf16[1,128,1536]{2,1,0:T(8,128)(2,1)S(1)} collective-permute-done((bf16[1,128,1536]{2,1,0:T(8,128)(2,1)S(1)}, bf16[1,128,1536]{2,1,0:T(8,128)(2,1)S(1)}, u32[]{:S(2)}, u32[]{:S(2)}) %collective-permute-start.38) | collective-permute-done | bytes 393248 | tf_op jit(solution)/shard_map/ppermute | solution.py:32
  188.8 5.7 %collective-permute-done.39.refs_2_ = bf16[64,1536]{1,0:T(8,128)(2,1)S(1)} collective-permute-done((bf16[64,1536]{1,0:T(8,128)(2,1)S(1)}, bf16[64,1536]{1,0:T(8,128)(2,1)S(1)}, u32[]{:S(2)}, u32[]{:S(2)}) %collective-permute-start.39) | collective-permute-done | bytes 196640 | tf_op jit(solution)/shard_map/ppermute | solution.py:38
  194.5 2.1 shard_map.237
  199.2 3.8 %all-to-all-start.3 = ((bf16[4,384,768]{2,1,0:T(8,128)(2,1)}), bf16[4,384,768]{2,1,0:T(8,128)(2,1)S(1)}, u32[]{:S(2)}, u32[]{:S(2)}) async-start(bf16[4,384,768]{2,1,0:T(8,128)(2,1)} %bitcast.25), calls=%async_computation.3 | async-start | bytes 4718592 | tf_op jit(solution)/shard_map/all_to_all | solution.py:1011
  204.2 2.0 shard_map.233
  210.4 3.1 collective-permute-done.41.refs_4_.refs_11_
  213.5 2.1 collective-permute-done.42.refs_5_.refs_12_
  218.1 9.2 %shard_map.238 = (bf16[8,8,32,384]{3,2,1,0:T(8,128)(2,1)}, bf16[512,640]{1,0:T(8,128)(2,1)}, bf16[4,8,32,384]{3,2,1,0:T(8,128)(2,1)}, bf16[4,64,640]{2,1,0:T(8,128)(2,1)}) custom-call(s32[10]{0:T(128)} %pad_add_fusion.refs_0_, s32[8]{0:T(128)} %refs_1_.9, bf16[64,1536]{1,0:T(8,128)(2,1)} %copy-done.2, ...), custom_call_target="tpu_custom_call" | custom-call | flops 1150000000 | bytes 3600000 | tf_op jit(solution)/shard_map/pallas_call | solution.py:122
  227.3 11.6 %shard_map.239 = (bf16[1536,640]{1,0:T(8,128)(2,1)}, bf16[2,48,1536]{2,1,0:T(8,128)(2,1)}, bf16[1,2,48,1536]{3,2,1,0:T(8,128)(2,1)}) custom-call(s32[10]{0:T(128)} %pad_add_fusion.refs_0_, bf16[320,1536]{1,0:T(8,128)(2,1)} %copy-done.1, bf16[320,1536]{1,0:T(8,128)(2,1)} %collective-permute-done.refs_3_.refs_2_, ...), custom_call_target="tpu_custom_call" | custom-call | flops 1150000000 | bytes 3600000 | tf_op jit(solution)/shard_map/pallas_call | solution.py:122
  239.4 2.5 collective-permute-done.48
  242.9 7.8 %shard_map.240 = (bf16[2,320,1536]{2,1,0:T(8,128)(2,1)}, bf16[2,320,1536]{2,1,0:T(8,128)(2,1)}) custom-call(bf16[8,8,32,384]{3,2,1,0:T(8,128)(2,1)} %get-tuple-element.118.refs_17_.refs_0_, bf16[512,640]{1,0:T(8,128)(2,1)} %get-tuple-element.116.refs_18_.refs_1_, bf16[4,8,32,384]{3,2,1,0:T(8,128)(2,1)} %copy-done.31, bf16[256,640]{1,0:T(8,128)(2,1)} %bitcast.69, ...), custom_call_target="tpu_custom_call" | custom-call | flops 1150000000 | bytes 3600000 | tf_op jit(solution)/shard_map/pallas_call | solution.py:122
  252.5 2.0 collective-permute-start.37
  254.4 6.5 %all-to-all-done.3.refs_0_ = bf16[4,384,768]{2,1,0:T(8,128)(2,1)S(1)} async-done(((bf16[4,384,768]{2,1,0:T(8,128)(2,1)}), bf16[4,384,768]{2,1,0:T(8,128)(2,1)S(1)}, u32[]{:S(2)}, u32[]{:S(2)}) %all-to-all-start.3) | async-done | bytes 2359328 | tf_op jit(solution)/shard_map/all_to_all | solution.py:1011
  262.4 3.7 %all-to-all-start.4 = ((bf16[8,48,1536]{2,1,0:T(8,128)(2,1)}), bf16[8,48,1536]{2,1,0:T(8,128)(2,1)S(1)}, u32[]{:S(2)}, u32[]{:S(2)}) async-start(bf16[8,48,1536]{2,1,0:T(8,128)(2,1)} %bitcast.27), calls=%async_computation.4 | async-start | bytes 2359296 | tf_op jit(solution)/shard_map/all_to_all | solution.py:1016
  266.5 4.4 %collective-permute-done.37.refs_2_ = bf16[64,1536]{1,0:T(8,128)(2,1)S(1)} collective-permute-done((bf16[64,1536]{1,0:T(8,128)(2,1)S(1)}, bf16[64,1536]{1,0:T(8,128)(2,1)S(1)}, u32[]{:S(2)}, u32[]{:S(2)}) %collective-permute-start.37) | collective-permute-done | bytes 196640 | tf_op jit(solution)/shard_map/ppermute | solution.py:38
  272.9 7.6 %collective-permute-done.50.refs_1_ = bf16[2,320,1536]{2,1,0:T(8,128)(2,1)} collective-permute-done((bf16[2,320,1536]{2,1,0:T(8,128)(2,1)}, bf16[2,320,1536]{2,1,0:T(8,128)(2,1)}, u32[]{:S(2)}, u32[]{:S(2)}) %collective-permute-start.50) | collective-permute-done | bytes 1966112 | tf_op jit(solution)/shard_map/ppermute | solution.py:32
  280.5 2.7 shard_map.242
  284.2 3.5 %collective-permute-start.51 = (bf16[1,320,1536]{2,1,0:T(8,128)(2,1)}, bf16[1,320,1536]{2,1,0:T(8,128)(2,1)S(1)}, u32[]{:S(2)}, u32[]{:S(2)}) collective-permute-start(bf16[1,320,1536]{2,1,0:T(8,128)(2,1)} %get-tuple-element.126), channel_id=1, source_target_pairs={{0,2},{1,5},{2,0},{3,7},{4,6},{5,1},{6,4},{7,3},{8,10},{9,13},{10,... | collective-permute-start | bytes 2949128 | tf_op jit(solution)/shard_map/ppermute | solution.py:32
  288.6 3.9 %all-to-all-start.5 = ((bf16[8,48,640]{2,1,0:T(8,128)(2,1)}), bf16[8,48,640]{2,1,0:T(8,128)(2,1)S(1)}, u32[]{:S(2)}, u32[]{:S(2)}) async-start(bf16[8,48,640]{2,1,0:T(8,128)(2,1)} %bitcast.68), calls=%async_computation.6 | async-start | bytes 983040 | tf_op jit(solution)/shard_map/all_to_all | solution.py:1118
  292.6 2.3 shard_map.243
  294.8 7.8 %collective-permute-done.51 = bf16[1,320,1536]{2,1,0:T(8,128)(2,1)S(1)} collective-permute-done((bf16[1,320,1536]{2,1,0:T(8,128)(2,1)}, bf16[1,320,1536]{2,1,0:T(8,128)(2,1)S(1)}, u32[]{:S(2)}, u32[]{:S(2)}) %collective-permute-start.51) | collective-permute-done | bytes 983072 | tf_op jit(solution)/shard_map/ppermute | solution.py:32
  303.3 3.7 %shard_map.244 = (f32[256,1536]{1,0:T(8,128)}, f32[64,1536]{1,0:T(8,128)}) custom-call(bf16[320,1536]{1,0:T(8,128)(2,1)S(1)} %bitcast.59, bf16[320,1536]{1,0:T(8,128)(2,1)S(1)} %bitcast.48, bf16[256,1536]{1,0:T(8,128)(2,1)S(1)} %bitcast.50, bf16[64,1536]{1,0:T(8,128)(2,1)S(1)} %bitcast.57, f32[64,1536]{1,0:T(8,128)S(1)} %copy-done.29), custom_call_target="tpu_custom_call" | custom-call | flops 5750000128 | bytes 18000000 | tf_op jit(solution)/shard_map/pallas_call | solution.py:122
  (214 shorter events, 68.1 us)
Async XLA Ops:
  11.3 20.8 %all-to-all-start = ((bf16[8,48,640]{2,1,0:T(8,128)(2,1)}), bf16[8,48,640]{2,1,0:T(8,128)(2,1)S(1)}, u32[]{:S(2)}, u32[]{:S(2)}) async-start(bf16[8,48,640]{2,1,0:T(8,128)(2,1)} %shard_map.221), calls=%async_computation | async-start | bytes 983040 | tf_op jit(solution)/shard_map/all_to_all | solution.py:843
  16.4 65.0 %all-gather.2.cloned.1.call-start = ((), (), s32[]{:S(2)}) async-start(), calls=%async_computation.8 | async-start | bytes 2457600 | tf_op jit(solution)/shard_map/all_gather | solution.py:844
  16.5 9.0 %collective-permute-start.7 = (bf16[48,1536]{1,0:T(8,128)(2,1)S(1)}, bf16[48,1536]{1,0:T(8,128)(2,1)S(1)}, u32[]{:S(2)}, u32[]{:S(2)}) collective-permute-start(bf16[48,1536]{1,0:T(8,128)(2,1)S(1)} %copy-done.40), channel_id=1, source_target_pairs={{0,8},{8,0},{16,24},{24,16},{1,9},{9,1},{17,25},{25,17},{2,10},{10... | collective-permute-start | bytes 442376 | tf_op jit(solution)/shard_map/ppermute | solution.py:38
  18.1 14.0 %collective-permute-start.8 = (bf16[48,1536]{1,0:T(8,128)(2,1)S(1)}, bf16[48,1536]{1,0:T(8,128)(2,1)S(1)}, u32[]{:S(2)}, u32[]{:S(2)}) collective-permute-start(bf16[48,1536]{1,0:T(8,128)(2,1)S(1)} %copy-done.40), channel_id=1, source_target_pairs={{0,16},{8,24},{16,0},{24,8},{1,17},{9,25},{17,1},{25,9},{2,18},{10... | collective-permute-start | bytes 442376 | tf_op jit(solution)/shard_map/ppermute | solution.py:38
  20.7 11.4 %collective-permute-start.9 = (bf16[48,1536]{1,0:T(8,128)(2,1)S(1)}, bf16[48,1536]{1,0:T(8,128)(2,1)S(1)}, u32[]{:S(2)}, u32[]{:S(2)}) collective-permute-start(bf16[48,1536]{1,0:T(8,128)(2,1)S(1)} %copy-done.40), channel_id=1, source_target_pairs={{0,24},{8,16},{16,8},{24,0},{1,25},{9,17},{17,9},{25,1},{2,26},{10... | collective-permute-start | bytes 442376 | tf_op jit(solution)/shard_map/ppermute | solution.py:38
  22.1 16.2 %collective-permute-start = (bf16[320,1536]{1,0:T(8,128)(2,1)S(1)}, bf16[320,1536]{1,0:T(8,128)(2,1)}, u32[]{:S(2)}, u32[]{:S(2)}) collective-permute-start(bf16[320,1536]{1,0:T(8,128)(2,1)S(1)} %shard_map.222.refs_2_.refs_1_), channel_id=1, source_target_pairs={{0,2},{1,5},{2,0},{3,7},{4,6},{5,1},{6,4},{7,3},{8,10},{9,13},{10,... | collective-permute-start | bytes 2949128 | tf_op jit(solution)/shard_map/ppermute | solution.py:32
  33.0 15.0 %collective-permute-start.1 = (bf16[320,1536]{1,0:T(8,128)(2,1)S(1)}, bf16[320,1536]{1,0:T(8,128)(2,1)}, u32[]{:S(2)}, u32[]{:S(2)}) collective-permute-start(bf16[320,1536]{1,0:T(8,128)(2,1)S(1)} %shard_map.222.refs_2_.refs_1_), channel_id=1, source_target_pairs={{0,4},{1,3},{2,6},{3,1},{4,0},{5,7},{6,2},{7,5},{8,12},{9,11},{10,... | collective-permute-start | bytes 2949128 | tf_op jit(solution)/shard_map/ppermute | solution.py:32
  38.4 25.2 %collective-permute-start.2 = (bf16[320,1536]{1,0:T(8,128)(2,1)}, bf16[320,1536]{1,0:T(8,128)(2,1)}, u32[]{:S(2)}, u32[]{:S(2)}) collective-permute-start(bf16[320,1536]{1,0:T(8,128)(2,1)} %collective-permute-done.refs_3_.refs_2_), channel_id=1, source_target_pairs={{0,4},{1,3},{2,6},{3,1},{4,0},{5,7},{6,2},{7,5},{8,12},{9,11},{10,... | collective-permute-start | bytes 2949128 | tf_op jit(solution)/shard_map/ppermute | solution.py:32
  43.6 27.9 %all-to-all-start.1 = ((bf16[8,48,1536]{2,1,0:T(8,128)(2,1)}), bf16[8,48,1536]{2,1,0:T(8,128)(2,1)S(1)}, u32[]{:S(2)}, u32[]{:S(2)}) async-start(bf16[8,48,1536]{2,1,0:T(8,128)(2,1)} %shard_map.227), calls=%async_computation.1 | async-start | bytes 2359296 | tf_op jit(solution)/shard_map/all_to_all | solution.py:858
  47.3 25.9 %collective-permute-start.3 = (bf16[320,1536]{1,0:T(8,128)(2,1)S(1)}, bf16[320,1536]{1,0:T(8,128)(2,1)}, u32[]{:S(2)}, u32[]{:S(2)}) collective-permute-start(bf16[320,1536]{1,0:T(8,128)(2,1)S(1)} %shard_map.222.refs_2_.refs_1_), channel_id=1, source_target_pairs={{0,1},{1,0},{2,3},{3,2},{4,5},{5,4},{6,7},{7,6},{8,9},{9,8},{10,11... | collective-permute-start | bytes 2949128 | tf_op jit(solution)/shard_map/ppermute | solution.py:38
  47.7 21.0 %collective-permute-start.10 = (bf16[64,1536]{1,0:T(8,128)(2,1)S(1)}, bf16[64,1536]{1,0:T(8,128)(2,1)S(1)}, u32[]{:S(2)}, u32[]{:S(2)}) collective-permute-start(bf16[64,1536]{1,0:T(8,128)(2,1)S(1)} %bitcast.45), channel_id=1, source_target_pairs={{0,8},{8,0},{16,24},{24,16},{1,9},{9,1},{17,25},{25,17},{2,10},{10... | collective-permute-start | bytes 589832 | tf_op jit(solution)/shard_map/ppermute | solution.py:38
  47.7 25.5 %collective-permute-start.4 = (bf16[320,1536]{1,0:T(8,128)(2,1)}, bf16[320,1536]{1,0:T(8,128)(2,1)}, u32[]{:S(2)}, u32[]{:S(2)}) collective-permute-start(bf16[320,1536]{1,0:T(8,128)(2,1)} %collective-permute-done.refs_3_.refs_2_), channel_id=1, source_target_pairs={{0,1},{1,0},{2,3},{3,2},{4,5},{5,4},{6,7},{7,6},{8,9},{9,8},{10,11... | collective-permute-start | bytes 2949128 | tf_op jit(solution)/shard_map/ppermute | solution.py:38
  48.0 25.3 %collective-permute-start.5 = (bf16[320,1536]{1,0:T(8,128)(2,1)}, bf16[320,1536]{1,0:T(8,128)(2,1)}, u32[]{:S(2)}, u32[]{:S(2)}) collective-permute-start(bf16[320,1536]{1,0:T(8,128)(2,1)} %collective-permute-done.1.refs_4_.refs_3_), channel_id=1, source_target_pairs={{0,1},{1,0},{2,3},{3,2},{4,5},{5,4},{6,7},{7,6},{8,9},{9,8},{10,11... | collective-permute-start | bytes 2949128 | tf_op jit(solution)/shard_map/ppermute | solution.py:38
  63.6 9.7 %collective-permute-start.6 = (bf16[320,1536]{1,0:T(8,128)(2,1)}, bf16[320,1536]{1,0:T(8,128)(2,1)}, u32[]{:S(2)}, u32[]{:S(2)}) collective-permute-start(bf16[320,1536]{1,0:T(8,128)(2,1)} %collective-permute-done.2.refs_5_.refs_4_), channel_id=1, source_target_pairs={{0,1},{1,0},{2,3},{3,2},{4,5},{5,4},{6,7},{7,6},{8,9},{9,8},{10,11... | collective-permute-start | bytes 2949128 | tf_op jit(solution)/shard_map/ppermute | solution.py:38
  68.7 26.8 %collective-permute-start.14 = (bf16[4,48,1536]{2,1,0:T(8,128)(2,1)S(1)}, bf16[4,48,1536]{2,1,0:T(8,128)(2,1)}, u32[]{:S(2)}, u32[]{:S(2)}) collective-permute-start(bf16[4,48,1536]{2,1,0:T(8,128)(2,1)S(1)} %pad_maximum_fusion.1.refs_3_.refs_10_), channel_id=1, source_target_pairs={{0,1},{1,0},{2,3},{3,2},{4,5},{5,4},{6,7},{7,6},{8,9},{9,8},{10,11... | collective-permute-start | bytes 1769480 | tf_op jit(solution)/shard_map/ppermute | solution.py:38
  73.3 20.6 %collective-permute-start.11 = (bf16[128,1536]{1,0:T(8,128)(2,1)S(1)}, bf16[128,1536]{1,0:T(8,128)(2,1)}, u32[]{:S(2)}, u32[]{:S(2)}) collective-permute-start(bf16[128,1536]{1,0:T(8,128)(2,1)S(1)} %pad_maximum_fusion.3.refs_4_.refs_0_), channel_id=1, source_target_pairs={{0,2},{1,5},{2,0},{3,7},{4,6},{5,1},{6,4},{7,3},{8,10},{9,13},{10,... | collective-permute-start | bytes 1179656 | tf_op jit(solution)/shard_map/ppermute | solution.py:32
  74.1 19.8 %collective-permute-start.12 = (bf16[128,1536]{1,0:T(8,128)(2,1)S(1)}, bf16[128,1536]{1,0:T(8,128)(2,1)}, u32[]{:S(2)}, u32[]{:S(2)}) collective-permute-start(bf16[128,1536]{1,0:T(8,128)(2,1)S(1)} %pad_maximum_fusion.3.refs_4_.refs_0_), channel_id=1, source_target_pairs={{0,4},{1,3},{2,6},{3,1},{4,0},{5,7},{6,2},{7,5},{8,12},{9,11},{10,... | collective-permute-start | bytes 1179656 | tf_op jit(solution)/shard_map/ppermute | solution.py:32
  75.6 67.5 %all-to-all-start.2 = ((bf16[4,384,768]{2,1,0:T(8,128)(2,1)}), bf16[4,384,768]{2,1,0:T(8,128)(2,1)S(1)}, u32[]{:S(2)}, u32[]{:S(2)}) async-start(bf16[4,384,768]{2,1,0:T(8,128)(2,1)} %pad_maximum_fusion), calls=%async_computation.2 | async-start | bytes 4718592 | tf_op jit(solution)/shard_map/all_to_all | solution.py:863
  94.0 8.1 %collective-permute-start.16 = (bf16[128,1536]{1,0:T(8,128)(2,1)}, bf16[128,1536]{1,0:T(8,128)(2,1)S(1)}, u32[]{:S(2)}, u32[]{:S(2)}) collective-permute-start(bf16[128,1536]{1,0:T(8,128)(2,1)} %collective-permute-done.11.refs_5_.refs_1_), channel_id=1, source_target_pairs={{0,4},{1,3},{2,6},{3,1},{4,0},{5,7},{6,2},{7,5},{8,12},{9,11},{10,... | collective-permute-start | bytes 1179656 | tf_op jit(solution)/shard_map/ppermute | solution.py:32
  100.3 7.8 %collective-permute-start.15 = (bf16[2,64,1536]{2,1,0:T(8,128)(2,1)S(1)}, bf16[2,64,1536]{2,1,0:T(8,128)(2,1)S(1)}, u32[]{:S(2)}, u32[]{:S(2)}) collective-permute-start(bf16[2,64,1536]{2,1,0:T(8,128)(2,1)S(1)} %get-tuple-element.83), channel_id=1, source_target_pairs={{0,4},{1,3},{2,6},{3,1},{4,0},{5,7},{6,2},{7,5},{8,12},{9,11},{10,... | collective-permute-start | bytes 1179656 | tf_op jit(solution)/shard_map/ppermute | solution.py:32
  119.6 15.6 %collective-permute-start.19 = (bf16[32,1536]{1,0:T(8,128)(2,1)S(1)}, bf16[32,1536]{1,0:T(8,128)(2,1)S(1)}, u32[]{:S(2)}, u32[]{:S(2)}) collective-permute-start(bf16[32,1536]{1,0:T(8,128)(2,1)S(1)} %get-tuple-element.147), channel_id=1, source_target_pairs={{0,8},{8,0},{16,24},{24,16},{1,9},{9,1},{17,25},{25,17},{2,10},{10... | collective-permute-start | bytes 294920 | tf_op jit(solution)/shard_map/ppermute | solution.py:38
  135.2 7.9 %collective-permute-start.20 = (bf16[128,1536]{1,0:T(8,128)(2,1)S(1)}, bf16[128,1536]{1,0:T(8,128)(2,1)}, u32[]{:S(2)}, u32[]{:S(2)}) collective-permute-start(bf16[128,1536]{1,0:T(8,128)(2,1)S(1)} %constant_dynamic-update-slice_fusion.refs_0_), channel_id=1, source_target_pairs={{0,2},{1,5},{2,0},{3,7},{4,6},{5,1},{6,4},{7,3},{8,10},{9,13},{10,... | collective-permute-start | bytes 1179656 | tf_op jit(solution)/shard_map/ppermute | solution.py:32
  143.1 12.0 %collective-permute-start.23 = (bf16[1536,768]{1,0:T(8,128)(2,1)S(1)}, bf16[1536,768]{1,0:T(8,128)(2,1)S(1)}, u32[]{:S(2)}, u32[]{:S(2)}) collective-permute-start(bf16[1536,768]{1,0:T(8,128)(2,1)S(1)} %bitcast.42), channel_id=1, source_target_pairs={{0,1},{1,0},{2,3},{3,2},{4,5},{5,4},{6,7},{7,6},{8,9},{9,8},{10,11... | collective-permute-start | bytes 7077896 | tf_op jit(solution)/shard_map/ppermute | solution.py:38
  143.1 7.8 %collective-permute-start.21 = (bf16[128,1536]{1,0:T(8,128)(2,1)S(1)}, bf16[128,1536]{1,0:T(8,128)(2,1)S(1)}, u32[]{:S(2)}, u32[]{:S(2)}) collective-permute-start(bf16[128,1536]{1,0:T(8,128)(2,1)S(1)} %constant_dynamic-update-slice_fusion.refs_0_), channel_id=1, source_target_pairs={{0,4},{1,3},{2,6},{3,1},{4,0},{5,7},{6,2},{7,5},{8,12},{9,11},{10,... | collective-permute-start | bytes 1179656 | tf_op jit(solution)/shard_map/ppermute | solution.py:32
  144.6 10.5 %collective-permute-start.22 = (bf16[128,1536]{1,0:T(8,128)(2,1)}, bf16[128,1536]{1,0:T(8,128)(2,1)S(1)}, u32[]{:S(2)}, u32[]{:S(2)}) collective-permute-start(bf16[128,1536]{1,0:T(8,128)(2,1)} %collective-permute-done.20.refs_1_), channel_id=1, source_target_pairs={{0,4},{1,3},{2,6},{3,1},{4,0},{5,7},{6,2},{7,5},{8,12},{9,11},{10,... | collective-permute-start | bytes 1179656 | tf_op jit(solution)/shard_map/ppermute | solution.py:32
  145.1 17.7 %collective-permute-start.30 = (bf16[128,1536]{1,0:T(8,128)(2,1)S(1)}, bf16[128,1536]{1,0:T(8,128)(2,1)S(1)}, u32[]{:S(2)}, u32[]{:S(2)}) collective-permute-start(bf16[128,1536]{1,0:T(8,128)(2,1)S(1)} %pad_maximum_fusion.3.refs_4_.refs_0_), channel_id=1, source_target_pairs={{0,1},{1,0},{2,3},{3,2},{4,5},{5,4},{6,7},{7,6},{8,9},{9,8},{10,11... | collective-permute-start | bytes 1179656 | tf_op jit(solution)/shard_map/ppermute | solution.py:38
  145.1 17.9 %collective-permute-start.31 = (bf16[128,1536]{1,0:T(8,128)(2,1)}, bf16[128,1536]{1,0:T(8,128)(2,1)S(1)}, u32[]{:S(2)}, u32[]{:S(2)}) collective-permute-start(bf16[128,1536]{1,0:T(8,128)(2,1)} %collective-permute-done.11.refs_5_.refs_1_), channel_id=1, source_target_pairs={{0,1},{1,0},{2,3},{3,2},{4,5},{5,4},{6,7},{7,6},{8,9},{9,8},{10,11... | collective-permute-start | bytes 1179656 | tf_op jit(solution)/shard_map/ppermute | solution.py:38
  150.9 12.6 %collective-permute-start.32 = (bf16[128,1536]{1,0:T(8,128)(2,1)}, bf16[128,1536]{1,0:T(8,128)(2,1)S(1)}, u32[]{:S(2)}, u32[]{:S(2)}) collective-permute-start(bf16[128,1536]{1,0:T(8,128)(2,1)} %collective-permute-done.12.refs_6_.refs_2_), channel_id=1, source_target_pairs={{0,1},{1,0},{2,3},{3,2},{4,5},{5,4},{6,7},{7,6},{8,9},{9,8},{10,11... | collective-permute-start | bytes 1179656 | tf_op jit(solution)/shard_map/ppermute | solution.py:38
  155.1 8.4 %collective-permute-start.33 = (bf16[128,1536]{1,0:T(8,128)(2,1)S(1)}, bf16[128,1536]{1,0:T(8,128)(2,1)S(1)}, u32[]{:S(2)}, u32[]{:S(2)}) collective-permute-start(bf16[128,1536]{1,0:T(8,128)(2,1)S(1)} %copy-done.4), channel_id=1, source_target_pairs={{0,1},{1,0},{2,3},{3,2},{4,5},{5,4},{6,7},{7,6},{8,9},{9,8},{10,11... | collective-permute-start | bytes 1179656 | tf_op jit(solution)/shard_map/ppermute | solution.py:38
  155.1 8.9 %collective-permute-start.25 = (bf16[128,1536]{1,0:T(8,128)(2,1)S(1)}, bf16[128,1536]{1,0:T(8,128)(2,1)S(1)}, u32[]{:S(2)}, u32[]{:S(2)}) collective-permute-start(bf16[128,1536]{1,0:T(8,128)(2,1)S(1)} %constant_dynamic-update-slice_fusion.refs_0_), channel_id=1, source_target_pairs={{0,1},{1,0},{2,3},{3,2},{4,5},{5,4},{6,7},{7,6},{8,9},{9,8},{10,11... | collective-permute-start | bytes 1179656 | tf_op jit(solution)/shard_map/ppermute | solution.py:38
  163.0 6.3 %collective-permute-start.26 = (bf16[128,1536]{1,0:T(8,128)(2,1)}, bf16[128,1536]{1,0:T(8,128)(2,1)S(1)}, u32[]{:S(2)}, u32[]{:S(2)}) collective-permute-start(bf16[128,1536]{1,0:T(8,128)(2,1)} %collective-permute-done.20.refs_1_), channel_id=1, source_target_pairs={{0,1},{1,0},{2,3},{3,2},{4,5},{5,4},{6,7},{7,6},{8,9},{9,8},{10,11... | collective-permute-start | bytes 1179656 | tf_op jit(solution)/shard_map/ppermute | solution.py:38
  164.0 12.0 %collective-permute-start.24 = (bf16[2,128,1536]{2,1,0:T(8,128)(2,1)S(1)}, bf16[2,128,1536]{2,1,0:T(8,128)(2,1)S(1)}, u32[]{:S(2)}, u32[]{:S(2)}) collective-permute-start(bf16[2,128,1536]{2,1,0:T(8,128)(2,1)S(1)} %get-tuple-element.94), channel_id=1, source_target_pairs={{0,4},{1,3},{2,6},{3,1},{4,0},{5,7},{6,2},{7,5},{8,12},{9,11},{10,... | collective-permute-start | bytes 2359304 | tf_op jit(solution)/shard_map/ppermute | solution.py:32
  177.3 10.5 %collective-permute-start.38 = (bf16[1,128,1536]{2,1,0:T(8,128)(2,1)S(1)}, bf16[1,128,1536]{2,1,0:T(8,128)(2,1)S(1)}, u32[]{:S(2)}, u32[]{:S(2)}) collective-permute-start(bf16[1,128,1536]{2,1,0:T(8,128)(2,1)S(1)} %get-tuple-element.100), channel_id=1, source_target_pairs={{0,2},{1,5},{2,0},{3,7},{4,6},{5,1},{6,4},{7,3},{8,10},{9,13},{10,... | collective-permute-start | bytes 1179656 | tf_op jit(solution)/shard_map/ppermute | solution.py:32
  180.9 22.2 %collective-permute-start.35 = (bf16[2,128,1536]{2,1,0:T(8,128)(2,1)S(1)}, bf16[2,128,1536]{2,1,0:T(8,128)(2,1)}, u32[]{:S(2)}, u32[]{:S(2)}) collective-permute-start(bf16[2,128,1536]{2,1,0:T(8,128)(2,1)S(1)} %get-tuple-element.103), channel_id=1, source_target_pairs={{0,4},{1,3},{2,6},{3,1},{4,0},{5,7},{6,2},{7,5},{8,12},{9,11},{10,... | collective-permute-start | bytes 2359304 | tf_op jit(solution)/shard_map/ppermute | solution.py:32
  197.4 11.4 %collective-permute-start.40 = (bf16[64,1536]{1,0:T(8,128)(2,1)S(1)}, bf16[64,1536]{1,0:T(8,128)(2,1)}, u32[]{:S(2)}, u32[]{:S(2)}) collective-permute-start(bf16[64,1536]{1,0:T(8,128)(2,1)S(1)} %get-tuple-element.109.refs_2_.refs_9_), channel_id=1, source_target_pairs={{0,2},{1,5},{2,0},{3,7},{4,6},{5,1},{6,4},{7,3},{8,10},{9,13},{10,... | collective-permute-start | bytes 589832 | tf_op jit(solution)/shard_map/ppermute | solution.py:32
  199.2 61.7 %all-to-all-start.3 = ((bf16[4,384,768]{2,1,0:T(8,128)(2,1)}), bf16[4,384,768]{2,1,0:T(8,128)(2,1)S(1)}, u32[]{:S(2)}, u32[]{:S(2)}) async-start(bf16[4,384,768]{2,1,0:T(8,128)(2,1)} %bitcast.25), calls=%async_computation.3 | async-start | bytes 4718592 | tf_op jit(solution)/shard_map/all_to_all | solution.py:1011
  203.0 85.6 %reduce-scatter.3.cloned.1.call-start = ((), (), s32[]{:S(2)}) async-start(), calls=%async_computation.9 | async-start | bytes 2457600 | tf_op jit(solution)/shard_map/reduce_scatter | solution.py:1073
  206.2 9.4 %collective-permute-start.36 = (bf16[1,128,1536]{2,1,0:T(8,128)(2,1)S(1)}, bf16[1,128,1536]{2,1,0:T(8,128)(2,1)S(1)}, u32[]{:S(2)}, u32[]{:S(2)}) collective-permute-start(bf16[1,128,1536]{2,1,0:T(8,128)(2,1)S(1)} %get-tuple-element.105), channel_id=1, source_target_pairs={{0,2},{1,5},{2,0},{3,7},{4,6},{5,1},{6,4},{7,3},{8,10},{9,13},{10,... | collective-permute-start | bytes 1179656 | tf_op jit(solution)/shard_map/ppermute | solution.py:32
  208.7 6.9 %collective-permute-start.42 = (bf16[64,1536]{1,0:T(8,128)(2,1)}, bf16[64,1536]{1,0:T(8,128)(2,1)S(1)}, u32[]{:S(2)}, u32[]{:S(2)}) collective-permute-start(bf16[64,1536]{1,0:T(8,128)(2,1)} %collective-permute-done.40.refs_3_.refs_10_), channel_id=1, source_target_pairs={{0,4},{1,3},{2,6},{3,1},{4,0},{5,7},{6,2},{7,5},{8,12},{9,11},{10,... | collective-permute-start | bytes 589832 | tf_op jit(solution)/shard_map/ppermute | solution.py:32
  209.9 29.6 %collective-permute-start.49 = (bf16[1536,640]{1,0:T(8,128)(2,1)}, bf16[1536,640]{1,0:T(8,128)(2,1)}, u32[]{:S(2)}, u32[]{:S(2)}) collective-permute-start(bf16[1536,640]{1,0:T(8,128)(2,1)} %all-gather.2.cloned.1.call-done.refs_10_.refs_19_.refs_4_), channel_id=1, source_target_pairs={{0,1},{1,0},{2,3},{3,2},{4,5},{5,4},{6,7},{7,6},{8,9},{9,8},{10,11... | collective-permute-start | bytes 5898248 | tf_op jit(solution)/shard_map/ppermute | solution.py:38
  209.9 6.3 %collective-permute-start.43 = (bf16[64,1536]{1,0:T(8,128)(2,1)S(1)}, bf16[64,1536]{1,0:T(8,128)(2,1)S(1)}, u32[]{:S(2)}, u32[]{:S(2)}) collective-permute-start(bf16[64,1536]{1,0:T(8,128)(2,1)S(1)} %get-tuple-element.109.refs_2_.refs_9_), channel_id=1, source_target_pairs={{0,1},{1,0},{2,3},{3,2},{4,5},{5,4},{6,7},{7,6},{8,9},{9,8},{10,11... | collective-permute-start | bytes 589832 | tf_op jit(solution)/shard_map/ppermute | solution.py:38
  250.7 29.8 %collective-permute-start.50 = (bf16[2,320,1536]{2,1,0:T(8,128)(2,1)}, bf16[2,320,1536]{2,1,0:T(8,128)(2,1)}, u32[]{:S(2)}, u32[]{:S(2)}) collective-permute-start(bf16[2,320,1536]{2,1,0:T(8,128)(2,1)} %get-tuple-element.122), channel_id=1, source_target_pairs={{0,4},{1,3},{2,6},{3,1},{4,0},{5,7},{6,2},{7,5},{8,12},{9,11},{10,... | collective-permute-start | bytes 5898248 | tf_op jit(solution)/shard_map/ppermute | solution.py:32
  252.5 18.4 %collective-permute-start.37 = (bf16[64,1536]{1,0:T(8,128)(2,1)S(1)}, bf16[64,1536]{1,0:T(8,128)(2,1)S(1)}, u32[]{:S(2)}, u32[]{:S(2)}) collective-permute-start(bf16[64,1536]{1,0:T(8,128)(2,1)S(1)} %shard_map.234), channel_id=1, source_target_pairs={{0,8},{8,0},{16,24},{24,16},{1,9},{9,1},{17,25},{25,17},{2,10},{10... | collective-permute-start | bytes 589832 | tf_op jit(solution)/shard_map/ppermute | solution.py:38
  262.4 26.3 %all-to-all-start.4 = ((bf16[8,48,1536]{2,1,0:T(8,128)(2,1)}), bf16[8,48,1536]{2,1,0:T(8,128)(2,1)S(1)}, u32[]{:S(2)}, u32[]{:S(2)}) async-start(bf16[8,48,1536]{2,1,0:T(8,128)(2,1)} %bitcast.27), calls=%async_computation.4 | async-start | bytes 2359296 | tf_op jit(solution)/shard_map/all_to_all | solution.py:1016
  266.1 44.7 %reduce-scatter.5.cloned.1.call-start = ((), (), s32[]{:S(2)}) async-start(), calls=%async_computation.10 | async-start | bytes 737280 | tf_op jit(solution)/shard_map/reduce_scatter | solution.py:1126
  266.1 6.5 %collective-permute-start.52 = (bf16[2,48,1536]{2,1,0:T(8,128)(2,1)}, bf16[2,48,1536]{2,1,0:T(8,128)(2,1)S(1)}, u32[]{:S(2)}, u32[]{:S(2)}) collective-permute-start(bf16[2,48,1536]{2,1,0:T(8,128)(2,1)} %bitcast.29), channel_id=1, source_target_pairs={{0,1},{1,0},{2,3},{3,2},{4,5},{5,4},{6,7},{7,6},{8,9},{9,8},{10,11... | collective-permute-start | bytes 884744 | tf_op jit(solution)/shard_map/ppermute | solution.py:38
  284.2 18.4 %collective-permute-start.51 = (bf16[1,320,1536]{2,1,0:T(8,128)(2,1)}, bf16[1,320,1536]{2,1,0:T(8,128)(2,1)S(1)}, u32[]{:S(2)}, u32[]{:S(2)}) collective-permute-start(bf16[1,320,1536]{2,1,0:T(8,128)(2,1)} %get-tuple-element.126), channel_id=1, source_target_pairs={{0,2},{1,5},{2,0},{3,7},{4,6},{5,1},{6,4},{7,3},{8,10},{9,13},{10,... | collective-permute-start | bytes 2949128 | tf_op jit(solution)/shard_map/ppermute | solution.py:32
  288.6 18.3 %all-to-all-start.5 = ((bf16[8,48,640]{2,1,0:T(8,128)(2,1)}), bf16[8,48,640]{2,1,0:T(8,128)(2,1)S(1)}, u32[]{:S(2)}, u32[]{:S(2)}) async-start(bf16[8,48,640]{2,1,0:T(8,128)(2,1)} %bitcast.68), calls=%async_computation.6 | async-start | bytes 983040 | tf_op jit(solution)/shard_map/all_to_all | solution.py:1118
  (60 other events, 409.0 us)
Sparse Core Ops, SparseCore 0:
  33.1 48.3 all-gather.1
  239.0 49.1 reduce-scatter.2
  290.5 20.2 reduce-scatter.4
